TPU v7x, 32 devices: a whole 2x2x4 slice. The times are simulated.
32 devices in a mesh: ctx: 16 (over z, x, core), tp: 2 (over y).
Axes of the slice: x: 2, y: 2, z: 4, core: 2. Of those that a mesh axis runs over, the one named last changes fastest.
Arguments:
- tokens: bfloat16 [1920, 8192], P('tp', 'ctx'), may hold values from -6 to 6
- norm_gain: float32 [1920], replicated, may hold values from 0.1 to 1.9
- w_in: bfloat16 [3, 1920, 1920], P(None, 'tp'), may hold values from -0.125 to 0.125
- w_short: float32 [3, 3, 1920], P(None, None, 'tp'), may hold values from -3 to 3
- decay_rate: float32 [16, 1920], P(None, 'tp'), as said below
- residue: float32 [16, 1920], P(None, 'tp'), may hold values from -1.5 to 1.5
- skip_gain: float32 [1920], P('tp'), may hold values from -3 to 3
- w_out: bfloat16 [1920, 1920], P('tp'), may hold values from -0.125 to 0.125
Outputs:
- mixed: bfloat16 [1920, 8192], P('tp', 'ctx')
Inputs may be any that keep to these rules, and one draw needn't show every extreme that they name: `decay_rate`: every rate lies between 0.2 / 8192 and 1 / 30.
All inputs are finite; a program needn't handle non-finite values.
Results may differ from a plain program's by a relative error of at most 0.0077.
Values may be sent and summed in bfloat16 or wider, within the bound.
No kernel may reach another device: no remote copies, remote signals or barrier semaphores. Data moves between devices by JAX's collectives and lax.ppermute only.
A program may use at most 256 MiB of HBM per device.

v0:
```python
import functools

import jax
import jax.numpy as jnp
from jax import lax
from jax.experimental import pallas as pl
from jax.experimental.pallas import tpu as pltpu
from jax.sharding import PartitionSpec as P


F32 = jnp.float32
BF16 = jnp.bfloat16
ROWS = 8
LANES = 128
BLOCK = 256
CHUNKS = 4
SPAN = 16
VMEM_LIMIT = 10 * 2**20
CONTRACT_LAST = (((1,), (1,)), ((), ()))
CONTRACT_FIRST = (((0,), (0,)), ((), ()))


def lane_groups(low, width):
    return [(start, min(LANES, low + width - start)) for start in range(low, low + width, LANES)]


def rows_as(row, width):
    return jnp.broadcast_to(row, (ROWS, width))


def tree_sum(terms):
    while len(terms) > 1:
        terms = [sum(terms[k + 1 : k + 2], terms[k]) for k in range(0, len(terms), 2)]
    return terms[0]


def token_picker(first_row, rows, tokens):
    length = tokens // ROWS
    row = lax.broadcasted_iota(jnp.int32, (rows, tokens), 0)
    column = lax.broadcasted_iota(jnp.int32, (rows, tokens), 1)
    wanted = lax.rem(row, ROWS) * length + lax.div(row, ROWS) + first_row // ROWS
    return jnp.where(column == wanted, 1.0, 0.0).astype(BF16)


def turned(pick, tokens):
    return lax.dot_general(pick, tokens, CONTRACT_LAST, preferred_element_type=F32).astype(BF16)


def first_rows(halo, size, tokens_ref, out_ref, edge_ref):
    tokens = tokens_ref.shape[1]
    row = lax.broadcasted_iota(jnp.int32, (halo, tokens), 0)
    column = lax.broadcasted_iota(jnp.int32, (halo, tokens), 1)
    last = edge_ref.shape[0]
    picks = [
        token_picker(size - halo, halo + size, tokens),
        jnp.where((row < last) & (column == tokens - last + row), 1.0, 0.0).astype(BF16),
    ]
    rows = turned(jnp.concatenate(picks, axis=0), tokens_ref[...])
    out_ref[...] = rows[: halo + size]
    edge_ref[...] = rows[halo + size : halo + size + last]


def next_rows(firsts, tokens_ref, *chunk_refs):
    tokens = tokens_ref.shape[1]
    for row, ref in zip(firsts, chunk_refs):
        ref[...] = turned(token_picker(row, ref.shape[0], tokens), tokens_ref[...])


def load_weights(places, w_hbm, out_ref, w_ref, sem):
    copies = [
        pltpu.make_async_copy(w_hbm.at[place], w_ref.at[place], sem.at[k])
        for k, place in enumerate(places)
    ]
    for copy in copies:
        copy.start()
    for (s, part), copy in zip(places, copies):
        copy.wait()
        out_ref[s, :, part] = w_ref[s, part, :].T


def short_conv(p_ref, short_ref, s, part, rows, taps):
    width = part.stop - part.start
    total = None
    for offset in range(taps):
        start = ROWS * (taps - 1 - offset)
        term = short_ref[offset, s : s + 1, part] * p_ref[start : start + rows, :width]
        total = term if total is None else total + term
    return total


def project(normed, w_ref, s, part):
    product = jnp.dot(normed, w_ref[s, :, part], preferred_element_type=F32)
    return product.astype(BF16).astype(F32)


def signal_stage(pieces, row, taps, *refs):
    refs = list(refs)
    me_ref = refs.pop(0)
    token_refs = [refs.pop(0) for _ in range(pieces)]
    x_ref, p_ref = refs[-2:]
    halo = ROWS * (taps - 1)
    rows, share = p_ref.shape[0] - halo, token_refs[0].shape[1]
    last, start = row == 0, row == rows
    fresh = last or start
    read = rows + halo if fresh else rows
    edge_refs = [refs.pop(0) for _ in range(pieces)] if last else []
    if not start:
        normed_in, _, _, states_in, tail_in = [refs.pop(0) for _ in range(5)]
    gain_ref, w_ref, short_ref, rate_ref = refs[:4]
    normed_ref, signal_ref, marks_ref, states_ref, tail_ref = refs[4:9]
    total_ref, sent_ref = refs[9:11] if last else (None, None)
    modes, channels = rate_ref.shape
    length = signal_ref.shape[0] // ROWS
    me = me_ref[0]

    values = [ref[...].astype(F32) for ref in token_refs]
    if last:
        preceded = jnp.where(me_ref[1] > 0, 1.0, 0.0)
        blank = jnp.zeros((ROWS - 1, share), F32)
        for s, ref in enumerate(edge_refs):
            edge = ref[...].astype(F32) * preceded
            front = [piece for k in range(taps - 1) for piece in (edge[k : k + 1], blank)]
            values[s] = jnp.concatenate(front + [values[s]], axis=0)
    for rank in range(pieces):
        chosen = values[0]
        for s in range(1, pieces):
            chosen = jnp.where(me == (rank - s) % pieces, values[s], chosen)
        x_ref[:, rank * share : (rank + 1) * share] = chosen
    features = x_ref[...]
    mean = jnp.mean(features * features, axis=1, keepdims=True)
    normed = features * lax.rsqrt(mean + 1e-06) * gain_ref[...]
    if last:
        ends = normed_in[normed_in.shape[0] - halo :, :].astype(F32)
        segment = lax.broadcasted_iota(jnp.int32, (ROWS, ends.shape[1]), 0)
        front = [
            jnp.where(segment >= 1, pltpu.roll(ends[at : at + ROWS], 1, 0), normed[at : at + ROWS])
            for at in range(0, halo, ROWS)
        ]
        normed = jnp.concatenate(front + [normed[halo:]], axis=0)
    normed = normed.astype(BF16)
    begin = row if fresh else halo + row
    normed_ref[begin : begin + read, :] = normed

    for low in range(0, channels, BLOCK):
        width = min(BLOCK, channels - low)
        part = slice(low, low + width)
        for s in (1, 2):
            if not fresh:
                p_ref[:halo, :width] = tail_in[s - 1, :, part]
            p_ref[halo + rows - read :, :width] = project(
                normed_ref[begin : begin + read, :], w_ref, s, part
            )
            tail_ref[s - 1, :, part] = p_ref[rows:, :width]
            short = short_conv(p_ref, short_ref, s, part, rows, taps)
            if s == 1:
                signal_ref[row : row + rows, part] = short
            else:
                signal_ref[row : row + rows, part] = signal_ref[row : row + rows, part] * short
        for start, size in lane_groups(low, width):
            lanes = slice(start, start + size)
            rate = [rows_as(rate_ref[n : n + 1, lanes], size) for n in range(modes)]
            decay = [jnp.exp(-r) for r in rate]

            if fresh:
                states = (jnp.zeros((ROWS, size), F32),) * modes
            else:
                states = tuple(states_in[n, :, lanes] for n in range(modes))
                for n in range(modes):
                    marks_ref[row // rows, n, :, lanes] = states[n]

            def step(i, states):
                here = pl.ds(pl.multiple_of(row + i * ROWS, ROWS), ROWS)
                now = signal_ref[here, lanes]
                return tuple(states[n] * decay[n] + now for n in range(modes))

            states = lax.fori_loop(0, rows // ROWS, step, states, unroll=8)
            if last:
                later = length - rows // ROWS
                for n in range(modes):
                    marks_ref[1, n, :, lanes] = states[n]
                states = tuple(
                    states_in[n, :, lanes] + jnp.exp(-rate[n] * later) * states[n]
                    for n in range(modes)
                )
            for n in range(modes):
                states_ref[n, :, lanes] = states[n]
            if last:
                left = lax.broadcasted_iota(jnp.int32, (ROWS, size), 0)
                left = ((ROWS - 1 - left) * length).astype(F32)
                for n in range(modes):
                    total_ref[n : n + 1, lanes] = jnp.sum(
                        states[n] * jnp.exp(-rate[n] * left), axis=0, keepdims=True
                    )
                sent_ref[:, lanes] = total_ref[:, lanes].astype(BF16)


def local_stage(row, rows, taps, *refs):
    normed_ref, signal_ref, states_ref, w_ref, short_ref, rate_ref, mode_ref, skip_ref = refs[:8]
    q_ref, local_ref = refs[8:10]
    begin_ref = refs[10] if row == 0 else None
    p_ref = refs[-1]
    modes, channels = rate_ref.shape
    length = signal_ref.shape[0] // ROWS
    for low in range(0, channels, BLOCK):
        width = min(BLOCK, channels - low)
        part = slice(low, low + width)
        normed = normed_ref[row : row + p_ref.shape[0], :]
        p_ref[:, :width] = project(normed, w_ref, 0, part)
        q_ref[:, part] = short_conv(p_ref, short_ref, 0, part, rows, taps)
        for start, size in lane_groups(low, width):
            lanes = slice(start, start + size)
            rate = [rows_as(rate_ref[n : n + 1, lanes], size) for n in range(modes)]
            segment = lax.broadcasted_iota(jnp.int32, (ROWS, size), 0)
            if row == 0:
                for n in range(modes):
                    run = states_ref[n, :, lanes]
                    for hop in (1, 2, 4):
                        weight = jnp.where(segment >= hop, jnp.exp(-rate[n] * (hop * length)), 0.0)
                        run = run + weight * pltpu.roll(run, hop, 0)
                    begin_ref[n, :, lanes] = jnp.where(segment >= 1, pltpu.roll(run, 1, 0), 0.0)
            lag = segment.astype(F32)
            filters = []
            for first_lag in range(0, SPAN, ROWS):
                values = tree_sum(
                    [
                        rows_as(mode_ref[n : n + 1, lanes], size)
                        * jnp.exp(-rate[n] * (lag + first_lag))
                        for n in range(modes)
                    ]
                )
                filters += [rows_as(values[j : j + 1, :], size) for j in range(ROWS)]
            filters[0] = filters[0] + skip_ref[:, lanes]

            def span(i, carry):
                base = i * (SPAN * ROWS)
                now = [
                    signal_ref[pl.ds(pl.multiple_of(row + base + k * ROWS, ROWS), ROWS), lanes]
                    for k in range(SPAN)
                ]
                for k in range(SPAN):
                    local_ref[pl.ds(pl.multiple_of(base + k * ROWS, ROWS), ROWS), lanes] = tree_sum(
                        [filters[j] * now[k - j] for j in range(k + 1)]
                    )
                return carry

            lax.fori_loop(0, rows // (SPAN * ROWS), span, 0)


def second_stage(pieces, row, rows, length, *refs):
    me_ref, q_ref, local_ref, begin_ref, marks_ref, carry_ref, rate_ref, mode_ref, w_ref = refs[:9]
    send_ref, own_ref, gated_ref = refs[9:]
    modes, channels = rate_ref.shape
    for start, size in lane_groups(0, channels):
        lanes = slice(start, start + size)
        rate = [rows_as(rate_ref[n : n + 1, lanes], size) for n in range(modes)]
        decay = [jnp.exp(-r) for r in rate]
        segment = lax.broadcasted_iota(jnp.int32, (ROWS, size), 0)
        past = (segment * length).astype(F32)
        for at in range(row, row + rows, SPAN * ROWS):
            mark = at // (SPAN * ROWS)
            states = []
            for n in range(modes):
                state = begin_ref[n, :, lanes] + jnp.exp(-rate[n] * past) * carry_ref[
                    n : n + 1, lanes
                ]
                if mark > 0:
                    state = marks_ref[1, n, :, lanes] + state * jnp.exp(-rate[n] * SPAN)
                if mark > 1:
                    state = marks_ref[mark, n, :, lanes] + state * jnp.exp(
                        -rate[n] * (SPAN * (mark - 1))
                    )
                states.append(mode_ref[n : n + 1, lanes] * state)

            def step(i, states):
                here = pl.ds(pl.multiple_of(at - row + i * ROWS, ROWS), ROWS)
                states = tuple(states[n] * decay[n] for n in range(modes))
                gated_ref[here, lanes] = q_ref[here, lanes] * tree_sum(
                    [local_ref[here, lanes]] + list(states)
                )
                return states

            lax.fori_loop(0, SPAN, step, tuple(states), unroll=4)
    product = jnp.dot(gated_ref[...].astype(BF16), w_ref[...], preferred_element_type=F32)
    share = own_ref.shape[1]
    me = me_ref[0]
    columns = [product[:, rank * share : (rank + 1) * share] for rank in range(pieces)]
    for s in range(pieces):
        chosen = columns[0]
        for rank in range(1, pieces):
            chosen = jnp.where(me == (rank - s) % pieces, columns[rank], chosen)
        if s == 0:
            own_ref[...] = chosen
        else:
            send_ref[(s - 1) * rows : s * rows, :] = chosen.astype(BF16)


def turned_back(rows, pick):
    return lax.dot_general(rows, pick, CONTRACT_FIRST, preferred_element_type=F32).astype(BF16)


def last_stage(pieces, sizes, row, more, *refs):
    chunks = len(sizes)
    own_refs, came_refs = refs[:chunks], refs[chunks : chunks * pieces]
    done_ref = refs[chunks * pieces] if more else None
    if more:
        out_ref, mixed_ref, rows_ref, sem = refs[-4:]
    else:
        out_ref, mixed_ref = refs[-2:]
    at = 0
    for j, size in enumerate(sizes):
        total = own_refs[j][...]
        for s in range(pieces - 1):
            total = total + came_refs[j * (pieces - 1) + s][...].astype(F32)
        mixed_ref[at : at + size, :] = total.astype(BF16)
        at += size
    if not more:
        pick = token_picker(row, at, out_ref.shape[1])
        out_ref[...] = turned_back(mixed_ref[...], pick)
        return
    share, tokens = rows_ref.shape
    pick = token_picker(row, at, tokens)
    copies = []
    for low in range(0, share, BLOCK):
        part = slice(low, min(low + BLOCK, share))
        rows_ref[part, :] = done_ref[part, :] + turned_back(mixed_ref[:, part], pick)
        copy = pltpu.make_async_copy(rows_ref.at[part], out_ref.at[part], sem.at[len(copies)])
        copy.start()
        copies.append(copy)
    for copy in copies:
        copy.wait()


def call(kernel, name, scalars, operands, outs, scratch, aliases={}, out_space=pltpu.VMEM):
    vmem = pl.BlockSpec(memory_space=pltpu.VMEM)
    smem = pl.BlockSpec(memory_space=pltpu.SMEM)
    return pl.pallas_call(
        kernel,
        out_shape=outs,
        in_specs=[smem] * len(scalars) + [vmem] * len(operands),
        out_specs=[pl.BlockSpec(memory_space=out_space)] * len(outs),
        scratch_shapes=scratch,
        input_output_aliases=aliases,
        compiler_params=pltpu.CompilerParams(vmem_limit_bytes=VMEM_LIMIT),
        cost_estimate=pl.CostEstimate(flops=1, bytes_accessed=1, transcendentals=0),
        name=name,
    )(*scalars, *operands)


def in_vmem(w):
    streams, channels, features = w.shape
    block = min(BLOCK, channels)
    places = [
        (s, slice(low, min(low + block, channels)))
        for s in (1, 2, 0)
        for low in range(0, channels, block)
    ]
    return pl.pallas_call(
        functools.partial(load_weights, places),
        out_shape=pltpu.VMEM((streams, features, channels), w.dtype),
        in_specs=[pl.BlockSpec(memory_space=pl.ANY)],
        out_specs=pl.BlockSpec(memory_space=pltpu.VMEM),
        scratch_shapes=[
            pltpu.VMEM(w.shape, w.dtype),
            pltpu.SemaphoreType.DMA((len(places),)),
        ],
        compiler_params=pltpu.CompilerParams(vmem_limit_bytes=46 * 2**20),
        cost_estimate=pl.CostEstimate(flops=1, bytes_accessed=1, transcendentals=0),
        name="load_weights",
    )(w)


def run_signal(pieces, row, rows, count, taps, place, tokens, edges, before, gain, w_in, w_short, rate):
    streams, features, channels = w_in.shape
    modes = rate.shape[0]
    halo = ROWS * (taps - 1)
    outs = [
        jax.ShapeDtypeStruct((halo + count, features), BF16),
        jax.ShapeDtypeStruct((count, channels), F32),
        jax.ShapeDtypeStruct((count // rows, modes, ROWS, channels), F32),
        jax.ShapeDtypeStruct((modes, ROWS, channels), F32),
        jax.ShapeDtypeStruct((streams - 1, halo, channels), F32),
    ]
    if row == 0:
        outs += [jax.ShapeDtypeStruct((modes, channels), kind) for kind in (F32, BF16)]
    return call(
        functools.partial(signal_stage, pieces, row, taps),
        "signal_stage",
        [place],
        list(tokens) + list(edges) + list(before) + [gain, w_in, w_short, rate],
        outs,
        [
            pltpu.VMEM((rows + (halo if row in (0, rows) else 0), features), F32),
            pltpu.VMEM((halo + rows, min(BLOCK, channels)), F32),
        ],
        aliases={1 + len(tokens) + len(edges) + k: k for k in range(3)} if before else {},
    )


def run_local(row, rows, taps, normed, signal, states, w_in, w_short, rate, mode, skip):
    channels = signal.shape[1]
    out = jax.ShapeDtypeStruct((rows, channels), F32)
    begin = jax.ShapeDtypeStruct(states.shape, F32)
    return call(
        functools.partial(local_stage, row, rows, taps),
        "local_stage",
        [],
        [normed, signal, states, w_in, w_short, rate, mode, skip],
        [out, out] + ([begin] if row == 0 else []),
        [pltpu.VMEM((rows + ROWS * (taps - 1), min(BLOCK, channels)), F32)],
    )


def run_second(pieces, row, rows, count, place, q, local, begin, marks, carry, rate, mode, w):
    channels, features = w.shape
    share = features // pieces
    return call(
        functools.partial(second_stage, pieces, row, rows, count // ROWS),
        "second_stage",
        [place],
        [q, local, begin, marks, carry, rate, mode, w],
        [
            jax.ShapeDtypeStruct((max(1, pieces - 1) * rows, share), BF16),
            jax.ShapeDtypeStruct((rows, share), F32),
        ],
        [pltpu.VMEM((rows, channels), F32)],
    )


def run_last(pieces, sizes, row, own, came, done, count):
    share = own[0].shape[1]
    scratch = [pltpu.VMEM((sum(sizes), share), BF16)]
    if done:
        scratch += [pltpu.VMEM((share, count), BF16), pltpu.SemaphoreType.DMA((-(-share // BLOCK),))]
    (out,) = call(
        functools.partial(last_stage, pieces, sizes, row, bool(done)),
        "last_stage",
        [],
        [*own, *came, *done],
        [jax.ShapeDtypeStruct((share, count), BF16)],
        scratch,
        out_space=pl.ANY if done else pltpu.VMEM,
    )
    return out


def rotate(value, axis, steps):
    count = lax.axis_size(axis)
    return lax.ppermute(value, axis, [((i + steps) % count, i) for i in range(count)])


def combine_states(span, stride, radix, count, *refs):
    place_ref, rate_ref, total_ref = refs[:3]
    others = refs[3 : 2 + radix]
    refs = refs[2 + radix :]
    carry_in = refs[0] if stride > 1 else None
    carry_ref = refs[1] if stride > 1 else refs[0]
    position = place_ref[1]
    digit = lax.rem(lax.div(position, stride), radix)
    inner = lax.rem(position, stride)
    unit = span * stride
    rate = rate_ref[...]
    before = jnp.zeros(rate.shape, F32)
    for shift in range(1, radix):
        reached = jnp.where(digit >= shift, 1.0, 0.0)
        other = others[shift - 1][...].astype(F32)
        before = before + jnp.exp(-rate * (unit * (shift - 1))) * (other * reached)
    if stride > 1:
        carry_ref[...] = carry_in[...] + jnp.exp(-rate * (span * inner).astype(F32)) * before
    else:
        carry_ref[...] = before
    if stride * radix < count:
        new = jnp.exp(-rate * (unit * (radix - 1 - digit)).astype(F32)) * total_ref[...]
        for shift in range(1, radix):
            at = lax.rem(digit - shift + radix, radix)
            weight = jnp.exp(-rate * (unit * (radix - 1 - at)).astype(F32))
            new = new + weight * others[shift - 1][...].astype(F32)
        refs[-2][...] = new
        refs[-1][...] = new.astype(BF16)


def carried_in(state, sent, rate, span, axis, place, between):
    count = lax.axis_size(axis)
    total, stride, carry = state, 1, []
    while stride < count:
        radix = 4 if count % (stride * 4) == 0 else 2
        assert count % (stride * radix) == 0
        group = stride * radix
        others = []
        for shift in range(1, radix):
            pairs = []
            for i in range(count):
                digit = (i // stride) % radix
                pairs.append((i + ((digit - shift) % radix - digit) * stride, i))
            others.append(lax.ppermute(sent, axis, pairs))
        others = between(stride, others)
        shape = jax.ShapeDtypeStruct(state.shape, F32)
        carry = call(
            functools.partial(combine_states, span, stride, radix, count),
            "combine_states",
            [place],
            [rate, total, *others, *carry],
            [shape, shape, jax.ShapeDtypeStruct(state.shape, BF16)] if group < count else [shape],
            [],
        )
        if group < count:
            *carry, total, sent = carry
        stride = group
    return carry[0]


def body(tokens, norm_gain, w_in, w_short, decay_rate, residue, skip_gain, w_out):
    pieces, count = lax.axis_size("tp"), lax.axis_size("ctx")
    share, rows = tokens.shape
    channels = w_in.shape[1]
    taps = w_short.shape[0]
    halo = ROWS * (taps - 1)
    size = SPAN * ROWS
    assert rows == CHUNKS * size
    bf16_rows = lambda size: jax.ShapeDtypeStruct((size, share), BF16)

    place = jnp.stack([lax.axis_index("tp"), lax.axis_index("ctx")]).astype(jnp.int32)
    tokens, place = lax.optimization_barrier((tokens, place))
    x1, edge = call(
        functools.partial(first_rows, halo, size), "first_rows", [], [tokens],
        [bf16_rows(halo + size), bf16_rows(taps - 1)], [],
    )
    edge = rotate(edge, "ctx", -1)
    tokens, x1 = lax.optimization_barrier((tokens, x1))
    x0, *others = call(
        functools.partial(next_rows, [0] + [j * size for j in range(2, CHUNKS)]), "next_rows",
        [], [tokens], [bf16_rows(size)] * (CHUNKS - 1), [],
    )
    x = [x1, *others, x0]
    residue, norm_gain, skip_gain, *_ = lax.optimization_barrier((residue, norm_gain, skip_gain, *x))
    mode = residue * jnp.sqrt(-jnp.expm1(-2.0 * decay_rate))
    gain = norm_gain[None, :]
    skip = skip_gain[None, :]
    w_in, mode, gain, skip, *_ = lax.optimization_barrier((w_in, mode, gain, skip, *x))
    w_in = in_vmem(w_in)
    edge, w_in = lax.optimization_barrier((edge, w_in))
    w_in = pltpu.with_memory_space_constraint(w_in, pltpu.VMEM)
    *parts, edges = [[part] + [rotate(part, "tp", s) for s in range(1, pieces)] for part in x + [edge]]

    before = []
    for part, j in zip(parts, list(range(1, CHUNKS)) + [0]):
        results = run_signal(
            pieces, j * size, size, rows, taps, place, part, [] if j else edges, before, gain, w_in,
            w_short, decay_rate,
        )
        before = results[:5]
    normed, signal, marks, states, _ = before
    state, sent, normed, signal, states = lax.optimization_barrier(
        (results[5], results[6], normed, signal, states)
    )
    out_sizes = [rows // 4] * 4
    out_rows = [sum(out_sizes[:j]) for j in range(4)]
    small = [w_in, w_short, decay_rate, mode, skip]
    done = []

    def local_part():
        k = len(done)
        done.append(run_local(out_rows[k], out_sizes[k], taps, normed, signal, states, *small))

    def between(stride, others):
        if stride > 1 and not done:
            local_part()
            others, done[-1] = lax.optimization_barrier((others, done[-1]))
        return others

    carry = carried_in(state, sent, decay_rate, rows, "ctx", place, between)
    if not done:
        local_part()
    begin = done[0][2]
    own, came = [], []
    for j in range(len(out_sizes)):
        if j >= 2:
            arrived = slice((j - 2) * (pieces - 1), (j - 1) * (pieces - 1))
            normed, signal, carry, came[arrived] = lax.optimization_barrier(
                (normed, signal, carry, came[arrived])
            )
        if j > 0:
            local_part()
        send, kept = run_second(
            pieces, out_rows[j], out_sizes[j], rows, place, *done[j][:2], begin, marks, carry,
            decay_rate, mode, w_out,
        )
        own.append(kept)
        for s in range(1, pieces):
            came.append(rotate(send[(s - 1) * out_sizes[j] : s * out_sizes[j]], "tp", -s))
    early = out_rows[-1]
    cut = (len(out_sizes) - 1) * (pieces - 1)
    done = run_last(pieces, out_sizes[:-1], 0, own[:-1], came[:cut], [], rows)
    return run_last(pieces, out_sizes[-1:], early, own[-1:], came[cut:], [done], rows)


def solution(mesh):
    placed = (
        P("tp", "ctx"),
        P(),
        P(None, "tp", None),
        P(None, None, "tp"),
        P(None, "tp"),
        P(None, "tp"),
        P("tp"),
        P("tp", None),
    )
    return jax.shard_map(
        body, mesh=mesh, in_specs=placed, out_specs=P("tp", "ctx"), check_vma=False
    )
```

profile of v0, /device:TPU:0, one launch (start us, length us, event | category | flops | bytes accessed | tf_op | source)
XLA Modules:
  0.0 77.3 jit_solution(3959445784203938421)
XLA Ops:
  0.0 0.1 pad_add_fusion.refs_0_
  0.1 1.2 %copy-done.2 = bf16[960,512]{1,0:T(8,128)(2,1)S(1)} copy-done((bf16[960,512]{1,0:T(8,128)(2,1)S(1)}, bf16[960,512]{1,0:T(8,128)(2,1)}, u32[]{:S(2)}) %copy-start.2) | copy-done | bytes 983064
  1.3 0.5 first_rows.1
  1.7 3.0 %collective-permute-start.5 = (bf16[144,960]{1,0:T(8,128)(2,1)S(1)}, bf16[144,960]{1,0:T(8,128)(2,1)S(1)}, u32[]{:S(2)}, u32[]{:S(2)}) collective-permute-start(bf16[144,960]{1,0:T(8,128)(2,1)S(1)} %get-tuple-element.89.refs_1_), channel_id=1, source_target_pairs={{1,0},{0,1},{3,2},{2,3},{5,4},{4,5},{7,6},{6,7},{9,8},{8,9},{11,10... | collective-permute-start | bytes 829448 | tf_op jit(solution)/shard_map/ppermute | solution.py:448
  4.8 1.0 %next_rows.1 = (bf16[128,960]{1,0:T(8,128)(2,1)S(1)}, bf16[128,960]{1,0:T(8,128)(2,1)S(1)}, bf16[128,960]{1,0:T(8,128)(2,1)S(1)}) custom-call(bf16[960,512]{1,0:T(8,128)(2,1)S(1)} %copy-done.2), custom_call_target="tpu_custom_call" | custom-call | flops 1 | bytes 1 | tf_op jit(solution)/shard_map/next_rows/pallas_call | solution.py:336
  5.8 0.1 collective-permute-start.4
  5.9 2.0 %collective-permute-start.3 = (bf16[128,960]{1,0:T(8,128)(2,1)S(1)}, bf16[128,960]{1,0:T(8,128)(2,1)S(1)}, u32[]{:S(2)}, u32[]{:S(2)}) collective-permute-start(bf16[128,960]{1,0:T(8,128)(2,1)S(1)} %get-tuple-element.91.refs_1_), channel_id=1, source_target_pairs={{1,0},{0,1},{3,2},{2,3},{5,4},{4,5},{7,6},{6,7},{9,8},{8,9},{11,10... | collective-permute-start | bytes 737288 | tf_op jit(solution)/shard_map/ppermute | solution.py:448
  7.9 0.1 collective-permute-start
  8.0 0.9 %sqrt_multiply_fusion.refs_6_.refs_7_ = f32[16,960]{1,0:T(8,128)S(1)} fusion(f32[16,960]{1,0:T(8,128)} %param.13, f32[16,960]{1,0:T(8,128)} %refs_6_.9), kind=kLoop, calls=%fused_computation | loop fusion | flops 46080 | bytes 184320 | tf_op jit(solution)/shard_map/mul | solution.py:535
  8.9 0.0 copy-start.1
  8.9 0.0 copy-start.3
  9.0 5.3 %load_weights.1.refs_4_.refs_9_.refs_11_.refs_3_ = bf16[3,1920,960]{2,1,0:T(8,128)(2,1)S(1)} custom-call(bf16[3,960,1920]{2,1,0:T(8,128)(2,1)} %w_hbm), custom_call_target="tpu_custom_call" | custom-call | flops 1 | bytes 1 | tf_op jit(solution)/shard_map/load_weights/pallas_call | solution.py:357
  14.3 0.0 collective-permute-done.1.refs_3_
  14.3 2.0 %collective-permute-start.2 = (bf16[2,960]{1,0:T(2,128)(2,1)S(1)}, bf16[2,960]{1,0:T(2,128)(2,1)S(1)}, u32[]{:S(2)}, u32[]{:S(2)}) collective-permute-start(bf16[2,960]{1,0:T(2,128)(2,1)S(1)} %collective-permute-done.1.refs_3_), channel_id=1, source_target_pairs={{1,0},{0,1},{3,2},{2,3},{5,4},{4,5},{7,6},{6,7},{9,8},{8,9},{11,10... | collective-permute-start | bytes 11528 | tf_op jit(solution)/shard_map/ppermute | solution.py:448
  16.3 3.7 %signal_stage.4 = (bf16[528,1920]{1,0:T(8,128)(2,1)S(1)}, f32[512,960]{1,0:T(8,128)S(1)}, f32[4,16,8,960]{3,2,1,0:T(8,128)S(1)}, f32[16,8,960]{2,1,0:T(8,128)S(1)}, f32[2,16,960]{2,1,0:T(8,128)S(1)}) custom-call(s32[2]{0:T(128)S(1)} %pad_add_fusion.refs_0_, bf16[144,960]{1,0:T(8,128)(2,1)S(1)} %get-tuple-element.89.refs_1_, ...), custom_call_target="tpu_custom_call" | custom-call | flops 1 | bytes 1 | tf_op jit(solution)/shard_map/signal_stage/pallas_call | solution.py:336
  20.1 3.5 %signal_stage.5 = (bf16[528,1920]{1,0:T(8,128)(2,1)S(1)}, f32[512,960]{1,0:T(8,128)S(1)}, f32[4,16,8,960]{3,2,1,0:T(8,128)S(1)}, f32[16,8,960]{2,1,0:T(8,128)S(1)}, f32[2,16,960]{2,1,0:T(8,128)S(1)}) custom-call(s32[2]{0:T(128)S(1)} %pad_add_fusion.refs_0_, ...), custom_call_target="tpu_custom_call", output_to_operand_aliasing={{0}: (3, {}), {1}: (4, {}), {2}: (5, {})} | custom-call | flops 1 | bytes 1 | tf_op jit(solution)/shard_map/signal_stage/pallas_call | solution.py:336
  23.5 0.3 collective-permute-done.3.refs_2_
  23.9 3.5 %signal_stage.6 = (bf16[528,1920]{1,0:T(8,128)(2,1)S(1)}, f32[512,960]{1,0:T(8,128)S(1)}, f32[4,16,8,960]{3,2,1,0:T(8,128)S(1)}, f32[16,8,960]{2,1,0:T(8,128)S(1)}, f32[2,16,960]{2,1,0:T(8,128)S(1)}) custom-call(s32[2]{0:T(128)S(1)} %pad_add_fusion.refs_0_, ...), custom_call_target="tpu_custom_call", output_to_operand_aliasing={{0}: (3, {}), {1}: (4, {}), {2}: (5, {})} | custom-call | flops 1 | bytes 1 | tf_op jit(solution)/shard_map/signal_stage/pallas_call | solution.py:336
  27.3 1.4 %collective-permute-done.2.refs_4_ = bf16[2,960]{1,0:T(2,128)(2,1)S(1)} collective-permute-done((bf16[2,960]{1,0:T(2,128)(2,1)S(1)}, bf16[2,960]{1,0:T(2,128)(2,1)S(1)}, u32[]{:S(2)}, u32[]{:S(2)}) %collective-permute-start.2) | collective-permute-done | bytes 3872 | tf_op jit(solution)/shard_map/ppermute | solution.py:448
  28.7 4.5 %signal_stage.7 = (bf16[528,1920]{1,0:T(8,128)(2,1)S(1)}, f32[512,960]{1,0:T(8,128)S(1)}, f32[4,16,8,960]{3,2,1,0:T(8,128)S(1)}, f32[16,8,960]{2,1,0:T(8,128)S(1...) custom-call(s32[2]{0:T(128)S(1)} %pad_add_fusion.refs_0_, ...), custom_call_target="tpu_custom_call", output_to_operand_aliasing={{0}: (5, {}), {1}: (6, {}), {2}: (7, {})} | custom-call | flops 1 | bytes 1 | tf_op jit(solution)/shard_map/signal_stage/pallas_call | solution.py:336
  33.2 1.7 %collective-permute-start.7 = (bf16[16,960]{1,0:T(8,128)(2,1)S(1)}, bf16[16,960]{1,0:T(8,128)(2,1)S(1)}, u32[]{:S(2)}, u32[]{:S(2)}) collective-permute-start(bf16[16,960]{1,0:T(8,128)(2,1)S(1)} %get-tuple-element.122), channel_id=1, source_target_pairs={{4,0},{6,2},{0,4},{2,6},{12,8},{14,10},{8,12},{10,14},{20,16},{22,... | collective-permute-start | bytes 92168 | tf_op jit(solution)/shard_map/ppermute | solution.py:494
  35.0 1.4 %collective-permute-start.8 = (bf16[16,960]{1,0:T(8,128)(2,1)S(1)}, bf16[16,960]{1,0:T(8,128)(2,1)S(1)}, u32[]{:S(2)}, u32[]{:S(2)}) collective-permute-start(bf16[16,960]{1,0:T(8,128)(2,1)S(1)} %get-tuple-element.122), channel_id=1, source_target_pairs={{2,0},{4,2},{6,4},{0,6},{10,8},{12,10},{14,12},{8,14},{18,16},{20,... | collective-permute-start | bytes 92168 | tf_op jit(solution)/shard_map/ppermute | solution.py:494
  36.4 0.2 collective-permute-done.6.refs_3_
  36.6 0.6 collective-permute-done.7.refs_4_
  37.2 0.8 %collective-permute-done.8.refs_5_ = bf16[16,960]{1,0:T(8,128)(2,1)S(1)} collective-permute-done((bf16[16,960]{1,0:T(8,128)(2,1)S(1)}, bf16[16,960]{1,0:T(8,128)(2,1)S(1)}, u32[]{:S(2)}, u32[]{:S(2)}) %collective-permute-start.8) | collective-permute-done | bytes 30752 | tf_op jit(solution)/shard_map/ppermute | solution.py:494
  38.0 0.6 combine_states.2
  38.7 2.7 %collective-permute-start.10 = (bf16[16,960]{1,0:T(8,128)(2,1)S(1)}, bf16[16,960]{1,0:T(8,128)(2,1)S(1)}, u32[]{:S(2)}, u32[]{:S(2)}) collective-permute-start(bf16[16,960]{1,0:T(8,128)(2,1)S(1)} %get-tuple-element.124), channel_id=1, source_target_pairs={{16,0},{18,2},{20,4},{22,6},{24,8},{26,10},{28,12},{30,14},{0,16},... | collective-permute-start | bytes 92168 | tf_op jit(solution)/shard_map/ppermute | solution.py:494
  41.3 1.4 %collective-permute-start.11 = (bf16[16,960]{1,0:T(8,128)(2,1)S(1)}, bf16[16,960]{1,0:T(8,128)(2,1)S(1)}, u32[]{:S(2)}, u32[]{:S(2)}) collective-permute-start(bf16[16,960]{1,0:T(8,128)(2,1)S(1)} %get-tuple-element.124), channel_id=1, source_target_pairs={{8,0},{10,2},{12,4},{14,6},{16,8},{18,10},{20,12},{22,14},{24,16},... | collective-permute-start | bytes 92168 | tf_op jit(solution)/shard_map/ppermute | solution.py:494
  42.7 0.7 collective-permute-start.9
  43.4 1.7 %local_stage.4 = (f32[128,960]{1,0:T(8,128)S(1)}, f32[128,960]{1,0:T(8,128)S(1)}, f32[16,8,960]{2,1,0:T(8,128)S(1)}) custom-call(bf16[528,1920]{1,0:T(8,128)(2,1)S(1)} %get-tuple-element.146.refs_0_, f32[512,960]{1,0:T(8,128)S(1)} %get-tuple-element.147.refs_1_, f32[16,8,960]{2,1,0:T(8,128)S(1)} %get-tuple-element.125.refs_2_, ...), custom_call_target="tpu_custom_call" | custom-call | flops 1 | bytes 1 | tf_op jit(solution)/shard_map/local_stage/pallas_call | solution.py:336
  45.0 0.2 collective-permute-done.11.refs_5_
  45.2 3.1 %collective-permute-done.9.refs_3_ = bf16[16,960]{1,0:T(8,128)(2,1)S(1)} collective-permute-done((bf16[16,960]{1,0:T(8,128)(2,1)S(1)}, bf16[16,960]{1,0:T(8,128)(2,1)S(1)}, u32[]{:S(2)}, u32[]{:S(2)}) %collective-permute-start.9) | collective-permute-done | bytes 30752 | tf_op jit(solution)/shard_map/ppermute | solution.py:494
  48.4 0.6 combine_states.3.refs_5_
  49.0 2.5 %second_stage.4 = (bf16[128,960]{1,0:T(8,128)(2,1)S(1)}, f32[128,960]{1,0:T(8,128)S(1)}) custom-call(s32[2]{0:T(128)S(1)} %pad_add_fusion.refs_0_, f32[128,960]{1,0:T(8,128)S(1)} %get-tuple-element.135.refs_1_, f32[128,960]{1,0:T(8,128)S(1)} %get-tuple-element.136.refs_2_, f32[16,8,960]{2,1,0:T(8,128)S(1)} %get-tuple-element.137.refs_3_, ...), custom_call_target="tpu_custom_call" | custom-call | flops 1 | bytes 1 | tf_op jit(solution)/shard_map/second_stage/pallas_call | solution.py:336
  51.5 1.6 %collective-permute-start.12 = (bf16[128,960]{1,0:T(8,128)(2,1)S(1)}, bf16[128,960]{1,0:T(8,128)(2,1)S(1)}, u32[]{:S(2)}, u32[]{:S(2)}) collective-permute-start(bf16[128,960]{1,0:T(8,128)(2,1)S(1)} %get-tuple-element.139), channel_id=1, source_target_pairs={{1,0},{0,1},{3,2},{2,3},{5,4},{4,5},{7,6},{6,7},{9,8},{8,9},{11,10... | collective-permute-start | bytes 737288 | tf_op jit(solution)/shard_map/ppermute | solution.py:448
  53.1 1.3 %local_stage.5 = (f32[128,960]{1,0:T(8,128)S(1)}, f32[128,960]{1,0:T(8,128)S(1)}) custom-call(bf16[528,1920]{1,0:T(8,128)(2,1)S(1)} %get-tuple-element.146.refs_0_, f32[512,960]{1,0:T(8,128)S(1)} %get-tuple-element.147.refs_1_, f32[16,8,960]{2,1,0:T(8,128)S(1)} %get-tuple-element.125.refs_2_, ...), custom_call_target="tpu_custom_call" | custom-call | flops 1 | bytes 1 | tf_op jit(solution)/shard_map/local_stage/pallas_call | solution.py:336
  54.4 2.4 %second_stage.5 = (bf16[128,960]{1,0:T(8,128)(2,1)S(1)}, f32[128,960]{1,0:T(8,128)S(1)}) custom-call(s32[2]{0:T(128)S(1)} %pad_add_fusion.refs_0_, f32[128,960]{1,0:T(8,128)S(1)} %get-tuple-element.143.refs_1_, f32[128,960]{1,0:T(8,128)S(1)} %get-tuple-element.144.refs_2_, f32[16,8,960]{2,1,0:T(8,128)S(1)} %get-tuple-element.137.refs_3_, ...), custom_call_target="tpu_custom_call" | custom-call | flops 1 | bytes 1 | tf_op jit(solution)/shard_map/second_stage/pallas_call | solution.py:336
  56.8 0.6 collective-permute-start.13
  57.4 1.9 %collective-permute-done.12.refs_3_ = bf16[128,960]{1,0:T(8,128)(2,1)S(1)} collective-permute-done((bf16[128,960]{1,0:T(8,128)(2,1)S(1)}, bf16[128,960]{1,0:T(8,128)(2,1)S(1)}, u32[]{:S(2)}, u32[]{:S(2)}) %collective-permute-start.12) | collective-permute-done | bytes 245792 | tf_op jit(solution)/shard_map/ppermute | solution.py:448
  59.3 1.3 %local_stage.7 = (f32[128,960]{1,0:T(8,128)S(1)}, f32[128,960]{1,0:T(8,128)S(1)}) custom-call(bf16[528,1920]{1,0:T(8,128)(2,1)S(1)} %get-tuple-element.146.refs_0_, f32[512,960]{1,0:T(8,128)S(1)} %get-tuple-element.147.refs_1_, f32[16,8,960]{2,1,0:T(8,128)S(1)} %get-tuple-element.125.refs_2_, ...), custom_call_target="tpu_custom_call" | custom-call | flops 1 | bytes 1 | tf_op jit(solution)/shard_map/local_stage/pallas_call | solution.py:336
  60.6 2.5 %second_stage.7 = (bf16[128,960]{1,0:T(8,128)(2,1)S(1)}, f32[128,960]{1,0:T(8,128)S(1)}) custom-call(s32[2]{0:T(128)S(1)} %pad_add_fusion.refs_0_, f32[128,960]{1,0:T(8,128)S(1)} %get-tuple-element.155.refs_1_, f32[128,960]{1,0:T(8,128)S(1)} %get-tuple-element.156.refs_2_, f32[16,8,960]{2,1,0:T(8,128)S(1)} %get-tuple-element.137.refs_3_, ...), custom_call_target="tpu_custom_call" | custom-call | flops 1 | bytes 1 | tf_op jit(solution)/shard_map/second_stage/pallas_call | solution.py:336
  63.1 2.5 %collective-permute-start.15 = (bf16[128,960]{1,0:T(8,128)(2,1)S(1)}, bf16[128,960]{1,0:T(8,128)(2,1)S(1)}, u32[]{:S(2)}, u32[]{:S(2)}) collective-permute-start(bf16[128,960]{1,0:T(8,128)(2,1)S(1)} %get-tuple-element.160), channel_id=1, source_target_pairs={{1,0},{0,1},{3,2},{2,3},{5,4},{4,5},{7,6},{6,7},{9,8},{8,9},{11,10... | collective-permute-start | bytes 737288 | tf_op jit(solution)/shard_map/ppermute | solution.py:448
  65.7 1.3 %local_stage.6 = (f32[128,960]{1,0:T(8,128)S(1)}, f32[128,960]{1,0:T(8,128)S(1)}) custom-call(bf16[528,1920]{1,0:T(8,128)(2,1)S(1)} %get-tuple-element.146.refs_0_, f32[512,960]{1,0:T(8,128)S(1)} %get-tuple-element.147.refs_1_, f32[16,8,960]{2,1,0:T(8,128)S(1)} %get-tuple-element.125.refs_2_, ...), custom_call_target="tpu_custom_call" | custom-call | flops 1 | bytes 1 | tf_op jit(solution)/shard_map/local_stage/pallas_call | solution.py:336
  67.0 2.5 %second_stage.6 = (bf16[128,960]{1,0:T(8,128)(2,1)S(1)}, f32[128,960]{1,0:T(8,128)S(1)}) custom-call(s32[2]{0:T(128)S(1)} %pad_add_fusion.refs_0_, f32[128,960]{1,0:T(8,128)S(1)} %get-tuple-element.148.refs_1_, f32[128,960]{1,0:T(8,128)S(1)} %get-tuple-element.149.refs_2_, f32[16,8,960]{2,1,0:T(8,128)S(1)} %get-tuple-element.137.refs_3_, ...), custom_call_target="tpu_custom_call" | custom-call | flops 1 | bytes 1 | tf_op jit(solution)/shard_map/second_stage/pallas_call | solution.py:336
  69.5 1.4 %collective-permute-start.14 = (bf16[128,960]{1,0:T(8,128)(2,1)S(1)}, bf16[128,960]{1,0:T(8,128)(2,1)S(1)}, u32[]{:S(2)}, u32[]{:S(2)}) collective-permute-start(bf16[128,960]{1,0:T(8,128)(2,1)S(1)} %get-tuple-element.152), channel_id=1, source_target_pairs={{1,0},{0,1},{3,2},{2,3},{5,4},{4,5},{7,6},{6,7},{9,8},{8,9},{11,10... | collective-permute-start | bytes 737288 | tf_op jit(solution)/shard_map/ppermute | solution.py:448
  70.9 0.7 last_stage.2.refs_2_
  71.6 4.3 %collective-permute-done.14.refs_1_ = bf16[128,960]{1,0:T(8,128)(2,1)S(1)} collective-permute-done((bf16[128,960]{1,0:T(8,128)(2,1)S(1)}, bf16[128,960]{1,0:T(8,128)(2,1)S(1)}, u32[]{:S(2)}, u32[]{:S(2)}) %collective-permute-start.14) | collective-permute-done | bytes 245792 | tf_op jit(solution)/shard_map/ppermute | solution.py:448
  75.9 1.2 %last_stage.3 = bf16[960,512]{1,0:T(8,128)(2,1)} custom-call(f32[128,960]{1,0:T(8,128)S(1)} %get-tuple-element.151.refs_0_, bf16[128,960]{1,0:T(8,128)(2,1)S(1)} %collective-permute-done.14.refs_1_, bf16[960,512]{1,0:T(8,128)(2,1)S(1)} %last_stage.2.refs_2_), custom_call_target="tpu_custom_call" | custom-call | flops 1 | bytes 1 | tf_op jit(solution)/shard_map/last_stage/pallas_call | solution.py:336
  (18 shorter events, 0.0 us)
Async XLA Ops:
  0.0 8.9 %copy-start.5 = (f32[1920]{0:T(1024)S(1)}, f32[1920]{0:T(1024)}, u32[]{:S(2)}) copy-start(f32[1920]{0:T(1024)} %param.9) | copy-start | bytes 23044
  0.1 1.2 %copy-start.2 = (bf16[960,512]{1,0:T(8,128)(2,1)S(1)}, bf16[960,512]{1,0:T(8,128)(2,1)}, u32[]{:S(2)}) copy-start(bf16[960,512]{1,0:T(8,128)(2,1)} %tokens_ref.1) | copy-start | bytes 2949124
  1.7 14.6 %collective-permute-start.5 = (bf16[144,960]{1,0:T(8,128)(2,1)S(1)}, bf16[144,960]{1,0:T(8,128)(2,1)S(1)}, u32[]{:S(2)}, u32[]{:S(2)}) collective-permute-start(bf16[144,960]{1,0:T(8,128)(2,1)S(1)} %get-tuple-element.89.refs_1_), channel_id=1, source_target_pairs={{1,0},{0,1},{3,2},{2,3},{5,4},{4,5},{7,6},{6,7},{9,8},{8,9},{11,10... | collective-permute-start | bytes 829448 | tf_op jit(solution)/shard_map/ppermute | solution.py:448
  5.8 14.2 %collective-permute-start.4 = (bf16[128,960]{1,0:T(8,128)(2,1)S(1)}, bf16[128,960]{1,0:T(8,128)(2,1)S(1)}, u32[]{:S(2)}, u32[]{:S(2)}) collective-permute-start(bf16[128,960]{1,0:T(8,128)(2,1)S(1)} %get-tuple-element.90.refs_1_), channel_id=1, source_target_pairs={{1,0},{0,1},{3,2},{2,3},{5,4},{4,5},{7,6},{6,7},{9,8},{8,9},{11,10... | collective-permute-start | bytes 737288 | tf_op jit(solution)/shard_map/ppermute | solution.py:448
  5.9 18.0 %collective-permute-start.3 = (bf16[128,960]{1,0:T(8,128)(2,1)S(1)}, bf16[128,960]{1,0:T(8,128)(2,1)S(1)}, u32[]{:S(2)}, u32[]{:S(2)}) collective-permute-start(bf16[128,960]{1,0:T(8,128)(2,1)S(1)} %get-tuple-element.91.refs_1_), channel_id=1, source_target_pairs={{1,0},{0,1},{3,2},{2,3},{5,4},{4,5},{7,6},{6,7},{9,8},{8,9},{11,10... | collective-permute-start | bytes 737288 | tf_op jit(solution)/shard_map/ppermute | solution.py:448
  7.9 20.8 %collective-permute-start = (bf16[128,960]{1,0:T(8,128)(2,1)S(1)}, bf16[128,960]{1,0:T(8,128)(2,1)S(1)}, u32[]{:S(2)}, u32[]{:S(2)}) collective-permute-start(bf16[128,960]{1,0:T(8,128)(2,1)S(1)} %get-tuple-element.87.refs_1_), channel_id=1, source_target_pairs={{1,0},{0,1},{3,2},{2,3},{5,4},{4,5},{7,6},{6,7},{9,8},{8,9},{11,10... | collective-permute-start | bytes 737288 | tf_op jit(solution)/shard_map/ppermute | solution.py:448
  8.0 6.3 %collective-permute-start.1 = (bf16[2,960]{1,0:T(2,128)(2,1)S(1)}, bf16[2,960]{1,0:T(2,128)(2,1)S(1)}, u32[]{:S(2)}, u32[]{:S(2)}) collective-permute-start(bf16[2,960]{1,0:T(2,128)(2,1)S(1)} %get-tuple-element.88), channel_id=1, source_target_pairs={{30,0},{0,2},{2,4},{4,6},{6,8},{8,10},{10,12},{12,14},{14,16},{16,... | collective-permute-start | bytes 11528 | tf_op jit(solution)/shard_map/ppermute | solution.py:448
  8.9 7.4 %copy-start.1 = (f32[16,960]{1,0:T(8,128)S(1)}, f32[16,960]{1,0:T(8,128)}, u32[]{:S(2)}) copy-start(f32[16,960]{1,0:T(8,128)} %refs_6_.9) | copy-start | bytes 184324
  8.9 7.4 %copy-start.3 = (f32[3,3,960]{2,1,0:T(4,128)S(1)}, f32[3,3,960]{2,1,0:T(4,128)}, u32[]{:S(2)}) copy-start(f32[3,3,960]{2,1,0:T(4,128)} %refs_4_.7) | copy-start | bytes 103684
  14.3 14.4 %collective-permute-start.2 = (bf16[2,960]{1,0:T(2,128)(2,1)S(1)}, bf16[2,960]{1,0:T(2,128)(2,1)S(1)}, u32[]{:S(2)}, u32[]{:S(2)}) collective-permute-start(bf16[2,960]{1,0:T(2,128)(2,1)S(1)} %collective-permute-done.1.refs_3_), channel_id=1, source_target_pairs={{1,0},{0,1},{3,2},{2,3},{5,4},{4,5},{7,6},{6,7},{9,8},{8,9},{11,10... | collective-permute-start | bytes 11528 | tf_op jit(solution)/shard_map/ppermute | solution.py:448
  28.7 14.6 %copy-start.4 = (f32[960]{0:T(1024)S(1)}, f32[960]{0:T(1024)}, u32[]{:S(2)}) copy-start(f32[960]{0:T(1024)} %param.14) | copy-start | bytes 11524
  33.2 3.3 %collective-permute-start.6 = (bf16[16,960]{1,0:T(8,128)(2,1)S(1)}, bf16[16,960]{1,0:T(8,128)(2,1)S(1)}, u32[]{:S(2)}, u32[]{:S(2)}) collective-permute-start(bf16[16,960]{1,0:T(8,128)(2,1)S(1)} %get-tuple-element.122), channel_id=1, source_target_pairs={{6,0},{0,2},{2,4},{4,6},{14,8},{8,10},{10,12},{12,14},{22,16},{16,... | collective-permute-start | bytes 92168 | tf_op jit(solution)/shard_map/ppermute | solution.py:494
  33.2 3.9 %collective-permute-start.7 = (bf16[16,960]{1,0:T(8,128)(2,1)S(1)}, bf16[16,960]{1,0:T(8,128)(2,1)S(1)}, u32[]{:S(2)}, u32[]{:S(2)}) collective-permute-start(bf16[16,960]{1,0:T(8,128)(2,1)S(1)} %get-tuple-element.122), channel_id=1, source_target_pairs={{4,0},{6,2},{0,4},{2,6},{12,8},{14,10},{8,12},{10,14},{20,16},{22,... | collective-permute-start | bytes 92168 | tf_op jit(solution)/shard_map/ppermute | solution.py:494
  35.0 3.0 %collective-permute-start.8 = (bf16[16,960]{1,0:T(8,128)(2,1)S(1)}, bf16[16,960]{1,0:T(8,128)(2,1)S(1)}, u32[]{:S(2)}, u32[]{:S(2)}) collective-permute-start(bf16[16,960]{1,0:T(8,128)(2,1)S(1)} %get-tuple-element.122), channel_id=1, source_target_pairs={{2,0},{4,2},{6,4},{0,6},{10,8},{12,10},{14,12},{8,14},{18,16},{20,... | collective-permute-start | bytes 92168 | tf_op jit(solution)/shard_map/ppermute | solution.py:494
  38.7 6.4 %collective-permute-start.10 = (bf16[16,960]{1,0:T(8,128)(2,1)S(1)}, bf16[16,960]{1,0:T(8,128)(2,1)S(1)}, u32[]{:S(2)}, u32[]{:S(2)}) collective-permute-start(bf16[16,960]{1,0:T(8,128)(2,1)S(1)} %get-tuple-element.124), channel_id=1, source_target_pairs={{16,0},{18,2},{20,4},{22,6},{24,8},{26,10},{28,12},{30,14},{0,16},... | collective-permute-start | bytes 92168 | tf_op jit(solution)/shard_map/ppermute | solution.py:494
  41.3 3.9 %collective-permute-start.11 = (bf16[16,960]{1,0:T(8,128)(2,1)S(1)}, bf16[16,960]{1,0:T(8,128)(2,1)S(1)}, u32[]{:S(2)}, u32[]{:S(2)}) collective-permute-start(bf16[16,960]{1,0:T(8,128)(2,1)S(1)} %get-tuple-element.124), channel_id=1, source_target_pairs={{8,0},{10,2},{12,4},{14,6},{16,8},{18,10},{20,12},{22,14},{24,16},... | collective-permute-start | bytes 92168 | tf_op jit(solution)/shard_map/ppermute | solution.py:494
  42.7 5.7 %collective-permute-start.9 = (bf16[16,960]{1,0:T(8,128)(2,1)S(1)}, bf16[16,960]{1,0:T(8,128)(2,1)S(1)}, u32[]{:S(2)}, u32[]{:S(2)}) collective-permute-start(bf16[16,960]{1,0:T(8,128)(2,1)S(1)} %get-tuple-element.124), channel_id=1, source_target_pairs={{24,0},{26,2},{28,4},{30,6},{0,8},{2,10},{4,12},{6,14},{8,16},{10,... | collective-permute-start | bytes 92168 | tf_op jit(solution)/shard_map/ppermute | solution.py:494
  43.4 5.6 %copy-start = (bf16[960,1920]{1,0:T(8,128)(2,1)S(1)}, bf16[960,1920]{1,0:T(8,128)(2,1)}, u32[]{:S(2)}) copy-start(bf16[960,1920]{1,0:T(8,128)(2,1)} %refs_8_.7) | copy-start | bytes 11059204
  51.5 7.8 %collective-permute-start.12 = (bf16[128,960]{1,0:T(8,128)(2,1)S(1)}, bf16[128,960]{1,0:T(8,128)(2,1)S(1)}, u32[]{:S(2)}, u32[]{:S(2)}) collective-permute-start(bf16[128,960]{1,0:T(8,128)(2,1)S(1)} %get-tuple-element.139), channel_id=1, source_target_pairs={{1,0},{0,1},{3,2},{2,3},{5,4},{4,5},{7,6},{6,7},{9,8},{8,9},{11,10... | collective-permute-start | bytes 737288 | tf_op jit(solution)/shard_map/ppermute | solution.py:448
  56.8 8.8 %collective-permute-start.13 = (bf16[128,960]{1,0:T(8,128)(2,1)S(1)}, bf16[128,960]{1,0:T(8,128)(2,1)S(1)}, u32[]{:S(2)}, u32[]{:S(2)}) collective-permute-start(bf16[128,960]{1,0:T(8,128)(2,1)S(1)} %get-tuple-element.145), channel_id=1, source_target_pairs={{1,0},{0,1},{3,2},{2,3},{5,4},{4,5},{7,6},{6,7},{9,8},{8,9},{11,10... | collective-permute-start | bytes 737288 | tf_op jit(solution)/shard_map/ppermute | solution.py:448
  63.1 7.7 %collective-permute-start.15 = (bf16[128,960]{1,0:T(8,128)(2,1)S(1)}, bf16[128,960]{1,0:T(8,128)(2,1)S(1)}, u32[]{:S(2)}, u32[]{:S(2)}) collective-permute-start(bf16[128,960]{1,0:T(8,128)(2,1)S(1)} %get-tuple-element.160), channel_id=1, source_target_pairs={{1,0},{0,1},{3,2},{2,3},{5,4},{4,5},{7,6},{6,7},{9,8},{8,9},{11,10... | collective-permute-start | bytes 737288 | tf_op jit(solution)/shard_map/ppermute | solution.py:448
  69.5 6.4 %collective-permute-start.14 = (bf16[128,960]{1,0:T(8,128)(2,1)S(1)}, bf16[128,960]{1,0:T(8,128)(2,1)S(1)}, u32[]{:S(2)}, u32[]{:S(2)}) collective-permute-start(bf16[128,960]{1,0:T(8,128)(2,1)S(1)} %get-tuple-element.152), channel_id=1, source_target_pairs={{1,0},{0,1},{3,2},{2,3},{5,4},{4,5},{7,6},{6,7},{9,8},{8,9},{11,10... | collective-permute-start | bytes 737288 | tf_op jit(solution)/shard_map/ppermute | solution.py:448
where the time goes:
time: 77.5 us; the launch traced here: 77.3 us
  Pallas kernels  40.6 us (52%)
  starting transfers between devices  21.2 us (27%)
  waiting for transfers between devices  12.9 us (17%)
  local copies, waits for them, and re-layouts  1.23 us (2%)
  other arithmetic  0.99 us (1%)
    pallas_call x18, Pallas kernels, call(): pl.pallas_call(kernel, out_shape=outs, in_specs=[smem] * len(scalars) + [...  35.3 us
    ppermute x10, starting transfers between devices, rotate(): lax.ppermute(value, axis, [((i + steps) % count, i) for i in range(count)])  13.3 us
    ppermute x10, waiting for transfers between devices, rotate(): lax.ppermute(value, axis, [((i + steps) % count, i) for i in range(count)])  7.95 us
    ppermute x6, starting transfers between devices, carried_in(): others.append(lax.ppermute(sent, axis, pairs))  7.87 us
    pallas_call x1, Pallas kernels, in_vmem(): pl.pallas_call(functools.partial(load_weights, places), out_shape=pltpu.V...  5.31 us
    ppermute x6, waiting for transfers between devices, carried_in(): others.append(lax.ppermute(sent, axis, pairs))  4.95 us
  transfers between devices with their start and end apart: 16, of which 9 were waited for; matrix products, arithmetic and copies ran while one was open for 1% of the time, Pallas kernels for 40%

commit v1 on v0

--- a/solution.py
+++ b/solution.py
@@ -26,6 +26,29 @@
 
 def rows_as(row, width):
     return jnp.broadcast_to(row, (ROWS, width))
+
+
+def decays(rate_ref, lanes, size, steps):
+    values = jnp.exp(-rate_ref[:, lanes] * steps)
+    return [rows_as(values[n : n + 1, :], size) for n in range(values.shape[0])]
+
+
+def sums_of_rows(values):
+    row = lax.broadcasted_iota(jnp.int32, values[0].shape, 0)
+    count = len(values)
+    values = list(values) + [jnp.zeros_like(values[0])] * (ROWS - count)
+    for hop in (4, 2, 1):
+        low = lax.rem(row, 2 * hop) < hop
+        joined = []
+        for a, b in zip(values[:hop], values[hop:]):
+            other = jnp.where(low, b, a)
+            if 2 * hop == ROWS:
+                other = pltpu.roll(other, hop, 0)
+            else:
+                other = jnp.where(low, pltpu.roll(other, ROWS - hop, 0), pltpu.roll(other, hop, 0))
+            joined.append(jnp.where(low, a, b) + other)
+        values = joined
+    return values[0][:count]
 
 
 def tree_sum(terms):
@@ -158,8 +181,7 @@
                 signal_ref[row : row + rows, part] = signal_ref[row : row + rows, part] * short
         for start, size in lane_groups(low, width):
             lanes = slice(start, start + size)
-            rate = [rows_as(rate_ref[n : n + 1, lanes], size) for n in range(modes)]
-            decay = [jnp.exp(-r) for r in rate]
+            decay = decays(rate_ref, lanes, size, 1.0)
 
             if fresh:
                 states = (jnp.zeros((ROWS, size), F32),) * modes
@@ -175,21 +197,22 @@
 
             states = lax.fori_loop(0, rows // ROWS, step, states, unroll=8)
             if last:
-                later = length - rows // ROWS
                 for n in range(modes):
                     marks_ref[1, n, :, lanes] = states[n]
-                states = tuple(
-                    states_in[n, :, lanes] + jnp.exp(-rate[n] * later) * states[n]
-                    for n in range(modes)
-                )
+                later = decays(rate_ref, lanes, size, float(length - rows // ROWS))
+                states = tuple(states_in[n, :, lanes] + later[n] * states[n] for n in range(modes))
             for n in range(modes):
                 states_ref[n, :, lanes] = states[n]
             if last:
                 left = lax.broadcasted_iota(jnp.int32, (ROWS, size), 0)
                 left = ((ROWS - 1 - left) * length).astype(F32)
-                for n in range(modes):
-                    total_ref[n : n + 1, lanes] = jnp.sum(
-                        states[n] * jnp.exp(-rate[n] * left), axis=0, keepdims=True
+                for low_mode in range(0, modes, ROWS):
+                    some = range(low_mode, min(low_mode + ROWS, modes))
+                    total_ref[low_mode : low_mode + len(some), lanes] = sums_of_rows(
+                        [
+                            states[n] * jnp.exp(-rows_as(rate_ref[n : n + 1, lanes], size) * left)
+                            for n in some
+                        ]
                     )
                 sent_ref[:, lanes] = total_ref[:, lanes].astype(BF16)
 
@@ -197,7 +220,7 @@
 def local_stage(row, rows, taps, *refs):
     normed_ref, signal_ref, states_ref, w_ref, short_ref, rate_ref, mode_ref, skip_ref = refs[:8]
     q_ref, local_ref = refs[8:10]
-    begin_ref = refs[10] if row == 0 else None
+    begin_ref, past_ref = refs[10:12] if row == 0 else (None, None)
     p_ref = refs[-1]
     modes, channels = rate_ref.shape
     length = signal_ref.shape[0] // ROWS
@@ -217,7 +240,11 @@
                     for hop in (1, 2, 4):
                         weight = jnp.where(segment >= hop, jnp.exp(-rate[n] * (hop * length)), 0.0)
                         run = run + weight * pltpu.roll(run, hop, 0)
-                    begin_ref[n, :, lanes] = jnp.where(segment >= 1, pltpu.roll(run, 1, 0), 0.0)
+                    mode = rows_as(mode_ref[n : n + 1, lanes], size)
+                    begin = jnp.where(segment >= 1, pltpu.roll(run, 1, 0), 0.0)
+                    begin_ref[n, :, lanes] = mode * begin
+                    past = (segment * length).astype(F32)
+                    past_ref[n, :, lanes] = mode * jnp.exp(-rate[n] * past)
             lag = segment.astype(F32)
             filters = []
             for first_lag in range(0, SPAN, ROWS):
@@ -246,30 +273,27 @@
             lax.fori_loop(0, rows // (SPAN * ROWS), span, 0)
 
 
-def second_stage(pieces, row, rows, length, *refs):
-    me_ref, q_ref, local_ref, begin_ref, marks_ref, carry_ref, rate_ref, mode_ref, w_ref = refs[:9]
-    send_ref, own_ref, gated_ref = refs[9:]
+def second_stage(pieces, row, rows, *refs):
+    me_ref, q_ref, local_ref, begin_ref, past_ref, marks_ref, carry_ref = refs[:7]
+    rate_ref, mode_ref, w_ref, send_ref, own_ref, gated_ref = refs[7:]
     modes, channels = rate_ref.shape
     for start, size in lane_groups(0, channels):
         lanes = slice(start, start + size)
-        rate = [rows_as(rate_ref[n : n + 1, lanes], size) for n in range(modes)]
-        decay = [jnp.exp(-r) for r in rate]
-        segment = lax.broadcasted_iota(jnp.int32, (ROWS, size), 0)
-        past = (segment * length).astype(F32)
+        decay = decays(rate_ref, lanes, size, 1.0)
         for at in range(row, row + rows, SPAN * ROWS):
             mark = at // (SPAN * ROWS)
-            states = []
-            for n in range(modes):
-                state = begin_ref[n, :, lanes] + jnp.exp(-rate[n] * past) * carry_ref[
-                    n : n + 1, lanes
-                ]
-                if mark > 0:
-                    state = marks_ref[1, n, :, lanes] + state * jnp.exp(-rate[n] * SPAN)
-                if mark > 1:
-                    state = marks_ref[mark, n, :, lanes] + state * jnp.exp(
-                        -rate[n] * (SPAN * (mark - 1))
-                    )
-                states.append(mode_ref[n : n + 1, lanes] * state)
+            states = [
+                begin_ref[n, :, lanes] + past_ref[n, :, lanes] * carry_ref[n : n + 1, lanes]
+                for n in range(modes)
+            ]
+            for known, steps in ((1, SPAN), (mark, SPAN * (mark - 1))):
+                if mark >= max(known, 1) and steps > 0:
+                    less = decays(rate_ref, lanes, size, float(steps))
+                    states = [
+                        mode_ref[n : n + 1, lanes] * marks_ref[known, n, :, lanes]
+                        + states[n] * less[n]
+                        for n in range(modes)
+                    ]
 
             def step(i, states):
                 here = pl.ds(pl.multiple_of(at - row + i * ROWS, ROWS), ROWS)
@@ -405,19 +429,19 @@
         "local_stage",
         [],
         [normed, signal, states, w_in, w_short, rate, mode, skip],
-        [out, out] + ([begin] if row == 0 else []),
+        [out, out] + ([begin, begin] if row == 0 else []),
         [pltpu.VMEM((rows + ROWS * (taps - 1), min(BLOCK, channels)), F32)],
     )
 
 
-def run_second(pieces, row, rows, count, place, q, local, begin, marks, carry, rate, mode, w):
+def run_second(pieces, row, rows, place, q, local, begin, past, marks, carry, rate, mode, w):
     channels, features = w.shape
     share = features // pieces
     return call(
-        functools.partial(second_stage, pieces, row, rows, count // ROWS),
+        functools.partial(second_stage, pieces, row, rows),
         "second_stage",
         [place],
-        [q, local, begin, marks, carry, rate, mode, w],
+        [q, local, begin, past, marks, carry, rate, mode, w],
         [
             jax.ShapeDtypeStruct((max(1, pieces - 1) * rows, share), BF16),
             jax.ShapeDtypeStruct((rows, share), F32),
@@ -486,13 +510,13 @@
         assert count % (stride * radix) == 0
         group = stride * radix
         others = []
-        for shift in range(1, radix):
+        for shift in reversed(range(1, radix)):
             pairs = []
             for i in range(count):
                 digit = (i // stride) % radix
                 pairs.append((i + ((digit - shift) % radix - digit) * stride, i))
             others.append(lax.ppermute(sent, axis, pairs))
-        others = between(stride, others)
+        others = between(stride, others[::-1])
         shape = jax.ShapeDtypeStruct(state.shape, F32)
         carry = call(
             functools.partial(combine_states, span, stride, radix, count),
@@ -570,7 +594,7 @@
     carry = carried_in(state, sent, decay_rate, rows, "ctx", place, between)
     if not done:
         local_part()
-    begin = done[0][2]
+    begin, past = done[0][2:]
     own, came = [], []
     for j in range(len(out_sizes)):
         if j >= 2:
@@ -581,7 +605,7 @@
         if j > 0:
             local_part()
         send, kept = run_second(
-            pieces, out_rows[j], out_sizes[j], rows, place, *done[j][:2], begin, marks, carry,
+            pieces, out_rows[j], out_sizes[j], place, *done[j][:2], begin, past, marks, carry,
             decay_rate, mode, w_out,
         )
         own.append(kept)

time: 77.5 us -> 77.3 us (level)
  transfers between devices with their start and end apart: 16 -> 16, of which waited for: 9 -> 9; matrix products, arithmetic and copies ran while one was open for 1% -> 1% of each run, Pallas kernels for 40% -> 39%
where the time goes in v1:
time: 77.3 us; the launch traced here: 77.1 us
  Pallas kernels  40.2 us (52%)
  starting transfers between devices  21.2 us (27%)
  waiting for transfers between devices  13.1 us (17%)
  local copies, waits for them, and re-layouts  1.23 us (2%)
  other arithmetic  0.99 us (1%)
    pallas_call x18, Pallas kernels, call(): pl.pallas_call(kernel, out_shape=outs, in_specs=[smem] * len(scalars) + [...  34.9 us
    ppermute x10, starting transfers between devices, rotate(): lax.ppermute(value, axis, [((i + steps) % count, i) for i in range(count)])  13.4 us
    ppermute x10, waiting for transfers between devices, rotate(): lax.ppermute(value, axis, [((i + steps) % count, i) for i in range(count)])  8.21 us
    ppermute x6, starting transfers between devices, carried_in(): others.append(lax.ppermute(sent, axis, pairs))  7.87 us
    pallas_call x1, Pallas kernels, in_vmem(): pl.pallas_call(functools.partial(load_weights, places), out_shape=pltpu.V...  5.31 us
    ppermute x6, waiting for transfers between devices, carried_in(): others.append(lax.ppermute(sent, axis, pairs))  4.86 us
  transfers between devices with their start and end apart: 16, of which 9 were waited for; matrix products, arithmetic and copies ran while one was open for 1% of the time, Pallas kernels for 39%

profile of v1, /device:TPU:0, one launch (start us, length us, event | category | flops | bytes accessed | tf_op | source)
XLA Modules:
  0.0 77.1 jit_solution(3609299536681455528)
XLA Ops:
  0.0 0.1 pad_add_fusion.refs_0_
  0.1 1.2 %copy-done.2 = bf16[960,512]{1,0:T(8,128)(2,1)S(1)} copy-done((bf16[960,512]{1,0:T(8,128)(2,1)S(1)}, bf16[960,512]{1,0:T(8,128)(2,1)}, u32[]{:S(2)}) %copy-start.2) | copy-done | bytes 983064
  1.3 0.5 first_rows.1
  1.7 3.0 %collective-permute-start.5 = (bf16[144,960]{1,0:T(8,128)(2,1)S(1)}, bf16[144,960]{1,0:T(8,128)(2,1)S(1)}, u32[]{:S(2)}, u32[]{:S(2)}) collective-permute-start(bf16[144,960]{1,0:T(8,128)(2,1)S(1)} %get-tuple-element.91.refs_1_), channel_id=1, source_target_pairs={{1,0},{0,1},{3,2},{2,3},{5,4},{4,5},{7,6},{6,7},{9,8},{8,9},{11,10... | collective-permute-start | bytes 829448 | tf_op jit(solution)/shard_map/ppermute | solution.py:472
  4.8 1.0 %next_rows.1 = (bf16[128,960]{1,0:T(8,128)(2,1)S(1)}, bf16[128,960]{1,0:T(8,128)(2,1)S(1)}, bf16[128,960]{1,0:T(8,128)(2,1)S(1)}) custom-call(bf16[960,512]{1,0:T(8,128)(2,1)S(1)} %copy-done.2), custom_call_target="tpu_custom_call" | custom-call | flops 1 | bytes 1 | tf_op jit(solution)/shard_map/next_rows/pallas_call | solution.py:360
  5.8 0.1 collective-permute-start.4
  5.9 2.0 %collective-permute-start.3 = (bf16[128,960]{1,0:T(8,128)(2,1)S(1)}, bf16[128,960]{1,0:T(8,128)(2,1)S(1)}, u32[]{:S(2)}, u32[]{:S(2)}) collective-permute-start(bf16[128,960]{1,0:T(8,128)(2,1)S(1)} %get-tuple-element.93.refs_1_), channel_id=1, source_target_pairs={{1,0},{0,1},{3,2},{2,3},{5,4},{4,5},{7,6},{6,7},{9,8},{8,9},{11,10... | collective-permute-start | bytes 737288 | tf_op jit(solution)/shard_map/ppermute | solution.py:472
  7.9 0.1 collective-permute-start
  8.0 0.9 %sqrt_multiply_fusion.refs_6_.refs_8_ = f32[16,960]{1,0:T(8,128)S(1)} fusion(f32[16,960]{1,0:T(8,128)} %param.13, f32[16,960]{1,0:T(8,128)} %refs_7_.7), kind=kLoop, calls=%fused_computation | loop fusion | flops 46080 | bytes 184320 | tf_op jit(solution)/shard_map/mul | solution.py:559
  8.9 0.0 copy-start.1
  8.9 0.0 copy-start.3
  9.0 5.3 %load_weights.1.refs_4_.refs_9_.refs_11_.refs_3_ = bf16[3,1920,960]{2,1,0:T(8,128)(2,1)S(1)} custom-call(bf16[3,960,1920]{2,1,0:T(8,128)(2,1)} %w_hbm), custom_call_target="tpu_custom_call" | custom-call | flops 1 | bytes 1 | tf_op jit(solution)/shard_map/load_weights/pallas_call | solution.py:381
  14.3 2.0 %collective-permute-start.2 = (bf16[2,960]{1,0:T(2,128)(2,1)S(1)}, bf16[2,960]{1,0:T(2,128)(2,1)S(1)}, u32[]{:S(2)}, u32[]{:S(2)}) collective-permute-start(bf16[2,960]{1,0:T(2,128)(2,1)S(1)} %collective-permute-done.1.refs_3_), channel_id=1, source_target_pairs={{1,0},{0,1},{3,2},{2,3},{5,4},{4,5},{7,6},{6,7},{9,8},{8,9},{11,10... | collective-permute-start | bytes 11528 | tf_op jit(solution)/shard_map/ppermute | solution.py:472
  16.3 3.7 %signal_stage.4 = (bf16[528,1920]{1,0:T(8,128)(2,1)S(1)}, f32[512,960]{1,0:T(8,128)S(1)}, f32[4,16,8,960]{3,2,1,0:T(8,128)S(1)}, f32[16,8,960]{2,1,0:T(8,128)S(1)}, f32[2,16,960]{2,1,0:T(8,128)S(1)}) custom-call(s32[2]{0:T(128)S(1)} %pad_add_fusion.refs_0_, bf16[144,960]{1,0:T(8,128)(2,1)S(1)} %get-tuple-element.91.refs_1_, ...), custom_call_target="tpu_custom_call" | custom-call | flops 1 | bytes 1 | tf_op jit(solution)/shard_map/signal_stage/pallas_call | solution.py:360
  20.0 3.4 %signal_stage.5 = (bf16[528,1920]{1,0:T(8,128)(2,1)S(1)}, f32[512,960]{1,0:T(8,128)S(1)}, f32[4,16,8,960]{3,2,1,0:T(8,128)S(1)}, f32[16,8,960]{2,1,0:T(8,128)S(1)}, f32[2,16,960]{2,1,0:T(8,128)S(1)}) custom-call(s32[2]{0:T(128)S(1)} %pad_add_fusion.refs_0_, ...), custom_call_target="tpu_custom_call", output_to_operand_aliasing={{0}: (3, {}), {1}: (4, {}), {2}: (5, {})} | custom-call | flops 1 | bytes 1 | tf_op jit(solution)/shard_map/signal_stage/pallas_call | solution.py:360
  23.4 0.4 collective-permute-done.3.refs_2_
  23.9 3.4 %signal_stage.6 = (bf16[528,1920]{1,0:T(8,128)(2,1)S(1)}, f32[512,960]{1,0:T(8,128)S(1)}, f32[4,16,8,960]{3,2,1,0:T(8,128)S(1)}, f32[16,8,960]{2,1,0:T(8,128)S(1)}, f32[2,16,960]{2,1,0:T(8,128)S(1)}) custom-call(s32[2]{0:T(128)S(1)} %pad_add_fusion.refs_0_, ...), custom_call_target="tpu_custom_call", output_to_operand_aliasing={{0}: (3, {}), {1}: (4, {}), {2}: (5, {})} | custom-call | flops 1 | bytes 1 | tf_op jit(solution)/shard_map/signal_stage/pallas_call | solution.py:360
  27.3 1.5 %collective-permute-done.2.refs_4_ = bf16[2,960]{1,0:T(2,128)(2,1)S(1)} collective-permute-done((bf16[2,960]{1,0:T(2,128)(2,1)S(1)}, bf16[2,960]{1,0:T(2,128)(2,1)S(1)}, u32[]{:S(2)}, u32[]{:S(2)}) %collective-permute-start.2) | collective-permute-done | bytes 3872 | tf_op jit(solution)/shard_map/ppermute | solution.py:472
  28.7 4.4 %signal_stage.7 = (bf16[528,1920]{1,0:T(8,128)(2,1)S(1)}, f32[512,960]{1,0:T(8,128)S(1)}, f32[4,16,8,960]{3,2,1,0:T(8,128)S(1)}, f32[16,8,960]{2,1,0:T(8,128)S(1...) custom-call(s32[2]{0:T(128)S(1)} %pad_add_fusion.refs_0_, ...), custom_call_target="tpu_custom_call", output_to_operand_aliasing={{0}: (5, {}), {1}: (6, {}), {2}: (7, {})} | custom-call | flops 1 | bytes 1 | tf_op jit(solution)/shard_map/signal_stage/pallas_call | solution.py:360
  33.1 1.7 %collective-permute-start.7 = (bf16[16,960]{1,0:T(8,128)(2,1)S(1)}, bf16[16,960]{1,0:T(8,128)(2,1)S(1)}, u32[]{:S(2)}, u32[]{:S(2)}) collective-permute-start(bf16[16,960]{1,0:T(8,128)(2,1)S(1)} %get-tuple-element.124), channel_id=1, source_target_pairs={{4,0},{6,2},{0,4},{2,6},{12,8},{14,10},{8,12},{10,14},{20,16},{22,... | collective-permute-start | bytes 92168 | tf_op jit(solution)/shard_map/ppermute | solution.py:518
  34.9 1.4 %collective-permute-start.8 = (bf16[16,960]{1,0:T(8,128)(2,1)S(1)}, bf16[16,960]{1,0:T(8,128)(2,1)S(1)}, u32[]{:S(2)}, u32[]{:S(2)}) collective-permute-start(bf16[16,960]{1,0:T(8,128)(2,1)S(1)} %get-tuple-element.124), channel_id=1, source_target_pairs={{2,0},{4,2},{6,4},{0,6},{10,8},{12,10},{14,12},{8,14},{18,16},{20,... | collective-permute-start | bytes 92168 | tf_op jit(solution)/shard_map/ppermute | solution.py:518
  36.3 0.2 collective-permute-done.6.refs_3_
  36.5 0.6 collective-permute-done.7.refs_4_
  37.1 0.8 %collective-permute-done.8.refs_5_ = bf16[16,960]{1,0:T(8,128)(2,1)S(1)} collective-permute-done((bf16[16,960]{1,0:T(8,128)(2,1)S(1)}, bf16[16,960]{1,0:T(8,128)(2,1)S(1)}, u32[]{:S(2)}, u32[]{:S(2)}) %collective-permute-start.8) | collective-permute-done | bytes 30752 | tf_op jit(solution)/shard_map/ppermute | solution.py:518
  37.9 0.6 combine_states.2
  38.5 2.7 %collective-permute-start.10 = (bf16[16,960]{1,0:T(8,128)(2,1)S(1)}, bf16[16,960]{1,0:T(8,128)(2,1)S(1)}, u32[]{:S(2)}, u32[]{:S(2)}) collective-permute-start(bf16[16,960]{1,0:T(8,128)(2,1)S(1)} %get-tuple-element.126), channel_id=1, source_target_pairs={{16,0},{18,2},{20,4},{22,6},{24,8},{26,10},{28,12},{30,14},{0,16},... | collective-permute-start | bytes 92168 | tf_op jit(solution)/shard_map/ppermute | solution.py:518
  41.2 1.4 %collective-permute-start.11 = (bf16[16,960]{1,0:T(8,128)(2,1)S(1)}, bf16[16,960]{1,0:T(8,128)(2,1)S(1)}, u32[]{:S(2)}, u32[]{:S(2)}) collective-permute-start(bf16[16,960]{1,0:T(8,128)(2,1)S(1)} %get-tuple-element.126), channel_id=1, source_target_pairs={{8,0},{10,2},{12,4},{14,6},{16,8},{18,10},{20,12},{22,14},{24,16},... | collective-permute-start | bytes 92168 | tf_op jit(solution)/shard_map/ppermute | solution.py:518
  42.6 0.7 collective-permute-start.9
  43.2 1.7 %local_stage.4 = (f32[128,960]{1,0:T(8,128)S(1)}, f32[128,960]{1,0:T(8,128)S(1)}, f32[16,8,960]{2,1,0:T(8,128)S(1)}, f32[16,8,960]{2,1,0:T(8,128)S(1)}) custom-call(bf16[528,1920]{1,0:T(8,128)(2,1)S(1)} %get-tuple-element.150.refs_0_, f32[512,960]{1,0:T(8,128)S(1)} %get-tuple-element.151.refs_1_, f32[16,8,960]{2,1,0:T(8,128)S(1)} %get-tuple-element.127.refs_2_, ...), custom_call_target="tpu_custom_call" | custom-call | flops 1 | bytes 1 | tf_op jit(solution)/shard_map/local_stage/pallas_call | solution.py:360
  45.0 0.1 collective-permute-done.11.refs_5_
  45.1 3.1 %collective-permute-done.9.refs_3_ = bf16[16,960]{1,0:T(8,128)(2,1)S(1)} collective-permute-done((bf16[16,960]{1,0:T(8,128)(2,1)S(1)}, bf16[16,960]{1,0:T(8,128)(2,1)S(1)}, u32[]{:S(2)}, u32[]{:S(2)}) %collective-permute-start.9) | collective-permute-done | bytes 30752 | tf_op jit(solution)/shard_map/ppermute | solution.py:518
  48.3 0.6 combine_states.3.refs_6_
  48.9 2.5 %second_stage.4 = (bf16[128,960]{1,0:T(8,128)(2,1)S(1)}, f32[128,960]{1,0:T(8,128)S(1)}) custom-call(s32[2]{0:T(128)S(1)} %pad_add_fusion.refs_0_, f32[128,960]{1,0:T(8,128)S(1)} %get-tuple-element.138.refs_1_, f32[128,960]{1,0:T(8,128)S(1)} %get-tuple-element.139.refs_2_, f32[16,8,960]{2,1,0:T(8,128)S(1)} %get-tuple-element.140.refs_3_, ...), custom_call_target="tpu_custom_call" | custom-call | flops 1 | bytes 1 | tf_op jit(solution)/shard_map/second_stage/pallas_call | solution.py:360
  51.4 1.6 %collective-permute-start.12 = (bf16[128,960]{1,0:T(8,128)(2,1)S(1)}, bf16[128,960]{1,0:T(8,128)(2,1)S(1)}, u32[]{:S(2)}, u32[]{:S(2)}) collective-permute-start(bf16[128,960]{1,0:T(8,128)(2,1)S(1)} %get-tuple-element.143), channel_id=1, source_target_pairs={{1,0},{0,1},{3,2},{2,3},{5,4},{4,5},{7,6},{6,7},{9,8},{8,9},{11,10... | collective-permute-start | bytes 737288 | tf_op jit(solution)/shard_map/ppermute | solution.py:472
  53.0 1.3 %local_stage.5 = (f32[128,960]{1,0:T(8,128)S(1)}, f32[128,960]{1,0:T(8,128)S(1)}) custom-call(bf16[528,1920]{1,0:T(8,128)(2,1)S(1)} %get-tuple-element.150.refs_0_, f32[512,960]{1,0:T(8,128)S(1)} %get-tuple-element.151.refs_1_, f32[16,8,960]{2,1,0:T(8,128)S(1)} %get-tuple-element.127.refs_2_, ...), custom_call_target="tpu_custom_call" | custom-call | flops 1 | bytes 1 | tf_op jit(solution)/shard_map/local_stage/pallas_call | solution.py:360
  54.2 2.3 %second_stage.5 = (bf16[128,960]{1,0:T(8,128)(2,1)S(1)}, f32[128,960]{1,0:T(8,128)S(1)}) custom-call(s32[2]{0:T(128)S(1)} %pad_add_fusion.refs_0_, f32[128,960]{1,0:T(8,128)S(1)} %get-tuple-element.147.refs_1_, f32[128,960]{1,0:T(8,128)S(1)} %get-tuple-element.148.refs_2_, f32[16,8,960]{2,1,0:T(8,128)S(1)} %get-tuple-element.140.refs_3_, ...), custom_call_target="tpu_custom_call" | custom-call | flops 1 | bytes 1 | tf_op jit(solution)/shard_map/second_stage/pallas_call | solution.py:360
  56.6 0.6 collective-permute-start.13
  57.2 2.1 %collective-permute-done.12.refs_3_ = bf16[128,960]{1,0:T(8,128)(2,1)S(1)} collective-permute-done((bf16[128,960]{1,0:T(8,128)(2,1)S(1)}, bf16[128,960]{1,0:T(8,128)(2,1)S(1)}, u32[]{:S(2)}, u32[]{:S(2)}) %collective-permute-start.12) | collective-permute-done | bytes 245792 | tf_op jit(solution)/shard_map/ppermute | solution.py:472
  59.2 1.3 %local_stage.7 = (f32[128,960]{1,0:T(8,128)S(1)}, f32[128,960]{1,0:T(8,128)S(1)}) custom-call(bf16[528,1920]{1,0:T(8,128)(2,1)S(1)} %get-tuple-element.150.refs_0_, f32[512,960]{1,0:T(8,128)S(1)} %get-tuple-element.151.refs_1_, f32[16,8,960]{2,1,0:T(8,128)S(1)} %get-tuple-element.127.refs_2_, ...), custom_call_target="tpu_custom_call" | custom-call | flops 1 | bytes 1 | tf_op jit(solution)/shard_map/local_stage/pallas_call | solution.py:360
  60.5 2.4 %second_stage.7 = (bf16[128,960]{1,0:T(8,128)(2,1)S(1)}, f32[128,960]{1,0:T(8,128)S(1)}) custom-call(s32[2]{0:T(128)S(1)} %pad_add_fusion.refs_0_, f32[128,960]{1,0:T(8,128)S(1)} %get-tuple-element.159.refs_1_, f32[128,960]{1,0:T(8,128)S(1)} %get-tuple-element.160.refs_2_, f32[16,8,960]{2,1,0:T(8,128)S(1)} %get-tuple-element.140.refs_3_, ...), custom_call_target="tpu_custom_call" | custom-call | flops 1 | bytes 1 | tf_op jit(solution)/shard_map/second_stage/pallas_call | solution.py:360
  63.0 2.6 %collective-permute-start.15 = (bf16[128,960]{1,0:T(8,128)(2,1)S(1)}, bf16[128,960]{1,0:T(8,128)(2,1)S(1)}, u32[]{:S(2)}, u32[]{:S(2)}) collective-permute-start(bf16[128,960]{1,0:T(8,128)(2,1)S(1)} %get-tuple-element.164), channel_id=1, source_target_pairs={{1,0},{0,1},{3,2},{2,3},{5,4},{4,5},{7,6},{6,7},{9,8},{8,9},{11,10... | collective-permute-start | bytes 737288 | tf_op jit(solution)/shard_map/ppermute | solution.py:472
  65.5 1.3 %local_stage.6 = (f32[128,960]{1,0:T(8,128)S(1)}, f32[128,960]{1,0:T(8,128)S(1)}) custom-call(bf16[528,1920]{1,0:T(8,128)(2,1)S(1)} %get-tuple-element.150.refs_0_, f32[512,960]{1,0:T(8,128)S(1)} %get-tuple-element.151.refs_1_, f32[16,8,960]{2,1,0:T(8,128)S(1)} %get-tuple-element.127.refs_2_, ...), custom_call_target="tpu_custom_call" | custom-call | flops 1 | bytes 1 | tf_op jit(solution)/shard_map/local_stage/pallas_call | solution.py:360
  66.8 2.4 %second_stage.6 = (bf16[128,960]{1,0:T(8,128)(2,1)S(1)}, f32[128,960]{1,0:T(8,128)S(1)}) custom-call(s32[2]{0:T(128)S(1)} %pad_add_fusion.refs_0_, f32[128,960]{1,0:T(8,128)S(1)} %get-tuple-element.152.refs_1_, f32[128,960]{1,0:T(8,128)S(1)} %get-tuple-element.153.refs_2_, f32[16,8,960]{2,1,0:T(8,128)S(1)} %get-tuple-element.140.refs_3_, ...), custom_call_target="tpu_custom_call" | custom-call | flops 1 | bytes 1 | tf_op jit(solution)/shard_map/second_stage/pallas_call | solution.py:360
  69.2 1.4 %collective-permute-start.14 = (bf16[128,960]{1,0:T(8,128)(2,1)S(1)}, bf16[128,960]{1,0:T(8,128)(2,1)S(1)}, u32[]{:S(2)}, u32[]{:S(2)}) collective-permute-start(bf16[128,960]{1,0:T(8,128)(2,1)S(1)} %get-tuple-element.156), channel_id=1, source_target_pairs={{1,0},{0,1},{3,2},{2,3},{5,4},{4,5},{7,6},{6,7},{9,8},{8,9},{11,10... | collective-permute-start | bytes 737288 | tf_op jit(solution)/shard_map/ppermute | solution.py:472
  70.7 0.0 collective-permute-done.15.refs_5_
  70.7 0.8 last_stage.2.refs_2_
  71.4 4.2 %collective-permute-done.14.refs_1_ = bf16[128,960]{1,0:T(8,128)(2,1)S(1)} collective-permute-done((bf16[128,960]{1,0:T(8,128)(2,1)S(1)}, bf16[128,960]{1,0:T(8,128)(2,1)S(1)}, u32[]{:S(2)}, u32[]{:S(2)}) %collective-permute-start.14) | collective-permute-done | bytes 245792 | tf_op jit(solution)/shard_map/ppermute | solution.py:472
  75.7 1.2 %last_stage.3 = bf16[960,512]{1,0:T(8,128)(2,1)} custom-call(f32[128,960]{1,0:T(8,128)S(1)} %get-tuple-element.155.refs_0_, bf16[128,960]{1,0:T(8,128)(2,1)S(1)} %collective-permute-done.14.refs_1_, bf16[960,512]{1,0:T(8,128)(2,1)S(1)} %last_stage.2.refs_2_), custom_call_target="tpu_custom_call" | custom-call | flops 1 | bytes 1 | tf_op jit(solution)/shard_map/last_stage/pallas_call | solution.py:360
  (18 shorter events, 0.0 us)
Async XLA Ops:
  0.0 8.9 %copy-start.5 = (f32[1920]{0:T(1024)S(1)}, f32[1920]{0:T(1024)}, u32[]{:S(2)}) copy-start(f32[1920]{0:T(1024)} %param.9) | copy-start | bytes 23044
  0.1 1.2 %copy-start.2 = (bf16[960,512]{1,0:T(8,128)(2,1)S(1)}, bf16[960,512]{1,0:T(8,128)(2,1)}, u32[]{:S(2)}) copy-start(bf16[960,512]{1,0:T(8,128)(2,1)} %tokens_ref.1) | copy-start | bytes 2949124
  1.7 14.6 %collective-permute-start.5 = (bf16[144,960]{1,0:T(8,128)(2,1)S(1)}, bf16[144,960]{1,0:T(8,128)(2,1)S(1)}, u32[]{:S(2)}, u32[]{:S(2)}) collective-permute-start(bf16[144,960]{1,0:T(8,128)(2,1)S(1)} %get-tuple-element.91.refs_1_), channel_id=1, source_target_pairs={{1,0},{0,1},{3,2},{2,3},{5,4},{4,5},{7,6},{6,7},{9,8},{8,9},{11,10... | collective-permute-start | bytes 829448 | tf_op jit(solution)/shard_map/ppermute | solution.py:472
  5.8 14.2 %collective-permute-start.4 = (bf16[128,960]{1,0:T(8,128)(2,1)S(1)}, bf16[128,960]{1,0:T(8,128)(2,1)S(1)}, u32[]{:S(2)}, u32[]{:S(2)}) collective-permute-start(bf16[128,960]{1,0:T(8,128)(2,1)S(1)} %get-tuple-element.92.refs_1_), channel_id=1, source_target_pairs={{1,0},{0,1},{3,2},{2,3},{5,4},{4,5},{7,6},{6,7},{9,8},{8,9},{11,10... | collective-permute-start | bytes 737288 | tf_op jit(solution)/shard_map/ppermute | solution.py:472
  5.9 18.0 %collective-permute-start.3 = (bf16[128,960]{1,0:T(8,128)(2,1)S(1)}, bf16[128,960]{1,0:T(8,128)(2,1)S(1)}, u32[]{:S(2)}, u32[]{:S(2)}) collective-permute-start(bf16[128,960]{1,0:T(8,128)(2,1)S(1)} %get-tuple-element.93.refs_1_), channel_id=1, source_target_pairs={{1,0},{0,1},{3,2},{2,3},{5,4},{4,5},{7,6},{6,7},{9,8},{8,9},{11,10... | collective-permute-start | bytes 737288 | tf_op jit(solution)/shard_map/ppermute | solution.py:472
  7.9 20.8 %collective-permute-start = (bf16[128,960]{1,0:T(8,128)(2,1)S(1)}, bf16[128,960]{1,0:T(8,128)(2,1)S(1)}, u32[]{:S(2)}, u32[]{:S(2)}) collective-permute-start(bf16[128,960]{1,0:T(8,128)(2,1)S(1)} %get-tuple-element.89.refs_1_), channel_id=1, source_target_pairs={{1,0},{0,1},{3,2},{2,3},{5,4},{4,5},{7,6},{6,7},{9,8},{8,9},{11,10... | collective-permute-start | bytes 737288 | tf_op jit(solution)/shard_map/ppermute | solution.py:472
  8.0 6.3 %collective-permute-start.1 = (bf16[2,960]{1,0:T(2,128)(2,1)S(1)}, bf16[2,960]{1,0:T(2,128)(2,1)S(1)}, u32[]{:S(2)}, u32[]{:S(2)}) collective-permute-start(bf16[2,960]{1,0:T(2,128)(2,1)S(1)} %get-tuple-element.90), channel_id=1, source_target_pairs={{30,0},{0,2},{2,4},{4,6},{6,8},{8,10},{10,12},{12,14},{14,16},{16,... | collective-permute-start | bytes 11528 | tf_op jit(solution)/shard_map/ppermute | solution.py:472
  8.9 7.4 %copy-start.1 = (f32[16,960]{1,0:T(8,128)S(1)}, f32[16,960]{1,0:T(8,128)}, u32[]{:S(2)}) copy-start(f32[16,960]{1,0:T(8,128)} %refs_7_.7) | copy-start | bytes 184324
  8.9 7.4 %copy-start.3 = (f32[3,3,960]{2,1,0:T(4,128)S(1)}, f32[3,3,960]{2,1,0:T(4,128)}, u32[]{:S(2)}) copy-start(f32[3,3,960]{2,1,0:T(4,128)} %refs_4_.7) | copy-start | bytes 103684
  14.3 14.4 %collective-permute-start.2 = (bf16[2,960]{1,0:T(2,128)(2,1)S(1)}, bf16[2,960]{1,0:T(2,128)(2,1)S(1)}, u32[]{:S(2)}, u32[]{:S(2)}) collective-permute-start(bf16[2,960]{1,0:T(2,128)(2,1)S(1)} %collective-permute-done.1.refs_3_), channel_id=1, source_target_pairs={{1,0},{0,1},{3,2},{2,3},{5,4},{4,5},{7,6},{6,7},{9,8},{8,9},{11,10... | collective-permute-start | bytes 11528 | tf_op jit(solution)/shard_map/ppermute | solution.py:472
  28.7 14.5 %copy-start.4 = (f32[960]{0:T(1024)S(1)}, f32[960]{0:T(1024)}, u32[]{:S(2)}) copy-start(f32[960]{0:T(1024)} %param.14) | copy-start | bytes 11524
  33.1 3.3 %collective-permute-start.6 = (bf16[16,960]{1,0:T(8,128)(2,1)S(1)}, bf16[16,960]{1,0:T(8,128)(2,1)S(1)}, u32[]{:S(2)}, u32[]{:S(2)}) collective-permute-start(bf16[16,960]{1,0:T(8,128)(2,1)S(1)} %get-tuple-element.124), channel_id=1, source_target_pairs={{6,0},{0,2},{2,4},{4,6},{14,8},{8,10},{10,12},{12,14},{22,16},{16,... | collective-permute-start | bytes 92168 | tf_op jit(solution)/shard_map/ppermute | solution.py:518
  33.1 3.9 %collective-permute-start.7 = (bf16[16,960]{1,0:T(8,128)(2,1)S(1)}, bf16[16,960]{1,0:T(8,128)(2,1)S(1)}, u32[]{:S(2)}, u32[]{:S(2)}) collective-permute-start(bf16[16,960]{1,0:T(8,128)(2,1)S(1)} %get-tuple-element.124), channel_id=1, source_target_pairs={{4,0},{6,2},{0,4},{2,6},{12,8},{14,10},{8,12},{10,14},{20,16},{22,... | collective-permute-start | bytes 92168 | tf_op jit(solution)/shard_map/ppermute | solution.py:518
  34.9 3.0 %collective-permute-start.8 = (bf16[16,960]{1,0:T(8,128)(2,1)S(1)}, bf16[16,960]{1,0:T(8,128)(2,1)S(1)}, u32[]{:S(2)}, u32[]{:S(2)}) collective-permute-start(bf16[16,960]{1,0:T(8,128)(2,1)S(1)} %get-tuple-element.124), channel_id=1, source_target_pairs={{2,0},{4,2},{6,4},{0,6},{10,8},{12,10},{14,12},{8,14},{18,16},{20,... | collective-permute-start | bytes 92168 | tf_op jit(solution)/shard_map/ppermute | solution.py:518
  38.5 6.5 %collective-permute-start.10 = (bf16[16,960]{1,0:T(8,128)(2,1)S(1)}, bf16[16,960]{1,0:T(8,128)(2,1)S(1)}, u32[]{:S(2)}, u32[]{:S(2)}) collective-permute-start(bf16[16,960]{1,0:T(8,128)(2,1)S(1)} %get-tuple-element.126), channel_id=1, source_target_pairs={{16,0},{18,2},{20,4},{22,6},{24,8},{26,10},{28,12},{30,14},{0,16},... | collective-permute-start | bytes 92168 | tf_op jit(solution)/shard_map/ppermute | solution.py:518
  41.2 3.9 %collective-permute-start.11 = (bf16[16,960]{1,0:T(8,128)(2,1)S(1)}, bf16[16,960]{1,0:T(8,128)(2,1)S(1)}, u32[]{:S(2)}, u32[]{:S(2)}) collective-permute-start(bf16[16,960]{1,0:T(8,128)(2,1)S(1)} %get-tuple-element.126), channel_id=1, source_target_pairs={{8,0},{10,2},{12,4},{14,6},{16,8},{18,10},{20,12},{22,14},{24,16},... | collective-permute-start | bytes 92168 | tf_op jit(solution)/shard_map/ppermute | solution.py:518
  42.6 5.7 %collective-permute-start.9 = (bf16[16,960]{1,0:T(8,128)(2,1)S(1)}, bf16[16,960]{1,0:T(8,128)(2,1)S(1)}, u32[]{:S(2)}, u32[]{:S(2)}) collective-permute-start(bf16[16,960]{1,0:T(8,128)(2,1)S(1)} %get-tuple-element.126), channel_id=1, source_target_pairs={{24,0},{26,2},{28,4},{30,6},{0,8},{2,10},{4,12},{6,14},{8,16},{10,... | collective-permute-start | bytes 92168 | tf_op jit(solution)/shard_map/ppermute | solution.py:518
  43.2 5.6 %copy-start = (bf16[960,1920]{1,0:T(8,128)(2,1)S(1)}, bf16[960,1920]{1,0:T(8,128)(2,1)}, u32[]{:S(2)}) copy-start(bf16[960,1920]{1,0:T(8,128)(2,1)} %refs_9_.7) | copy-start | bytes 11059204
  51.4 7.9 %collective-permute-start.12 = (bf16[128,960]{1,0:T(8,128)(2,1)S(1)}, bf16[128,960]{1,0:T(8,128)(2,1)S(1)}, u32[]{:S(2)}, u32[]{:S(2)}) collective-permute-start(bf16[128,960]{1,0:T(8,128)(2,1)S(1)} %get-tuple-element.143), channel_id=1, source_target_pairs={{1,0},{0,1},{3,2},{2,3},{5,4},{4,5},{7,6},{6,7},{9,8},{8,9},{11,10... | collective-permute-start | bytes 737288 | tf_op jit(solution)/shard_map/ppermute | solution.py:472
  56.6 8.9 %collective-permute-start.13 = (bf16[128,960]{1,0:T(8,128)(2,1)S(1)}, bf16[128,960]{1,0:T(8,128)(2,1)S(1)}, u32[]{:S(2)}, u32[]{:S(2)}) collective-permute-start(bf16[128,960]{1,0:T(8,128)(2,1)S(1)} %get-tuple-element.149), channel_id=1, source_target_pairs={{1,0},{0,1},{3,2},{2,3},{5,4},{4,5},{7,6},{6,7},{9,8},{8,9},{11,10... | collective-permute-start | bytes 737288 | tf_op jit(solution)/shard_map/ppermute | solution.py:472
  63.0 7.7 %collective-permute-start.15 = (bf16[128,960]{1,0:T(8,128)(2,1)S(1)}, bf16[128,960]{1,0:T(8,128)(2,1)S(1)}, u32[]{:S(2)}, u32[]{:S(2)}) collective-permute-start(bf16[128,960]{1,0:T(8,128)(2,1)S(1)} %get-tuple-element.164), channel_id=1, source_target_pairs={{1,0},{0,1},{3,2},{2,3},{5,4},{4,5},{7,6},{6,7},{9,8},{8,9},{11,10... | collective-permute-start | bytes 737288 | tf_op jit(solution)/shard_map/ppermute | solution.py:472
  69.2 6.4 %collective-permute-start.14 = (bf16[128,960]{1,0:T(8,128)(2,1)S(1)}, bf16[128,960]{1,0:T(8,128)(2,1)S(1)}, u32[]{:S(2)}, u32[]{:S(2)}) collective-permute-start(bf16[128,960]{1,0:T(8,128)(2,1)S(1)} %get-tuple-element.156), channel_id=1, source_target_pairs={{1,0},{0,1},{3,2},{2,3},{5,4},{4,5},{7,6},{6,7},{9,8},{8,9},{11,10... | collective-permute-start | bytes 737288 | tf_op jit(solution)/shard_map/ppermute | solution.py:472

commit v2 on v1

--- a/solution.py
+++ b/solution.py
@@ -486,7 +486,7 @@
     before = jnp.zeros(rate.shape, F32)
     for shift in range(1, radix):
         reached = jnp.where(digit >= shift, 1.0, 0.0)
-        other = others[shift - 1][...].astype(F32)
+        other = others[shift - 1][: rate.shape[0], :].astype(F32)
         before = before + jnp.exp(-rate * (unit * (shift - 1))) * (other * reached)
     if stride > 1:
         carry_ref[...] = carry_in[...] + jnp.exp(-rate * (span * inner).astype(F32)) * before
@@ -497,14 +497,18 @@
         for shift in range(1, radix):
             at = lax.rem(digit - shift + radix, radix)
             weight = jnp.exp(-rate * (unit * (radix - 1 - at)).astype(F32))
-            new = new + weight * others[shift - 1][...].astype(F32)
-        refs[-2][...] = new
-        refs[-1][...] = new.astype(BF16)
+            new = new + weight * others[shift - 1][: rate.shape[0], :].astype(F32)
+        refs[-3][...] = new
+        refs[-2][...] = new.astype(BF16)
+        modes = new.shape[0]
+        refs[-1][:modes, :] = new.astype(BF16)
+        refs[-1][modes:, :] = jnp.zeros((refs[-1].shape[0] - modes, new.shape[1]), BF16)
 
 
 def carried_in(state, sent, rate, span, axis, place, between):
     count = lax.axis_size(axis)
-    total, stride, carry = state, 1, []
+    total, stride, carry, longer = state, 1, [], None
+    modes, channels = state.shape
     while stride < count:
         radix = 4 if count % (stride * 4) == 0 else 2
         assert count % (stride * radix) == 0
@@ -515,7 +519,8 @@
             for i in range(count):
                 digit = (i // stride) % radix
                 pairs.append((i + ((digit - shift) % radix - digit) * stride, i))
-            others.append(lax.ppermute(sent, axis, pairs))
+            first = shift == 1 and longer is not None
+            others.append(lax.ppermute(longer if first else sent, axis, pairs))
         others = between(stride, others[::-1])
         shape = jax.ShapeDtypeStruct(state.shape, F32)
         carry = call(
@@ -523,11 +528,12 @@
             "combine_states",
             [place],
             [rate, total, *others, *carry],
-            [shape, shape, jax.ShapeDtypeStruct(state.shape, BF16)] if group < count else [shape],
+            [shape] if group == count else [shape, shape]
+            + [jax.ShapeDtypeStruct((rows, channels), BF16) for rows in (modes, modes + ROWS)],
             [],
         )
         if group < count:
-            *carry, total, sent = carry
+            *carry, total, sent, longer = carry
         stride = group
     return carry[0]
 

time: 77.3 us -> 76.1 us (0.984)
  waiting for transfers between devices: 13.1 us -> 11.6 us
    ppermute x6, waiting for transfers between devices: 4.86 us -> 2.41 us  [carried_in(): others.append(lax.ppermute(longer if first else sent, axis, pairs))]
    ppermute x10, waiting for transfers between devices: 8.21 us -> 9.18 us  [rotate(): lax.ppermute(value, axis, [((i + steps) % count, i) for i in range(count)])]
    ppermute x6, starting transfers between devices: 7.87 us -> 8.76 us  [carried_in(): others.append(lax.ppermute(longer if first else sent, axis, pairs))]
  transfers between devices with their start and end apart: 16 -> 16, of which waited for: 9 -> 10; matrix products, arithmetic and copies ran while one was open for 1% -> 1% of each run, Pallas kernels for 39% -> 40%
where the time goes in v2:
time: 76.1 us; the launch traced here: 76 us
  Pallas kernels  40.2 us (53%)
  starting transfers between devices  21.6 us (28%)
  waiting for transfers between devices  11.6 us (15%)
  local copies, waits for them, and re-layouts  1.23 us (2%)
  other arithmetic  0.99 us (1%)
    pallas_call x18, Pallas kernels, call(): pl.pallas_call(kernel, out_shape=outs, in_specs=[smem] * len(scalars) + [...  34.9 us
    ppermute x10, starting transfers between devices, rotate(): lax.ppermute(value, axis, [((i + steps) % count, i) for i in range(count)])  12.8 us
    ppermute x10, waiting for transfers between devices, rotate(): lax.ppermute(value, axis, [((i + steps) % count, i) for i in range(count)])  9.18 us
    ppermute x6, starting transfers between devices, carried_in(): others.append(lax.ppermute(longer if first else sent, axis, pairs))  8.76 us
    pallas_call x1, Pallas kernels, in_vmem(): pl.pallas_call(functools.partial(load_weights, places), out_shape=pltpu.V...  5.31 us
    ppermute x6, waiting for transfers between devices, carried_in(): others.append(lax.ppermute(longer if first else sent, axis, pairs))  2.41 us
  transfers between devices with their start and end apart: 16, of which 10 were waited for; matrix products, arithmetic and copies ran while one was open for 1% of the time, Pallas kernels for 40%

profile of v2, /device:TPU:0, one launch (start us, length us, event | category | flops | bytes accessed | tf_op | source)
XLA Modules:
  0.0 76.0 jit_solution(6983632502225751791)
XLA Ops:
  0.0 0.1 pad_add_fusion.refs_0_
  0.1 1.2 %copy-done.2 = bf16[960,512]{1,0:T(8,128)(2,1)S(1)} copy-done((bf16[960,512]{1,0:T(8,128)(2,1)S(1)}, bf16[960,512]{1,0:T(8,128)(2,1)}, u32[]{:S(2)}) %copy-start.2) | copy-done | bytes 983064
  1.3 0.5 first_rows.1
  1.7 3.0 %collective-permute-start.5 = (bf16[144,960]{1,0:T(8,128)(2,1)S(1)}, bf16[144,960]{1,0:T(8,128)(2,1)S(1)}, u32[]{:S(2)}, u32[]{:S(2)}) collective-permute-start(bf16[144,960]{1,0:T(8,128)(2,1)S(1)} %get-tuple-element.92.refs_1_), channel_id=1, source_target_pairs={{1,0},{0,1},{3,2},{2,3},{5,4},{4,5},{7,6},{6,7},{9,8},{8,9},{11,10... | collective-permute-start | bytes 829448 | tf_op jit(solution)/shard_map/ppermute | solution.py:472
  4.8 1.0 %next_rows.1 = (bf16[128,960]{1,0:T(8,128)(2,1)S(1)}, bf16[128,960]{1,0:T(8,128)(2,1)S(1)}, bf16[128,960]{1,0:T(8,128)(2,1)S(1)}) custom-call(bf16[960,512]{1,0:T(8,128)(2,1)S(1)} %copy-done.2), custom_call_target="tpu_custom_call" | custom-call | flops 1 | bytes 1 | tf_op jit(solution)/shard_map/next_rows/pallas_call | solution.py:360
  5.8 0.1 collective-permute-start.4
  5.9 2.0 %collective-permute-start.3 = (bf16[128,960]{1,0:T(8,128)(2,1)S(1)}, bf16[128,960]{1,0:T(8,128)(2,1)S(1)}, u32[]{:S(2)}, u32[]{:S(2)}) collective-permute-start(bf16[128,960]{1,0:T(8,128)(2,1)S(1)} %get-tuple-element.94.refs_1_), channel_id=1, source_target_pairs={{1,0},{0,1},{3,2},{2,3},{5,4},{4,5},{7,6},{6,7},{9,8},{8,9},{11,10... | collective-permute-start | bytes 737288 | tf_op jit(solution)/shard_map/ppermute | solution.py:472
  7.9 0.1 collective-permute-start
  8.0 0.9 %sqrt_multiply_fusion.refs_6_.refs_8_ = f32[16,960]{1,0:T(8,128)S(1)} fusion(f32[16,960]{1,0:T(8,128)} %param.13, f32[16,960]{1,0:T(8,128)} %refs_7_.7), kind=kLoop, calls=%fused_computation | loop fusion | flops 46080 | bytes 184320 | tf_op jit(solution)/shard_map/mul | solution.py:565
  8.9 0.0 copy-start.1
  8.9 0.0 copy-start.3
  9.0 5.3 %load_weights.1.refs_4_.refs_9_.refs_11_.refs_3_ = bf16[3,1920,960]{2,1,0:T(8,128)(2,1)S(1)} custom-call(bf16[3,960,1920]{2,1,0:T(8,128)(2,1)} %w_hbm), custom_call_target="tpu_custom_call" | custom-call | flops 1 | bytes 1 | tf_op jit(solution)/shard_map/load_weights/pallas_call | solution.py:381
  14.3 2.0 %collective-permute-start.2 = (bf16[2,960]{1,0:T(2,128)(2,1)S(1)}, bf16[2,960]{1,0:T(2,128)(2,1)S(1)}, u32[]{:S(2)}, u32[]{:S(2)}) collective-permute-start(bf16[2,960]{1,0:T(2,128)(2,1)S(1)} %collective-permute-done.1.refs_3_), channel_id=1, source_target_pairs={{1,0},{0,1},{3,2},{2,3},{5,4},{4,5},{7,6},{6,7},{9,8},{8,9},{11,10... | collective-permute-start | bytes 11528 | tf_op jit(solution)/shard_map/ppermute | solution.py:472
  16.3 3.7 %signal_stage.4 = (bf16[528,1920]{1,0:T(8,128)(2,1)S(1)}, f32[512,960]{1,0:T(8,128)S(1)}, f32[4,16,8,960]{3,2,1,0:T(8,128)S(1)}, f32[16,8,960]{2,1,0:T(8,128)S(1)}, f32[2,16,960]{2,1,0:T(8,128)S(1)}) custom-call(s32[2]{0:T(128)S(1)} %pad_add_fusion.refs_0_, bf16[144,960]{1,0:T(8,128)(2,1)S(1)} %get-tuple-element.92.refs_1_, ...), custom_call_target="tpu_custom_call" | custom-call | flops 1 | bytes 1 | tf_op jit(solution)/shard_map/signal_stage/pallas_call | solution.py:360
  20.0 3.4 %signal_stage.5 = (bf16[528,1920]{1,0:T(8,128)(2,1)S(1)}, f32[512,960]{1,0:T(8,128)S(1)}, f32[4,16,8,960]{3,2,1,0:T(8,128)S(1)}, f32[16,8,960]{2,1,0:T(8,128)S(1)}, f32[2,16,960]{2,1,0:T(8,128)S(1)}) custom-call(s32[2]{0:T(128)S(1)} %pad_add_fusion.refs_0_, ...), custom_call_target="tpu_custom_call", output_to_operand_aliasing={{0}: (3, {}), {1}: (4, {}), {2}: (5, {})} | custom-call | flops 1 | bytes 1 | tf_op jit(solution)/shard_map/signal_stage/pallas_call | solution.py:360
  23.4 0.4 collective-permute-done.3.refs_2_
  23.9 3.4 %signal_stage.6 = (bf16[528,1920]{1,0:T(8,128)(2,1)S(1)}, f32[512,960]{1,0:T(8,128)S(1)}, f32[4,16,8,960]{3,2,1,0:T(8,128)S(1)}, f32[16,8,960]{2,1,0:T(8,128)S(1)}, f32[2,16,960]{2,1,0:T(8,128)S(1)}) custom-call(s32[2]{0:T(128)S(1)} %pad_add_fusion.refs_0_, ...), custom_call_target="tpu_custom_call", output_to_operand_aliasing={{0}: (3, {}), {1}: (4, {}), {2}: (5, {})} | custom-call | flops 1 | bytes 1 | tf_op jit(solution)/shard_map/signal_stage/pallas_call | solution.py:360
  27.3 1.5 %collective-permute-done.2.refs_4_ = bf16[2,960]{1,0:T(2,128)(2,1)S(1)} collective-permute-done((bf16[2,960]{1,0:T(2,128)(2,1)S(1)}, bf16[2,960]{1,0:T(2,128)(2,1)S(1)}, u32[]{:S(2)}, u32[]{:S(2)}) %collective-permute-start.2) | collective-permute-done | bytes 3872 | tf_op jit(solution)/shard_map/ppermute | solution.py:472
  28.7 4.4 %signal_stage.7 = (bf16[528,1920]{1,0:T(8,128)(2,1)S(1)}, f32[512,960]{1,0:T(8,128)S(1)}, f32[4,16,8,960]{3,2,1,0:T(8,128)S(1)}, f32[16,8,960]{2,1,0:T(8,128)S(1...) custom-call(s32[2]{0:T(128)S(1)} %pad_add_fusion.refs_0_, ...), custom_call_target="tpu_custom_call", output_to_operand_aliasing={{0}: (5, {}), {1}: (6, {}), {2}: (7, {})} | custom-call | flops 1 | bytes 1 | tf_op jit(solution)/shard_map/signal_stage/pallas_call | solution.py:360
  33.1 1.7 %collective-permute-start.7 = (bf16[16,960]{1,0:T(8,128)(2,1)S(1)}, bf16[16,960]{1,0:T(8,128)(2,1)S(1)}, u32[]{:S(2)}, u32[]{:S(2)}) collective-permute-start(bf16[16,960]{1,0:T(8,128)(2,1)S(1)} %get-tuple-element.125), channel_id=1, source_target_pairs={{4,0},{6,2},{0,4},{2,6},{12,8},{14,10},{8,12},{10,14},{20,16},{22,... | collective-permute-start | bytes 92168 | tf_op jit(solution)/shard_map/ppermute | solution.py:523
  34.9 1.4 %collective-permute-start.8 = (bf16[16,960]{1,0:T(8,128)(2,1)S(1)}, bf16[16,960]{1,0:T(8,128)(2,1)S(1)}, u32[]{:S(2)}, u32[]{:S(2)}) collective-permute-start(bf16[16,960]{1,0:T(8,128)(2,1)S(1)} %get-tuple-element.125), channel_id=1, source_target_pairs={{2,0},{4,2},{6,4},{0,6},{10,8},{12,10},{14,12},{8,14},{18,16},{20,... | collective-permute-start | bytes 92168 | tf_op jit(solution)/shard_map/ppermute | solution.py:523
  36.3 0.2 collective-permute-done.6.refs_3_
  36.5 0.6 collective-permute-done.7.refs_4_
  37.1 0.8 %collective-permute-done.8.refs_5_ = bf16[16,960]{1,0:T(8,128)(2,1)S(1)} collective-permute-done((bf16[16,960]{1,0:T(8,128)(2,1)S(1)}, bf16[16,960]{1,0:T(8,128)(2,1)S(1)}, u32[]{:S(2)}, u32[]{:S(2)}) %collective-permute-start.8) | collective-permute-done | bytes 30752 | tf_op jit(solution)/shard_map/ppermute | solution.py:523
  37.9 0.6 combine_states.2
  38.5 1.6 %collective-permute-start.9 = (bf16[24,960]{1,0:T(8,128)(2,1)S(1)}, bf16[24,960]{1,0:T(8,128)(2,1)S(1)}, u32[]{:S(2)}, u32[]{:S(2)}) collective-permute-start(bf16[24,960]{1,0:T(8,128)(2,1)S(1)} %get-tuple-element.127), channel_id=1, source_target_pairs={{24,0},{26,2},{28,4},{30,6},{0,8},{2,10},{4,12},{6,14},{8,16},{10,... | collective-permute-start | bytes 138248 | tf_op jit(solution)/shard_map/ppermute | solution.py:523
  40.2 2.6 %collective-permute-start.10 = (bf16[16,960]{1,0:T(8,128)(2,1)S(1)}, bf16[16,960]{1,0:T(8,128)(2,1)S(1)}, u32[]{:S(2)}, u32[]{:S(2)}) collective-permute-start(bf16[16,960]{1,0:T(8,128)(2,1)S(1)} %get-tuple-element.128), channel_id=1, source_target_pairs={{16,0},{18,2},{20,4},{22,6},{24,8},{26,10},{28,12},{30,14},{0,16},... | collective-permute-start | bytes 92168 | tf_op jit(solution)/shard_map/ppermute | solution.py:523
  42.8 1.3 %collective-permute-start.11 = (bf16[16,960]{1,0:T(8,128)(2,1)S(1)}, bf16[16,960]{1,0:T(8,128)(2,1)S(1)}, u32[]{:S(2)}, u32[]{:S(2)}) collective-permute-start(bf16[16,960]{1,0:T(8,128)(2,1)S(1)} %get-tuple-element.128), channel_id=1, source_target_pairs={{8,0},{10,2},{12,4},{14,6},{16,8},{18,10},{20,12},{22,14},{24,16},... | collective-permute-start | bytes 92168 | tf_op jit(solution)/shard_map/ppermute | solution.py:523
  44.1 1.7 %local_stage.4 = (f32[128,960]{1,0:T(8,128)S(1)}, f32[128,960]{1,0:T(8,128)S(1)}, f32[16,8,960]{2,1,0:T(8,128)S(1)}, f32[16,8,960]{2,1,0:T(8,128)S(1)}) custom-call(bf16[528,1920]{1,0:T(8,128)(2,1)S(1)} %get-tuple-element.152.refs_0_, f32[512,960]{1,0:T(8,128)S(1)} %get-tuple-element.153.refs_1_, f32[16,8,960]{2,1,0:T(8,128)S(1)} %get-tuple-element.129.refs_2_, ...), custom_call_target="tpu_custom_call" | custom-call | flops 1 | bytes 1 | tf_op jit(solution)/shard_map/local_stage/pallas_call | solution.py:360
  45.9 0.3 collective-permute-done.10.refs_4_
  46.2 0.5 collective-permute-done.11.refs_5_
  46.7 0.6 combine_states.3.refs_6_
  47.3 2.5 %second_stage.4 = (bf16[128,960]{1,0:T(8,128)(2,1)S(1)}, f32[128,960]{1,0:T(8,128)S(1)}) custom-call(s32[2]{0:T(128)S(1)} %pad_add_fusion.refs_0_, f32[128,960]{1,0:T(8,128)S(1)} %get-tuple-element.140.refs_1_, f32[128,960]{1,0:T(8,128)S(1)} %get-tuple-element.141.refs_2_, f32[16,8,960]{2,1,0:T(8,128)S(1)} %get-tuple-element.142.refs_3_, ...), custom_call_target="tpu_custom_call" | custom-call | flops 1 | bytes 1 | tf_op jit(solution)/shard_map/second_stage/pallas_call | solution.py:360
  49.8 1.6 %collective-permute-start.12 = (bf16[128,960]{1,0:T(8,128)(2,1)S(1)}, bf16[128,960]{1,0:T(8,128)(2,1)S(1)}, u32[]{:S(2)}, u32[]{:S(2)}) collective-permute-start(bf16[128,960]{1,0:T(8,128)(2,1)S(1)} %get-tuple-element.145), channel_id=1, source_target_pairs={{1,0},{0,1},{3,2},{2,3},{5,4},{4,5},{7,6},{6,7},{9,8},{8,9},{11,10... | collective-permute-start | bytes 737288 | tf_op jit(solution)/shard_map/ppermute | solution.py:472
  51.4 1.3 %local_stage.5 = (f32[128,960]{1,0:T(8,128)S(1)}, f32[128,960]{1,0:T(8,128)S(1)}) custom-call(bf16[528,1920]{1,0:T(8,128)(2,1)S(1)} %get-tuple-element.152.refs_0_, f32[512,960]{1,0:T(8,128)S(1)} %get-tuple-element.153.refs_1_, f32[16,8,960]{2,1,0:T(8,128)S(1)} %get-tuple-element.129.refs_2_, ...), custom_call_target="tpu_custom_call" | custom-call | flops 1 | bytes 1 | tf_op jit(solution)/shard_map/local_stage/pallas_call | solution.py:360
  52.7 2.3 %second_stage.5 = (bf16[128,960]{1,0:T(8,128)(2,1)S(1)}, f32[128,960]{1,0:T(8,128)S(1)}) custom-call(s32[2]{0:T(128)S(1)} %pad_add_fusion.refs_0_, f32[128,960]{1,0:T(8,128)S(1)} %get-tuple-element.149.refs_1_, f32[128,960]{1,0:T(8,128)S(1)} %get-tuple-element.150.refs_2_, f32[16,8,960]{2,1,0:T(8,128)S(1)} %get-tuple-element.142.refs_3_, ...), custom_call_target="tpu_custom_call" | custom-call | flops 1 | bytes 1 | tf_op jit(solution)/shard_map/second_stage/pallas_call | solution.py:360
  55.0 0.6 collective-permute-start.13
  55.6 2.6 %collective-permute-done.12.refs_3_ = bf16[128,960]{1,0:T(8,128)(2,1)S(1)} collective-permute-done((bf16[128,960]{1,0:T(8,128)(2,1)S(1)}, bf16[128,960]{1,0:T(8,128)(2,1)S(1)}, u32[]{:S(2)}, u32[]{:S(2)}) %collective-permute-start.12) | collective-permute-done | bytes 245792 | tf_op jit(solution)/shard_map/ppermute | solution.py:472
  58.2 1.3 %local_stage.7 = (f32[128,960]{1,0:T(8,128)S(1)}, f32[128,960]{1,0:T(8,128)S(1)}) custom-call(bf16[528,1920]{1,0:T(8,128)(2,1)S(1)} %get-tuple-element.152.refs_0_, f32[512,960]{1,0:T(8,128)S(1)} %get-tuple-element.153.refs_1_, f32[16,8,960]{2,1,0:T(8,128)S(1)} %get-tuple-element.129.refs_2_, ...), custom_call_target="tpu_custom_call" | custom-call | flops 1 | bytes 1 | tf_op jit(solution)/shard_map/local_stage/pallas_call | solution.py:360
  59.5 2.4 %second_stage.7 = (bf16[128,960]{1,0:T(8,128)(2,1)S(1)}, f32[128,960]{1,0:T(8,128)S(1)}) custom-call(s32[2]{0:T(128)S(1)} %pad_add_fusion.refs_0_, f32[128,960]{1,0:T(8,128)S(1)} %get-tuple-element.161.refs_1_, f32[128,960]{1,0:T(8,128)S(1)} %get-tuple-element.162.refs_2_, f32[16,8,960]{2,1,0:T(8,128)S(1)} %get-tuple-element.142.refs_3_, ...), custom_call_target="tpu_custom_call" | custom-call | flops 1 | bytes 1 | tf_op jit(solution)/shard_map/second_stage/pallas_call | solution.py:360
  61.9 2.5 %collective-permute-start.15 = (bf16[128,960]{1,0:T(8,128)(2,1)S(1)}, bf16[128,960]{1,0:T(8,128)(2,1)S(1)}, u32[]{:S(2)}, u32[]{:S(2)}) collective-permute-start(bf16[128,960]{1,0:T(8,128)(2,1)S(1)} %get-tuple-element.166), channel_id=1, source_target_pairs={{1,0},{0,1},{3,2},{2,3},{5,4},{4,5},{7,6},{6,7},{9,8},{8,9},{11,10... | collective-permute-start | bytes 737288 | tf_op jit(solution)/shard_map/ppermute | solution.py:472
  64.4 1.3 %local_stage.6 = (f32[128,960]{1,0:T(8,128)S(1)}, f32[128,960]{1,0:T(8,128)S(1)}) custom-call(bf16[528,1920]{1,0:T(8,128)(2,1)S(1)} %get-tuple-element.152.refs_0_, f32[512,960]{1,0:T(8,128)S(1)} %get-tuple-element.153.refs_1_, f32[16,8,960]{2,1,0:T(8,128)S(1)} %get-tuple-element.129.refs_2_, ...), custom_call_target="tpu_custom_call" | custom-call | flops 1 | bytes 1 | tf_op jit(solution)/shard_map/local_stage/pallas_call | solution.py:360
  65.7 2.4 %second_stage.6 = (bf16[128,960]{1,0:T(8,128)(2,1)S(1)}, f32[128,960]{1,0:T(8,128)S(1)}) custom-call(s32[2]{0:T(128)S(1)} %pad_add_fusion.refs_0_, f32[128,960]{1,0:T(8,128)S(1)} %get-tuple-element.154.refs_1_, f32[128,960]{1,0:T(8,128)S(1)} %get-tuple-element.155.refs_2_, f32[16,8,960]{2,1,0:T(8,128)S(1)} %get-tuple-element.142.refs_3_, ...), custom_call_target="tpu_custom_call" | custom-call | flops 1 | bytes 1 | tf_op jit(solution)/shard_map/second_stage/pallas_call | solution.py:360
  68.1 1.0 %collective-permute-start.14 = (bf16[128,960]{1,0:T(8,128)(2,1)S(1)}, bf16[128,960]{1,0:T(8,128)(2,1)S(1)}, u32[]{:S(2)}, u32[]{:S(2)}) collective-permute-start(bf16[128,960]{1,0:T(8,128)(2,1)S(1)} %get-tuple-element.158), channel_id=1, source_target_pairs={{1,0},{0,1},{3,2},{2,3},{5,4},{4,5},{7,6},{6,7},{9,8},{8,9},{11,10... | collective-permute-start | bytes 737288 | tf_op jit(solution)/shard_map/ppermute | solution.py:472
  69.1 0.1 collective-permute-done.15.refs_5_
  69.2 0.8 last_stage.2.refs_2_
  70.0 4.5 %collective-permute-done.14.refs_1_ = bf16[128,960]{1,0:T(8,128)(2,1)S(1)} collective-permute-done((bf16[128,960]{1,0:T(8,128)(2,1)S(1)}, bf16[128,960]{1,0:T(8,128)(2,1)S(1)}, u32[]{:S(2)}, u32[]{:S(2)}) %collective-permute-start.14) | collective-permute-done | bytes 245792 | tf_op jit(solution)/shard_map/ppermute | solution.py:472
  74.5 1.2 %last_stage.3 = bf16[960,512]{1,0:T(8,128)(2,1)} custom-call(f32[128,960]{1,0:T(8,128)S(1)} %get-tuple-element.157.refs_0_, bf16[128,960]{1,0:T(8,128)(2,1)S(1)} %collective-permute-done.14.refs_1_, bf16[960,512]{1,0:T(8,128)(2,1)S(1)} %last_stage.2.refs_2_), custom_call_target="tpu_custom_call" | custom-call | flops 1 | bytes 1 | tf_op jit(solution)/shard_map/last_stage/pallas_call | solution.py:360
  (18 shorter events, 0.0 us)
Async XLA Ops:
  0.0 8.9 %copy-start.5 = (f32[1920]{0:T(1024)S(1)}, f32[1920]{0:T(1024)}, u32[]{:S(2)}) copy-start(f32[1920]{0:T(1024)} %param.9) | copy-start | bytes 23044
  0.1 1.2 %copy-start.2 = (bf16[960,512]{1,0:T(8,128)(2,1)S(1)}, bf16[960,512]{1,0:T(8,128)(2,1)}, u32[]{:S(2)}) copy-start(bf16[960,512]{1,0:T(8,128)(2,1)} %tokens_ref.1) | copy-start | bytes 2949124
  1.7 14.6 %collective-permute-start.5 = (bf16[144,960]{1,0:T(8,128)(2,1)S(1)}, bf16[144,960]{1,0:T(8,128)(2,1)S(1)}, u32[]{:S(2)}, u32[]{:S(2)}) collective-permute-start(bf16[144,960]{1,0:T(8,128)(2,1)S(1)} %get-tuple-element.92.refs_1_), channel_id=1, source_target_pairs={{1,0},{0,1},{3,2},{2,3},{5,4},{4,5},{7,6},{6,7},{9,8},{8,9},{11,10... | collective-permute-start | bytes 829448 | tf_op jit(solution)/shard_map/ppermute | solution.py:472
  5.8 14.2 %collective-permute-start.4 = (bf16[128,960]{1,0:T(8,128)(2,1)S(1)}, bf16[128,960]{1,0:T(8,128)(2,1)S(1)}, u32[]{:S(2)}, u32[]{:S(2)}) collective-permute-start(bf16[128,960]{1,0:T(8,128)(2,1)S(1)} %get-tuple-element.93.refs_1_), channel_id=1, source_target_pairs={{1,0},{0,1},{3,2},{2,3},{5,4},{4,5},{7,6},{6,7},{9,8},{8,9},{11,10... | collective-permute-start | bytes 737288 | tf_op jit(solution)/shard_map/ppermute | solution.py:472
  5.9 18.0 %collective-permute-start.3 = (bf16[128,960]{1,0:T(8,128)(2,1)S(1)}, bf16[128,960]{1,0:T(8,128)(2,1)S(1)}, u32[]{:S(2)}, u32[]{:S(2)}) collective-permute-start(bf16[128,960]{1,0:T(8,128)(2,1)S(1)} %get-tuple-element.94.refs_1_), channel_id=1, source_target_pairs={{1,0},{0,1},{3,2},{2,3},{5,4},{4,5},{7,6},{6,7},{9,8},{8,9},{11,10... | collective-permute-start | bytes 737288 | tf_op jit(solution)/shard_map/ppermute | solution.py:472
  7.9 20.8 %collective-permute-start = (bf16[128,960]{1,0:T(8,128)(2,1)S(1)}, bf16[128,960]{1,0:T(8,128)(2,1)S(1)}, u32[]{:S(2)}, u32[]{:S(2)}) collective-permute-start(bf16[128,960]{1,0:T(8,128)(2,1)S(1)} %get-tuple-element.90.refs_1_), channel_id=1, source_target_pairs={{1,0},{0,1},{3,2},{2,3},{5,4},{4,5},{7,6},{6,7},{9,8},{8,9},{11,10... | collective-permute-start | bytes 737288 | tf_op jit(solution)/shard_map/ppermute | solution.py:472
  8.0 6.3 %collective-permute-start.1 = (bf16[2,960]{1,0:T(2,128)(2,1)S(1)}, bf16[2,960]{1,0:T(2,128)(2,1)S(1)}, u32[]{:S(2)}, u32[]{:S(2)}) collective-permute-start(bf16[2,960]{1,0:T(2,128)(2,1)S(1)} %get-tuple-element.91), channel_id=1, source_target_pairs={{30,0},{0,2},{2,4},{4,6},{6,8},{8,10},{10,12},{12,14},{14,16},{16,... | collective-permute-start | bytes 11528 | tf_op jit(solution)/shard_map/ppermute | solution.py:472
  8.9 7.4 %copy-start.1 = (f32[16,960]{1,0:T(8,128)S(1)}, f32[16,960]{1,0:T(8,128)}, u32[]{:S(2)}) copy-start(f32[16,960]{1,0:T(8,128)} %refs_7_.7) | copy-start | bytes 184324
  8.9 7.4 %copy-start.3 = (f32[3,3,960]{2,1,0:T(4,128)S(1)}, f32[3,3,960]{2,1,0:T(4,128)}, u32[]{:S(2)}) copy-start(f32[3,3,960]{2,1,0:T(4,128)} %refs_4_.7) | copy-start | bytes 103684
  14.3 14.4 %collective-permute-start.2 = (bf16[2,960]{1,0:T(2,128)(2,1)S(1)}, bf16[2,960]{1,0:T(2,128)(2,1)S(1)}, u32[]{:S(2)}, u32[]{:S(2)}) collective-permute-start(bf16[2,960]{1,0:T(2,128)(2,1)S(1)} %collective-permute-done.1.refs_3_), channel_id=1, source_target_pairs={{1,0},{0,1},{3,2},{2,3},{5,4},{4,5},{7,6},{6,7},{9,8},{8,9},{11,10... | collective-permute-start | bytes 11528 | tf_op jit(solution)/shard_map/ppermute | solution.py:472
  28.7 15.4 %copy-start.4 = (f32[960]{0:T(1024)S(1)}, f32[960]{0:T(1024)}, u32[]{:S(2)}) copy-start(f32[960]{0:T(1024)} %param.14) | copy-start | bytes 11524
  33.1 3.3 %collective-permute-start.6 = (bf16[16,960]{1,0:T(8,128)(2,1)S(1)}, bf16[16,960]{1,0:T(8,128)(2,1)S(1)}, u32[]{:S(2)}, u32[]{:S(2)}) collective-permute-start(bf16[16,960]{1,0:T(8,128)(2,1)S(1)} %get-tuple-element.125), channel_id=1, source_target_pairs={{6,0},{0,2},{2,4},{4,6},{14,8},{8,10},{10,12},{12,14},{22,16},{16,... | collective-permute-start | bytes 92168 | tf_op jit(solution)/shard_map/ppermute | solution.py:523
  33.1 3.9 %collective-permute-start.7 = (bf16[16,960]{1,0:T(8,128)(2,1)S(1)}, bf16[16,960]{1,0:T(8,128)(2,1)S(1)}, u32[]{:S(2)}, u32[]{:S(2)}) collective-permute-start(bf16[16,960]{1,0:T(8,128)(2,1)S(1)} %get-tuple-element.125), channel_id=1, source_target_pairs={{4,0},{6,2},{0,4},{2,6},{12,8},{14,10},{8,12},{10,14},{20,16},{22,... | collective-permute-start | bytes 92168 | tf_op jit(solution)/shard_map/ppermute | solution.py:523
  34.9 3.0 %collective-permute-start.8 = (bf16[16,960]{1,0:T(8,128)(2,1)S(1)}, bf16[16,960]{1,0:T(8,128)(2,1)S(1)}, u32[]{:S(2)}, u32[]{:S(2)}) collective-permute-start(bf16[16,960]{1,0:T(8,128)(2,1)S(1)} %get-tuple-element.125), channel_id=1, source_target_pairs={{2,0},{4,2},{6,4},{0,6},{10,8},{12,10},{14,12},{8,14},{18,16},{20,... | collective-permute-start | bytes 92168 | tf_op jit(solution)/shard_map/ppermute | solution.py:523
  38.5 8.2 %collective-permute-start.9 = (bf16[24,960]{1,0:T(8,128)(2,1)S(1)}, bf16[24,960]{1,0:T(8,128)(2,1)S(1)}, u32[]{:S(2)}, u32[]{:S(2)}) collective-permute-start(bf16[24,960]{1,0:T(8,128)(2,1)S(1)} %get-tuple-element.127), channel_id=1, source_target_pairs={{24,0},{26,2},{28,4},{30,6},{0,8},{2,10},{4,12},{6,14},{8,16},{10,... | collective-permute-start | bytes 138248 | tf_op jit(solution)/shard_map/ppermute | solution.py:523
  40.2 6.0 %collective-permute-start.10 = (bf16[16,960]{1,0:T(8,128)(2,1)S(1)}, bf16[16,960]{1,0:T(8,128)(2,1)S(1)}, u32[]{:S(2)}, u32[]{:S(2)}) collective-permute-start(bf16[16,960]{1,0:T(8,128)(2,1)S(1)} %get-tuple-element.128), channel_id=1, source_target_pairs={{16,0},{18,2},{20,4},{22,6},{24,8},{26,10},{28,12},{30,14},{0,16},... | collective-permute-start | bytes 92168 | tf_op jit(solution)/shard_map/ppermute | solution.py:523
  42.8 3.9 %collective-permute-start.11 = (bf16[16,960]{1,0:T(8,128)(2,1)S(1)}, bf16[16,960]{1,0:T(8,128)(2,1)S(1)}, u32[]{:S(2)}, u32[]{:S(2)}) collective-permute-start(bf16[16,960]{1,0:T(8,128)(2,1)S(1)} %get-tuple-element.128), channel_id=1, source_target_pairs={{8,0},{10,2},{12,4},{14,6},{16,8},{18,10},{20,12},{22,14},{24,16},... | collective-permute-start | bytes 92168 | tf_op jit(solution)/shard_map/ppermute | solution.py:523
  44.1 3.2 %copy-start = (bf16[960,1920]{1,0:T(8,128)(2,1)S(1)}, bf16[960,1920]{1,0:T(8,128)(2,1)}, u32[]{:S(2)}) copy-start(bf16[960,1920]{1,0:T(8,128)(2,1)} %refs_9_.7) | copy-start | bytes 11059204
  49.8 8.4 %collective-permute-start.12 = (bf16[128,960]{1,0:T(8,128)(2,1)S(1)}, bf16[128,960]{1,0:T(8,128)(2,1)S(1)}, u32[]{:S(2)}, u32[]{:S(2)}) collective-permute-start(bf16[128,960]{1,0:T(8,128)(2,1)S(1)} %get-tuple-element.145), channel_id=1, source_target_pairs={{1,0},{0,1},{3,2},{2,3},{5,4},{4,5},{7,6},{6,7},{9,8},{8,9},{11,10... | collective-permute-start | bytes 737288 | tf_op jit(solution)/shard_map/ppermute | solution.py:472
  55.0 9.4 %collective-permute-start.13 = (bf16[128,960]{1,0:T(8,128)(2,1)S(1)}, bf16[128,960]{1,0:T(8,128)(2,1)S(1)}, u32[]{:S(2)}, u32[]{:S(2)}) collective-permute-start(bf16[128,960]{1,0:T(8,128)(2,1)S(1)} %get-tuple-element.151), channel_id=1, source_target_pairs={{1,0},{0,1},{3,2},{2,3},{5,4},{4,5},{7,6},{6,7},{9,8},{8,9},{11,10... | collective-permute-start | bytes 737288 | tf_op jit(solution)/shard_map/ppermute | solution.py:472
  61.9 7.3 %collective-permute-start.15 = (bf16[128,960]{1,0:T(8,128)(2,1)S(1)}, bf16[128,960]{1,0:T(8,128)(2,1)S(1)}, u32[]{:S(2)}, u32[]{:S(2)}) collective-permute-start(bf16[128,960]{1,0:T(8,128)(2,1)S(1)} %get-tuple-element.166), channel_id=1, source_target_pairs={{1,0},{0,1},{3,2},{2,3},{5,4},{4,5},{7,6},{6,7},{9,8},{8,9},{11,10... | collective-permute-start | bytes 737288 | tf_op jit(solution)/shard_map/ppermute | solution.py:472
  68.1 6.4 %collective-permute-start.14 = (bf16[128,960]{1,0:T(8,128)(2,1)S(1)}, bf16[128,960]{1,0:T(8,128)(2,1)S(1)}, u32[]{:S(2)}, u32[]{:S(2)}) collective-permute-start(bf16[128,960]{1,0:T(8,128)(2,1)S(1)} %get-tuple-element.158), channel_id=1, source_target_pairs={{1,0},{0,1},{3,2},{2,3},{5,4},{4,5},{7,6},{6,7},{9,8},{8,9},{11,10... | collective-permute-start | bytes 737288 | tf_op jit(solution)/shard_map/ppermute | solution.py:472

commit v3 on v2

--- a/solution.py
+++ b/solution.py
@@ -521,7 +521,7 @@
                 pairs.append((i + ((digit - shift) % radix - digit) * stride, i))
             first = shift == 1 and longer is not None
             others.append(lax.ppermute(longer if first else sent, axis, pairs))
-        others = between(stride, others[::-1])
+        others = between(others[::-1])
         shape = jax.ShapeDtypeStruct(state.shape, F32)
         carry = call(
             functools.partial(combine_states, span, stride, radix, count),
@@ -591,8 +591,8 @@
         k = len(done)
         done.append(run_local(out_rows[k], out_sizes[k], taps, normed, signal, states, *small))
 
-    def between(stride, others):
-        if stride > 1 and not done:
+    def between(others):
+        if not done:
             local_part()
             others, done[-1] = lax.optimization_barrier((others, done[-1]))
         return others

time: 76.1 us -> 76.3 us (level)
  transfers between devices with their start and end apart: 16 -> 16, of which waited for: 10 -> 7; matrix products, arithmetic and copies ran while one was open for 1% -> 1% of each run, Pallas kernels for 40% -> 40%
where the time goes in v3:
time: 76.3 us; the launch traced here: 76.1 us
  Pallas kernels  40.2 us (53%)
  starting transfers between devices  21.6 us (28%)
  waiting for transfers between devices  11.7 us (15%)
  local copies, waits for them, and re-layouts  1.23 us (2%)
  other arithmetic  0.99 us (1%)
    pallas_call x18, Pallas kernels, call(): pl.pallas_call(kernel, out_shape=outs, in_specs=[smem] * len(scalars) + [...  34.9 us
    ppermute x10, starting transfers between devices, rotate(): lax.ppermute(value, axis, [((i + steps) % count, i) for i in range(count)])  12.9 us
    ppermute x10, waiting for transfers between devices, rotate(): lax.ppermute(value, axis, [((i + steps) % count, i) for i in range(count)])  9.13 us
    ppermute x6, starting transfers between devices, carried_in(): others.append(lax.ppermute(longer if first else sent, axis, pairs))  8.74 us
    pallas_call x1, Pallas kernels, in_vmem(): pl.pallas_call(functools.partial(load_weights, places), out_shape=pltpu.V...  5.31 us
    ppermute x6, waiting for transfers between devices, carried_in(): others.append(lax.ppermute(longer if first else sent, axis, pairs))  2.58 us
  transfers between devices with their start and end apart: 16, of which 7 were waited for; matrix products, arithmetic and copies ran while one was open for 1% of the time, Pallas kernels for 40%

profile of v3, /device:TPU:0, one launch (start us, length us, event | category | flops | bytes accessed | tf_op | source)
XLA Modules:
  0.0 76.1 jit_solution(15478480989354305901)
XLA Ops:
  0.0 0.1 pad_add_fusion.refs_0_
  0.1 1.2 %copy-done.2 = bf16[960,512]{1,0:T(8,128)(2,1)S(1)} copy-done((bf16[960,512]{1,0:T(8,128)(2,1)S(1)}, bf16[960,512]{1,0:T(8,128)(2,1)}, u32[]{:S(2)}) %copy-start.2) | copy-done | bytes 983064
  1.3 0.5 first_rows.1
  1.7 3.0 %collective-permute-start.5 = (bf16[144,960]{1,0:T(8,128)(2,1)S(1)}, bf16[144,960]{1,0:T(8,128)(2,1)S(1)}, u32[]{:S(2)}, u32[]{:S(2)}) collective-permute-start(bf16[144,960]{1,0:T(8,128)(2,1)S(1)} %get-tuple-element.92.refs_1_), channel_id=1, source_target_pairs={{1,0},{0,1},{3,2},{2,3},{5,4},{4,5},{7,6},{6,7},{9,8},{8,9},{11,10... | collective-permute-start | bytes 829448 | tf_op jit(solution)/shard_map/ppermute | solution.py:472
  4.8 1.0 %next_rows.1 = (bf16[128,960]{1,0:T(8,128)(2,1)S(1)}, bf16[128,960]{1,0:T(8,128)(2,1)S(1)}, bf16[128,960]{1,0:T(8,128)(2,1)S(1)}) custom-call(bf16[960,512]{1,0:T(8,128)(2,1)S(1)} %copy-done.2), custom_call_target="tpu_custom_call" | custom-call | flops 1 | bytes 1 | tf_op jit(solution)/shard_map/next_rows/pallas_call | solution.py:360
  5.8 0.1 collective-permute-start.4
  5.9 2.0 %collective-permute-start.3 = (bf16[128,960]{1,0:T(8,128)(2,1)S(1)}, bf16[128,960]{1,0:T(8,128)(2,1)S(1)}, u32[]{:S(2)}, u32[]{:S(2)}) collective-permute-start(bf16[128,960]{1,0:T(8,128)(2,1)S(1)} %get-tuple-element.94.refs_1_), channel_id=1, source_target_pairs={{1,0},{0,1},{3,2},{2,3},{5,4},{4,5},{7,6},{6,7},{9,8},{8,9},{11,10... | collective-permute-start | bytes 737288 | tf_op jit(solution)/shard_map/ppermute | solution.py:472
  7.9 0.1 collective-permute-start
  8.0 0.0 collective-permute-start.1
  8.0 0.9 %sqrt_multiply_fusion.refs_6_.refs_8_ = f32[16,960]{1,0:T(8,128)S(1)} fusion(f32[16,960]{1,0:T(8,128)} %param.13, f32[16,960]{1,0:T(8,128)} %refs_7_.7), kind=kLoop, calls=%fused_computation | loop fusion | flops 46080 | bytes 184320 | tf_op jit(solution)/shard_map/mul | solution.py:565
  8.9 0.0 copy-start.1
  8.9 0.0 copy-start.3
  9.0 5.3 %load_weights.1.refs_4_.refs_9_.refs_11_.refs_3_ = bf16[3,1920,960]{2,1,0:T(8,128)(2,1)S(1)} custom-call(bf16[3,960,1920]{2,1,0:T(8,128)(2,1)} %w_hbm), custom_call_target="tpu_custom_call" | custom-call | flops 1 | bytes 1 | tf_op jit(solution)/shard_map/load_weights/pallas_call | solution.py:381
  14.3 0.0 collective-permute-done.1.refs_3_
  14.3 2.0 %collective-permute-start.2 = (bf16[2,960]{1,0:T(2,128)(2,1)S(1)}, bf16[2,960]{1,0:T(2,128)(2,1)S(1)}, u32[]{:S(2)}, u32[]{:S(2)}) collective-permute-start(bf16[2,960]{1,0:T(2,128)(2,1)S(1)} %collective-permute-done.1.refs_3_), channel_id=1, source_target_pairs={{1,0},{0,1},{3,2},{2,3},{5,4},{4,5},{7,6},{6,7},{9,8},{8,9},{11,10... | collective-permute-start | bytes 11528 | tf_op jit(solution)/shard_map/ppermute | solution.py:472
  16.3 0.0 collective-permute-done.5.refs_2_
  16.3 3.7 %signal_stage.4 = (bf16[528,1920]{1,0:T(8,128)(2,1)S(1)}, f32[512,960]{1,0:T(8,128)S(1)}, f32[4,16,8,960]{3,2,1,0:T(8,128)S(1)}, f32[16,8,960]{2,1,0:T(8,128)S(1)}, f32[2,16,960]{2,1,0:T(8,128)S(1)}) custom-call(s32[2]{0:T(128)S(1)} %pad_add_fusion.refs_0_, bf16[144,960]{1,0:T(8,128)(2,1)S(1)} %get-tuple-element.92.refs_1_, ...), custom_call_target="tpu_custom_call" | custom-call | flops 1 | bytes 1 | tf_op jit(solution)/shard_map/signal_stage/pallas_call | solution.py:360
  20.0 3.4 %signal_stage.5 = (bf16[528,1920]{1,0:T(8,128)(2,1)S(1)}, f32[512,960]{1,0:T(8,128)S(1)}, f32[4,16,8,960]{3,2,1,0:T(8,128)S(1)}, f32[16,8,960]{2,1,0:T(8,128)S(1)}, f32[2,16,960]{2,1,0:T(8,128)S(1)}) custom-call(s32[2]{0:T(128)S(1)} %pad_add_fusion.refs_0_, ...), custom_call_target="tpu_custom_call", output_to_operand_aliasing={{0}: (3, {}), {1}: (4, {}), {2}: (5, {})} | custom-call | flops 1 | bytes 1 | tf_op jit(solution)/shard_map/signal_stage/pallas_call | solution.py:360
  23.4 0.4 collective-permute-done.3.refs_2_
  23.9 3.4 %signal_stage.6 = (bf16[528,1920]{1,0:T(8,128)(2,1)S(1)}, f32[512,960]{1,0:T(8,128)S(1)}, f32[4,16,8,960]{3,2,1,0:T(8,128)S(1)}, f32[16,8,960]{2,1,0:T(8,128)S(1)}, f32[2,16,960]{2,1,0:T(8,128)S(1)}) custom-call(s32[2]{0:T(128)S(1)} %pad_add_fusion.refs_0_, ...), custom_call_target="tpu_custom_call", output_to_operand_aliasing={{0}: (3, {}), {1}: (4, {}), {2}: (5, {})} | custom-call | flops 1 | bytes 1 | tf_op jit(solution)/shard_map/signal_stage/pallas_call | solution.py:360
  27.3 1.5 %collective-permute-done.2.refs_4_ = bf16[2,960]{1,0:T(2,128)(2,1)S(1)} collective-permute-done((bf16[2,960]{1,0:T(2,128)(2,1)S(1)}, bf16[2,960]{1,0:T(2,128)(2,1)S(1)}, u32[]{:S(2)}, u32[]{:S(2)}) %collective-permute-start.2) | collective-permute-done | bytes 3872 | tf_op jit(solution)/shard_map/ppermute | solution.py:472
  28.7 4.4 %signal_stage.7 = (bf16[528,1920]{1,0:T(8,128)(2,1)S(1)}, f32[512,960]{1,0:T(8,128)S(1)}, f32[4,16,8,960]{3,2,1,0:T(8,128)S(1)}, f32[16,8,960]{2,1,0:T(8,128)S(1...) custom-call(s32[2]{0:T(128)S(1)} %pad_add_fusion.refs_0_, ...), custom_call_target="tpu_custom_call", output_to_operand_aliasing={{0}: (5, {}), {1}: (6, {}), {2}: (7, {})} | custom-call | flops 1 | bytes 1 | tf_op jit(solution)/shard_map/signal_stage/pallas_call | solution.py:360
  33.1 1.7 %collective-permute-start.7 = (bf16[16,960]{1,0:T(8,128)(2,1)S(1)}, bf16[16,960]{1,0:T(8,128)(2,1)S(1)}, u32[]{:S(2)}, u32[]{:S(2)}) collective-permute-start(bf16[16,960]{1,0:T(8,128)(2,1)S(1)} %get-tuple-element.125), channel_id=1, source_target_pairs={{4,0},{6,2},{0,4},{2,6},{12,8},{14,10},{8,12},{10,14},{20,16},{22,... | collective-permute-start | bytes 92168 | tf_op jit(solution)/shard_map/ppermute | solution.py:523
  34.9 1.4 %collective-permute-start.8 = (bf16[16,960]{1,0:T(8,128)(2,1)S(1)}, bf16[16,960]{1,0:T(8,128)(2,1)S(1)}, u32[]{:S(2)}, u32[]{:S(2)}) collective-permute-start(bf16[16,960]{1,0:T(8,128)(2,1)S(1)} %get-tuple-element.125), channel_id=1, source_target_pairs={{2,0},{4,2},{6,4},{0,6},{10,8},{12,10},{14,12},{8,14},{18,16},{20,... | collective-permute-start | bytes 92168 | tf_op jit(solution)/shard_map/ppermute | solution.py:523
  36.3 1.7 %local_stage.4 = (f32[128,960]{1,0:T(8,128)S(1)}, f32[128,960]{1,0:T(8,128)S(1)}, f32[16,8,960]{2,1,0:T(8,128)S(1)}, f32[16,8,960]{2,1,0:T(8,128)S(1)}) custom-call(bf16[528,1920]{1,0:T(8,128)(2,1)S(1)} %get-tuple-element.152.refs_0_, f32[512,960]{1,0:T(8,128)S(1)} %get-tuple-element.153.refs_1_, f32[16,8,960]{2,1,0:T(8,128)S(1)} %get-tuple-element.126.refs_2_, ...), custom_call_target="tpu_custom_call" | custom-call | flops 1 | bytes 1 | tf_op jit(solution)/shard_map/local_stage/pallas_call | solution.py:360
  38.1 0.6 combine_states.2
  38.7 1.6 %collective-permute-start.9 = (bf16[24,960]{1,0:T(8,128)(2,1)S(1)}, bf16[24,960]{1,0:T(8,128)(2,1)S(1)}, u32[]{:S(2)}, u32[]{:S(2)}) collective-permute-start(bf16[24,960]{1,0:T(8,128)(2,1)S(1)} %get-tuple-element.137), channel_id=1, source_target_pairs={{24,0},{26,2},{28,4},{30,6},{0,8},{2,10},{4,12},{6,14},{8,16},{10,... | collective-permute-start | bytes 138248 | tf_op jit(solution)/shard_map/ppermute | solution.py:523
  40.4 2.6 %collective-permute-start.10 = (bf16[16,960]{1,0:T(8,128)(2,1)S(1)}, bf16[16,960]{1,0:T(8,128)(2,1)S(1)}, u32[]{:S(2)}, u32[]{:S(2)}) collective-permute-start(bf16[16,960]{1,0:T(8,128)(2,1)S(1)} %get-tuple-element.138), channel_id=1, source_target_pairs={{16,0},{18,2},{20,4},{22,6},{24,8},{26,10},{28,12},{30,14},{0,16},... | collective-permute-start | bytes 92168 | tf_op jit(solution)/shard_map/ppermute | solution.py:523
  43.0 1.3 %collective-permute-start.11 = (bf16[16,960]{1,0:T(8,128)(2,1)S(1)}, bf16[16,960]{1,0:T(8,128)(2,1)S(1)}, u32[]{:S(2)}, u32[]{:S(2)}) collective-permute-start(bf16[16,960]{1,0:T(8,128)(2,1)S(1)} %get-tuple-element.138), channel_id=1, source_target_pairs={{8,0},{10,2},{12,4},{14,6},{16,8},{18,10},{20,12},{22,14},{24,16},... | collective-permute-start | bytes 92168 | tf_op jit(solution)/shard_map/ppermute | solution.py:523
  44.3 1.9 %collective-permute-done.10.refs_4_ = bf16[16,960]{1,0:T(8,128)(2,1)S(1)} collective-permute-done((bf16[16,960]{1,0:T(8,128)(2,1)S(1)}, bf16[16,960]{1,0:T(8,128)(2,1)S(1)}, u32[]{:S(2)}, u32[]{:S(2)}) %collective-permute-start.10) | collective-permute-done | bytes 30752 | tf_op jit(solution)/shard_map/ppermute | solution.py:523
  46.2 0.6 collective-permute-done.11.refs_5_
  46.9 0.6 combine_states.3.refs_6_
  47.5 2.5 %second_stage.4 = (bf16[128,960]{1,0:T(8,128)(2,1)S(1)}, f32[128,960]{1,0:T(8,128)S(1)}) custom-call(s32[2]{0:T(128)S(1)} %pad_add_fusion.refs_0_, f32[128,960]{1,0:T(8,128)S(1)} %get-tuple-element.140.refs_1_, f32[128,960]{1,0:T(8,128)S(1)} %get-tuple-element.141.refs_2_, f32[16,8,960]{2,1,0:T(8,128)S(1)} %get-tuple-element.142.refs_3_, ...), custom_call_target="tpu_custom_call" | custom-call | flops 1 | bytes 1 | tf_op jit(solution)/shard_map/second_stage/pallas_call | solution.py:360
  50.0 1.6 %collective-permute-start.12 = (bf16[128,960]{1,0:T(8,128)(2,1)S(1)}, bf16[128,960]{1,0:T(8,128)(2,1)S(1)}, u32[]{:S(2)}, u32[]{:S(2)}) collective-permute-start(bf16[128,960]{1,0:T(8,128)(2,1)S(1)} %get-tuple-element.145), channel_id=1, source_target_pairs={{1,0},{0,1},{3,2},{2,3},{5,4},{4,5},{7,6},{6,7},{9,8},{8,9},{11,10... | collective-permute-start | bytes 737288 | tf_op jit(solution)/shard_map/ppermute | solution.py:472
  51.6 1.3 %local_stage.5 = (f32[128,960]{1,0:T(8,128)S(1)}, f32[128,960]{1,0:T(8,128)S(1)}) custom-call(bf16[528,1920]{1,0:T(8,128)(2,1)S(1)} %get-tuple-element.152.refs_0_, f32[512,960]{1,0:T(8,128)S(1)} %get-tuple-element.153.refs_1_, f32[16,8,960]{2,1,0:T(8,128)S(1)} %get-tuple-element.126.refs_2_, ...), custom_call_target="tpu_custom_call" | custom-call | flops 1 | bytes 1 | tf_op jit(solution)/shard_map/local_stage/pallas_call | solution.py:360
  52.8 2.3 %second_stage.5 = (bf16[128,960]{1,0:T(8,128)(2,1)S(1)}, f32[128,960]{1,0:T(8,128)S(1)}) custom-call(s32[2]{0:T(128)S(1)} %pad_add_fusion.refs_0_, f32[128,960]{1,0:T(8,128)S(1)} %get-tuple-element.149.refs_1_, f32[128,960]{1,0:T(8,128)S(1)} %get-tuple-element.150.refs_2_, f32[16,8,960]{2,1,0:T(8,128)S(1)} %get-tuple-element.142.refs_3_, ...), custom_call_target="tpu_custom_call" | custom-call | flops 1 | bytes 1 | tf_op jit(solution)/shard_map/second_stage/pallas_call | solution.py:360
  55.2 0.6 collective-permute-start.13
  55.8 2.6 %collective-permute-done.12.refs_3_ = bf16[128,960]{1,0:T(8,128)(2,1)S(1)} collective-permute-done((bf16[128,960]{1,0:T(8,128)(2,1)S(1)}, bf16[128,960]{1,0:T(8,128)(2,1)S(1)}, u32[]{:S(2)}, u32[]{:S(2)}) %collective-permute-start.12) | collective-permute-done | bytes 245792 | tf_op jit(solution)/shard_map/ppermute | solution.py:472
  58.3 1.3 %local_stage.7 = (f32[128,960]{1,0:T(8,128)S(1)}, f32[128,960]{1,0:T(8,128)S(1)}) custom-call(bf16[528,1920]{1,0:T(8,128)(2,1)S(1)} %get-tuple-element.152.refs_0_, f32[512,960]{1,0:T(8,128)S(1)} %get-tuple-element.153.refs_1_, f32[16,8,960]{2,1,0:T(8,128)S(1)} %get-tuple-element.126.refs_2_, ...), custom_call_target="tpu_custom_call" | custom-call | flops 1 | bytes 1 | tf_op jit(solution)/shard_map/local_stage/pallas_call | solution.py:360
  59.6 2.4 %second_stage.7 = (bf16[128,960]{1,0:T(8,128)(2,1)S(1)}, f32[128,960]{1,0:T(8,128)S(1)}) custom-call(s32[2]{0:T(128)S(1)} %pad_add_fusion.refs_0_, f32[128,960]{1,0:T(8,128)S(1)} %get-tuple-element.161.refs_1_, f32[128,960]{1,0:T(8,128)S(1)} %get-tuple-element.162.refs_2_, f32[16,8,960]{2,1,0:T(8,128)S(1)} %get-tuple-element.142.refs_3_, ...), custom_call_target="tpu_custom_call" | custom-call | flops 1 | bytes 1 | tf_op jit(solution)/shard_map/second_stage/pallas_call | solution.py:360
  62.0 2.5 %collective-permute-start.15 = (bf16[128,960]{1,0:T(8,128)(2,1)S(1)}, bf16[128,960]{1,0:T(8,128)(2,1)S(1)}, u32[]{:S(2)}, u32[]{:S(2)}) collective-permute-start(bf16[128,960]{1,0:T(8,128)(2,1)S(1)} %get-tuple-element.166), channel_id=1, source_target_pairs={{1,0},{0,1},{3,2},{2,3},{5,4},{4,5},{7,6},{6,7},{9,8},{8,9},{11,10... | collective-permute-start | bytes 737288 | tf_op jit(solution)/shard_map/ppermute | solution.py:472
  64.6 1.3 %local_stage.6 = (f32[128,960]{1,0:T(8,128)S(1)}, f32[128,960]{1,0:T(8,128)S(1)}) custom-call(bf16[528,1920]{1,0:T(8,128)(2,1)S(1)} %get-tuple-element.152.refs_0_, f32[512,960]{1,0:T(8,128)S(1)} %get-tuple-element.153.refs_1_, f32[16,8,960]{2,1,0:T(8,128)S(1)} %get-tuple-element.126.refs_2_, ...), custom_call_target="tpu_custom_call" | custom-call | flops 1 | bytes 1 | tf_op jit(solution)/shard_map/local_stage/pallas_call | solution.py:360
  65.9 2.4 %second_stage.6 = (bf16[128,960]{1,0:T(8,128)(2,1)S(1)}, f32[128,960]{1,0:T(8,128)S(1)}) custom-call(s32[2]{0:T(128)S(1)} %pad_add_fusion.refs_0_, f32[128,960]{1,0:T(8,128)S(1)} %get-tuple-element.154.refs_1_, f32[128,960]{1,0:T(8,128)S(1)} %get-tuple-element.155.refs_2_, f32[16,8,960]{2,1,0:T(8,128)S(1)} %get-tuple-element.142.refs_3_, ...), custom_call_target="tpu_custom_call" | custom-call | flops 1 | bytes 1 | tf_op jit(solution)/shard_map/second_stage/pallas_call | solution.py:360
  68.3 1.0 %collective-permute-start.14 = (bf16[128,960]{1,0:T(8,128)(2,1)S(1)}, bf16[128,960]{1,0:T(8,128)(2,1)S(1)}, u32[]{:S(2)}, u32[]{:S(2)}) collective-permute-start(bf16[128,960]{1,0:T(8,128)(2,1)S(1)} %get-tuple-element.158), channel_id=1, source_target_pairs={{1,0},{0,1},{3,2},{2,3},{5,4},{4,5},{7,6},{6,7},{9,8},{8,9},{11,10... | collective-permute-start | bytes 737288 | tf_op jit(solution)/shard_map/ppermute | solution.py:472
  69.3 0.5 collective-permute-done.15.refs_5_
  69.7 0.8 last_stage.2.refs_2_
  70.5 4.2 %collective-permute-done.14.refs_1_ = bf16[128,960]{1,0:T(8,128)(2,1)S(1)} collective-permute-done((bf16[128,960]{1,0:T(8,128)(2,1)S(1)}, bf16[128,960]{1,0:T(8,128)(2,1)S(1)}, u32[]{:S(2)}, u32[]{:S(2)}) %collective-permute-start.14) | collective-permute-done | bytes 245792 | tf_op jit(solution)/shard_map/ppermute | solution.py:472
  74.7 1.2 %last_stage.3 = bf16[960,512]{1,0:T(8,128)(2,1)} custom-call(f32[128,960]{1,0:T(8,128)S(1)} %get-tuple-element.157.refs_0_, bf16[128,960]{1,0:T(8,128)(2,1)S(1)} %collective-permute-done.14.refs_1_, bf16[960,512]{1,0:T(8,128)(2,1)S(1)} %last_stage.2.refs_2_), custom_call_target="tpu_custom_call" | custom-call | flops 1 | bytes 1 | tf_op jit(solution)/shard_map/last_stage/pallas_call | solution.py:360
  (18 shorter events, 0.0 us)
Async XLA Ops:
  0.0 8.9 %copy-start.5 = (f32[1920]{0:T(1024)S(1)}, f32[1920]{0:T(1024)}, u32[]{:S(2)}) copy-start(f32[1920]{0:T(1024)} %param.9) | copy-start | bytes 23044
  0.1 1.2 %copy-start.2 = (bf16[960,512]{1,0:T(8,128)(2,1)S(1)}, bf16[960,512]{1,0:T(8,128)(2,1)}, u32[]{:S(2)}) copy-start(bf16[960,512]{1,0:T(8,128)(2,1)} %tokens_ref.1) | copy-start | bytes 2949124
  1.7 14.6 %collective-permute-start.5 = (bf16[144,960]{1,0:T(8,128)(2,1)S(1)}, bf16[144,960]{1,0:T(8,128)(2,1)S(1)}, u32[]{:S(2)}, u32[]{:S(2)}) collective-permute-start(bf16[144,960]{1,0:T(8,128)(2,1)S(1)} %get-tuple-element.92.refs_1_), channel_id=1, source_target_pairs={{1,0},{0,1},{3,2},{2,3},{5,4},{4,5},{7,6},{6,7},{9,8},{8,9},{11,10... | collective-permute-start | bytes 829448 | tf_op jit(solution)/shard_map/ppermute | solution.py:472
  5.8 14.2 %collective-permute-start.4 = (bf16[128,960]{1,0:T(8,128)(2,1)S(1)}, bf16[128,960]{1,0:T(8,128)(2,1)S(1)}, u32[]{:S(2)}, u32[]{:S(2)}) collective-permute-start(bf16[128,960]{1,0:T(8,128)(2,1)S(1)} %get-tuple-element.93.refs_1_), channel_id=1, source_target_pairs={{1,0},{0,1},{3,2},{2,3},{5,4},{4,5},{7,6},{6,7},{9,8},{8,9},{11,10... | collective-permute-start | bytes 737288 | tf_op jit(solution)/shard_map/ppermute | solution.py:472
  5.9 18.0 %collective-permute-start.3 = (bf16[128,960]{1,0:T(8,128)(2,1)S(1)}, bf16[128,960]{1,0:T(8,128)(2,1)S(1)}, u32[]{:S(2)}, u32[]{:S(2)}) collective-permute-start(bf16[128,960]{1,0:T(8,128)(2,1)S(1)} %get-tuple-element.94.refs_1_), channel_id=1, source_target_pairs={{1,0},{0,1},{3,2},{2,3},{5,4},{4,5},{7,6},{6,7},{9,8},{8,9},{11,10... | collective-permute-start | bytes 737288 | tf_op jit(solution)/shard_map/ppermute | solution.py:472
  7.9 20.8 %collective-permute-start = (bf16[128,960]{1,0:T(8,128)(2,1)S(1)}, bf16[128,960]{1,0:T(8,128)(2,1)S(1)}, u32[]{:S(2)}, u32[]{:S(2)}) collective-permute-start(bf16[128,960]{1,0:T(8,128)(2,1)S(1)} %get-tuple-element.90.refs_1_), channel_id=1, source_target_pairs={{1,0},{0,1},{3,2},{2,3},{5,4},{4,5},{7,6},{6,7},{9,8},{8,9},{11,10... | collective-permute-start | bytes 737288 | tf_op jit(solution)/shard_map/ppermute | solution.py:472
  8.0 6.3 %collective-permute-start.1 = (bf16[2,960]{1,0:T(2,128)(2,1)S(1)}, bf16[2,960]{1,0:T(2,128)(2,1)S(1)}, u32[]{:S(2)}, u32[]{:S(2)}) collective-permute-start(bf16[2,960]{1,0:T(2,128)(2,1)S(1)} %get-tuple-element.91), channel_id=1, source_target_pairs={{30,0},{0,2},{2,4},{4,6},{6,8},{8,10},{10,12},{12,14},{14,16},{16,... | collective-permute-start | bytes 11528 | tf_op jit(solution)/shard_map/ppermute | solution.py:472
  8.9 7.4 %copy-start.1 = (f32[16,960]{1,0:T(8,128)S(1)}, f32[16,960]{1,0:T(8,128)}, u32[]{:S(2)}) copy-start(f32[16,960]{1,0:T(8,128)} %refs_7_.7) | copy-start | bytes 184324
  8.9 7.4 %copy-start.3 = (f32[3,3,960]{2,1,0:T(4,128)S(1)}, f32[3,3,960]{2,1,0:T(4,128)}, u32[]{:S(2)}) copy-start(f32[3,3,960]{2,1,0:T(4,128)} %refs_4_.7) | copy-start | bytes 103684
  14.3 14.4 %collective-permute-start.2 = (bf16[2,960]{1,0:T(2,128)(2,1)S(1)}, bf16[2,960]{1,0:T(2,128)(2,1)S(1)}, u32[]{:S(2)}, u32[]{:S(2)}) collective-permute-start(bf16[2,960]{1,0:T(2,128)(2,1)S(1)} %collective-permute-done.1.refs_3_), channel_id=1, source_target_pairs={{1,0},{0,1},{3,2},{2,3},{5,4},{4,5},{7,6},{6,7},{9,8},{8,9},{11,10... | collective-permute-start | bytes 11528 | tf_op jit(solution)/shard_map/ppermute | solution.py:472
  28.7 7.6 %copy-start.4 = (f32[960]{0:T(1024)S(1)}, f32[960]{0:T(1024)}, u32[]{:S(2)}) copy-start(f32[960]{0:T(1024)} %param.14) | copy-start | bytes 11524
  33.1 4.9 %collective-permute-start.6 = (bf16[16,960]{1,0:T(8,128)(2,1)S(1)}, bf16[16,960]{1,0:T(8,128)(2,1)S(1)}, u32[]{:S(2)}, u32[]{:S(2)}) collective-permute-start(bf16[16,960]{1,0:T(8,128)(2,1)S(1)} %get-tuple-element.125), channel_id=1, source_target_pairs={{6,0},{0,2},{2,4},{4,6},{14,8},{8,10},{10,12},{12,14},{22,16},{16,... | collective-permute-start | bytes 92168 | tf_op jit(solution)/shard_map/ppermute | solution.py:523
  33.1 4.9 %collective-permute-start.7 = (bf16[16,960]{1,0:T(8,128)(2,1)S(1)}, bf16[16,960]{1,0:T(8,128)(2,1)S(1)}, u32[]{:S(2)}, u32[]{:S(2)}) collective-permute-start(bf16[16,960]{1,0:T(8,128)(2,1)S(1)} %get-tuple-element.125), channel_id=1, source_target_pairs={{4,0},{6,2},{0,4},{2,6},{12,8},{14,10},{8,12},{10,14},{20,16},{22,... | collective-permute-start | bytes 92168 | tf_op jit(solution)/shard_map/ppermute | solution.py:523
  34.9 3.2 %collective-permute-start.8 = (bf16[16,960]{1,0:T(8,128)(2,1)S(1)}, bf16[16,960]{1,0:T(8,128)(2,1)S(1)}, u32[]{:S(2)}, u32[]{:S(2)}) collective-permute-start(bf16[16,960]{1,0:T(8,128)(2,1)S(1)} %get-tuple-element.125), channel_id=1, source_target_pairs={{2,0},{4,2},{6,4},{0,6},{10,8},{12,10},{14,12},{8,14},{18,16},{20,... | collective-permute-start | bytes 92168 | tf_op jit(solution)/shard_map/ppermute | solution.py:523
  36.3 11.2 %copy-start = (bf16[960,1920]{1,0:T(8,128)(2,1)S(1)}, bf16[960,1920]{1,0:T(8,128)(2,1)}, u32[]{:S(2)}) copy-start(bf16[960,1920]{1,0:T(8,128)(2,1)} %refs_9_.7) | copy-start | bytes 11059204
  38.7 8.1 %collective-permute-start.9 = (bf16[24,960]{1,0:T(8,128)(2,1)S(1)}, bf16[24,960]{1,0:T(8,128)(2,1)S(1)}, u32[]{:S(2)}, u32[]{:S(2)}) collective-permute-start(bf16[24,960]{1,0:T(8,128)(2,1)S(1)} %get-tuple-element.137), channel_id=1, source_target_pairs={{24,0},{26,2},{28,4},{30,6},{0,8},{2,10},{4,12},{6,14},{8,16},{10,... | collective-permute-start | bytes 138248 | tf_op jit(solution)/shard_map/ppermute | solution.py:523
  40.4 5.9 %collective-permute-start.10 = (bf16[16,960]{1,0:T(8,128)(2,1)S(1)}, bf16[16,960]{1,0:T(8,128)(2,1)S(1)}, u32[]{:S(2)}, u32[]{:S(2)}) collective-permute-start(bf16[16,960]{1,0:T(8,128)(2,1)S(1)} %get-tuple-element.138), channel_id=1, source_target_pairs={{16,0},{18,2},{20,4},{22,6},{24,8},{26,10},{28,12},{30,14},{0,16},... | collective-permute-start | bytes 92168 | tf_op jit(solution)/shard_map/ppermute | solution.py:523
  43.0 3.9 %collective-permute-start.11 = (bf16[16,960]{1,0:T(8,128)(2,1)S(1)}, bf16[16,960]{1,0:T(8,128)(2,1)S(1)}, u32[]{:S(2)}, u32[]{:S(2)}) collective-permute-start(bf16[16,960]{1,0:T(8,128)(2,1)S(1)} %get-tuple-element.138), channel_id=1, source_target_pairs={{8,0},{10,2},{12,4},{14,6},{16,8},{18,10},{20,12},{22,14},{24,16},... | collective-permute-start | bytes 92168 | tf_op jit(solution)/shard_map/ppermute | solution.py:523
  50.0 8.3 %collective-permute-start.12 = (bf16[128,960]{1,0:T(8,128)(2,1)S(1)}, bf16[128,960]{1,0:T(8,128)(2,1)S(1)}, u32[]{:S(2)}, u32[]{:S(2)}) collective-permute-start(bf16[128,960]{1,0:T(8,128)(2,1)S(1)} %get-tuple-element.145), channel_id=1, source_target_pairs={{1,0},{0,1},{3,2},{2,3},{5,4},{4,5},{7,6},{6,7},{9,8},{8,9},{11,10... | collective-permute-start | bytes 737288 | tf_op jit(solution)/shard_map/ppermute | solution.py:472
  55.2 9.4 %collective-permute-start.13 = (bf16[128,960]{1,0:T(8,128)(2,1)S(1)}, bf16[128,960]{1,0:T(8,128)(2,1)S(1)}, u32[]{:S(2)}, u32[]{:S(2)}) collective-permute-start(bf16[128,960]{1,0:T(8,128)(2,1)S(1)} %get-tuple-element.151), channel_id=1, source_target_pairs={{1,0},{0,1},{3,2},{2,3},{5,4},{4,5},{7,6},{6,7},{9,8},{8,9},{11,10... | collective-permute-start | bytes 737288 | tf_op jit(solution)/shard_map/ppermute | solution.py:472
  62.0 7.7 %collective-permute-start.15 = (bf16[128,960]{1,0:T(8,128)(2,1)S(1)}, bf16[128,960]{1,0:T(8,128)(2,1)S(1)}, u32[]{:S(2)}, u32[]{:S(2)}) collective-permute-start(bf16[128,960]{1,0:T(8,128)(2,1)S(1)} %get-tuple-element.166), channel_id=1, source_target_pairs={{1,0},{0,1},{3,2},{2,3},{5,4},{4,5},{7,6},{6,7},{9,8},{8,9},{11,10... | collective-permute-start | bytes 737288 | tf_op jit(solution)/shard_map/ppermute | solution.py:472
  68.3 6.4 %collective-permute-start.14 = (bf16[128,960]{1,0:T(8,128)(2,1)S(1)}, bf16[128,960]{1,0:T(8,128)(2,1)S(1)}, u32[]{:S(2)}, u32[]{:S(2)}) collective-permute-start(bf16[128,960]{1,0:T(8,128)(2,1)S(1)} %get-tuple-element.158), channel_id=1, source_target_pairs={{1,0},{0,1},{3,2},{2,3},{5,4},{4,5},{7,6},{6,7},{9,8},{8,9},{11,10... | collective-permute-start | bytes 737288 | tf_op jit(solution)/shard_map/ppermute | solution.py:472

commit v4 on v3

--- a/solution.py
+++ b/solution.py
@@ -75,12 +75,12 @@
     column = lax.broadcasted_iota(jnp.int32, (halo, tokens), 1)
     last = edge_ref.shape[0]
     picks = [
-        token_picker(size - halo, halo + size, tokens),
+        token_picker(size, size, tokens),
         jnp.where((row < last) & (column == tokens - last + row), 1.0, 0.0).astype(BF16),
     ]
     rows = turned(jnp.concatenate(picks, axis=0), tokens_ref[...])
-    out_ref[...] = rows[: halo + size]
-    edge_ref[...] = rows[halo + size : halo + size + last]
+    out_ref[...] = rows[:size]
+    edge_ref[...] = rows[size : size + last]
 
 
 def next_rows(firsts, tokens_ref, *chunk_refs):
@@ -122,15 +122,17 @@
     token_refs = [refs.pop(0) for _ in range(pieces)]
     x_ref, p_ref = refs[-2:]
     halo = ROWS * (taps - 1)
-    rows, share = p_ref.shape[0] - halo, token_refs[0].shape[1]
+    rows, share = token_refs[0].shape
     last, start = row == 0, row == rows
     fresh = last or start
-    read = rows + halo if fresh else rows
+    read = rows + halo if last else rows
     edge_refs = [refs.pop(0) for _ in range(pieces)] if last else []
     if not start:
         normed_in, _, _, states_in, tail_in = [refs.pop(0) for _ in range(5)]
+    heads_in = refs.pop(0) if last else None
     gain_ref, w_ref, short_ref, rate_ref = refs[:4]
     normed_ref, signal_ref, marks_ref, states_ref, tail_ref = refs[4:9]
+    heads_ref = refs[9] if start else None
     total_ref, sent_ref = refs[9:11] if last else (None, None)
     modes, channels = rate_ref.shape
     length = signal_ref.shape[0] // ROWS
@@ -161,26 +163,34 @@
         ]
         normed = jnp.concatenate(front + [normed[halo:]], axis=0)
     normed = normed.astype(BF16)
-    begin = row if fresh else halo + row
+    begin = 0 if last else halo + row
     normed_ref[begin : begin + read, :] = normed
 
     for low in range(0, channels, BLOCK):
         width = min(BLOCK, channels - low)
         part = slice(low, low + width)
         for s in (1, 2):
-            if not fresh:
+            if start:
+                p_ref[:halo, :width] = jnp.zeros((halo, width), F32)
+            elif not last:
                 p_ref[:halo, :width] = tail_in[s - 1, :, part]
-            p_ref[halo + rows - read :, :width] = project(
+            p_ref[halo + rows - read : halo + rows, :width] = project(
                 normed_ref[begin : begin + read, :], w_ref, s, part
             )
-            tail_ref[s - 1, :, part] = p_ref[rows:, :width]
-            short = short_conv(p_ref, short_ref, s, part, rows, taps)
+            if last:
+                p_ref[halo + rows :, :width] = heads_in[s - 1, :, part]
+            if start:
+                heads_ref[s - 1, :, part] = p_ref[halo : 2 * halo, :width]
+            tail_ref[s - 1, :, part] = p_ref[rows : rows + halo, :width]
+            short = short_conv(p_ref, short_ref, s, part, p_ref.shape[0] - halo, taps)
+            front = halo if start else 0
+            there = slice(row + front, row + short.shape[0])
             if s == 1:
-                signal_ref[row : row + rows, part] = short
+                signal_ref[there, part] = short[front:]
             else:
-                signal_ref[row : row + rows, part] = signal_ref[row : row + rows, part] * short
-        for start, size in lane_groups(low, width):
-            lanes = slice(start, start + size)
+                signal_ref[there, part] = signal_ref[there, part] * short[front:]
+        for lane, size in lane_groups(low, width):
+            lanes = slice(lane, lane + size)
             decay = decays(rate_ref, lanes, size, 1.0)
 
             if fresh:
@@ -195,11 +205,19 @@
                 now = signal_ref[here, lanes]
                 return tuple(states[n] * decay[n] + now for n in range(modes))
 
-            states = lax.fori_loop(0, rows // ROWS, step, states, unroll=8)
+            steps = rows // ROWS
+            skipped = taps - 1 if start else 0
+            unroll = next(k for k in (8, 7, 4, 2, 1) if (steps - skipped) % k == 0)
+            states = lax.fori_loop(skipped, steps, step, states, unroll=unroll)
             if last:
                 for n in range(modes):
                     marks_ref[1, n, :, lanes] = states[n]
-                later = decays(rate_ref, lanes, size, float(length - rows // ROWS))
+                for at in range(rows, rows + halo, ROWS):
+                    now = signal_ref[at : at + ROWS, lanes]
+                    states = tuple(states[n] * decay[n] + now for n in range(modes))
+                for n in range(modes):
+                    marks_ref[0, n, :, lanes] = states[n]
+                later = decays(rate_ref, lanes, size, float(length - steps - (taps - 1)))
                 states = tuple(states_in[n, :, lanes] + later[n] * states[n] for n in range(modes))
             for n in range(modes):
                 states_ref[n, :, lanes] = states[n]
@@ -273,7 +291,7 @@
             lax.fori_loop(0, rows // (SPAN * ROWS), span, 0)
 
 
-def second_stage(pieces, row, rows, *refs):
+def second_stage(pieces, row, rows, ahead, *refs):
     me_ref, q_ref, local_ref, begin_ref, past_ref, marks_ref, carry_ref = refs[:7]
     rate_ref, mode_ref, w_ref, send_ref, own_ref, gated_ref = refs[7:]
     modes, channels = rate_ref.shape
@@ -286,12 +304,19 @@
                 begin_ref[n, :, lanes] + past_ref[n, :, lanes] * carry_ref[n : n + 1, lanes]
                 for n in range(modes)
             ]
-            for known, steps in ((1, SPAN), (mark, SPAN * (mark - 1))):
-                if mark >= max(known, 1) and steps > 0:
-                    less = decays(rate_ref, lanes, size, float(steps))
+            for known, steps in ((mark, SPAN * mark), (0, SPAN * (mark - 1) - ahead)):
+                if steps <= 0:
+                    continue
+                less = decays(rate_ref, lanes, size, float(steps))
+                mode = [mode_ref[n : n + 1, lanes] for n in range(modes)]
+                if known:
                     states = [
-                        mode_ref[n : n + 1, lanes] * marks_ref[known, n, :, lanes]
-                        + states[n] * less[n]
+                        mode[n] * marks_ref[known, n, :, lanes] + states[n] * less[n]
+                        for n in range(modes)
+                    ]
+                else:
+                    states = [
+                        states[n] + mode[n] * marks_ref[0, n, :, lanes] * less[n]
                         for n in range(modes)
                     ]
 
@@ -404,6 +429,8 @@
         jax.ShapeDtypeStruct((modes, ROWS, channels), F32),
         jax.ShapeDtypeStruct((streams - 1, halo, channels), F32),
     ]
+    if row == rows:
+        outs.append(outs[-1])
     if row == 0:
         outs += [jax.ShapeDtypeStruct((modes, channels), kind) for kind in (F32, BF16)]
     return call(
@@ -413,8 +440,8 @@
         list(tokens) + list(edges) + list(before) + [gain, w_in, w_short, rate],
         outs,
         [
-            pltpu.VMEM((rows + (halo if row in (0, rows) else 0), features), F32),
-            pltpu.VMEM((halo + rows, min(BLOCK, channels)), F32),
+            pltpu.VMEM((rows + (halo if row == 0 else 0), features), F32),
+            pltpu.VMEM((rows + halo * (2 if row == 0 else 1), min(BLOCK, channels)), F32),
         ],
         aliases={1 + len(tokens) + len(edges) + k: k for k in range(3)} if before else {},
     )
@@ -434,11 +461,11 @@
     )
 
 
-def run_second(pieces, row, rows, place, q, local, begin, past, marks, carry, rate, mode, w):
+def run_second(pieces, row, rows, ahead, place, q, local, begin, past, marks, carry, rate, mode, w):
     channels, features = w.shape
     share = features // pieces
     return call(
-        functools.partial(second_stage, pieces, row, rows),
+        functools.partial(second_stage, pieces, row, rows, ahead),
         "second_stage",
         [place],
         [q, local, begin, past, marks, carry, rate, mode, w],
@@ -552,7 +579,7 @@
     tokens, place = lax.optimization_barrier((tokens, place))
     x1, edge = call(
         functools.partial(first_rows, halo, size), "first_rows", [], [tokens],
-        [bf16_rows(halo + size), bf16_rows(taps - 1)], [],
+        [bf16_rows(size), bf16_rows(taps - 1)], [],
     )
     edge = rotate(edge, "ctx", -1)
     tokens, x1 = lax.optimization_barrier((tokens, x1))
@@ -574,10 +601,13 @@
     before = []
     for part, j in zip(parts, list(range(1, CHUNKS)) + [0]):
         results = run_signal(
-            pieces, j * size, size, rows, taps, place, part, [] if j else edges, before, gain, w_in,
+            pieces, j * size, size, rows, taps, place, part, [] if j else edges,
+            before if j else [*before, heads], gain, w_in,
             w_short, decay_rate,
         )
         before = results[:5]
+        if j == 1:
+            heads = results[5]
     normed, signal, marks, states, _ = before
     state, sent, normed, signal, states = lax.optimization_barrier(
         (results[5], results[6], normed, signal, states)
@@ -611,7 +641,7 @@
         if j > 0:
             local_part()
         send, kept = run_second(
-            pieces, out_rows[j], out_sizes[j], place, *done[j][:2], begin, past, marks, carry,
+            pieces, out_rows[j], out_sizes[j], taps - 1, place, *done[j][:2], begin, past, marks, carry,
             decay_rate, mode, w_out,
         )
         own.append(kept)

time: 76.3 us -> 75.4 us (0.988)
  transfers between devices with their start and end apart: 16 -> 16, of which waited for: 7 -> 5; matrix products, arithmetic and copies ran while one was open for 1% -> 1% of each run, Pallas kernels for 40% -> 40%
where the time goes in v4:
time: 75.4 us; the launch traced here: 75.2 us
  Pallas kernels  40.1 us (53%)
  starting transfers between devices  21.5 us (29%)
  waiting for transfers between devices  11 us (15%)
  local copies, waits for them, and re-layouts  1.23 us (2%)
  other arithmetic  0.99 us (1%)
    pallas_call x18, Pallas kernels, call(): pl.pallas_call(kernel, out_shape=outs, in_specs=[smem] * len(scalars) + [...  34.8 us
    ppermute x10, starting transfers between devices, rotate(): lax.ppermute(value, axis, [((i + steps) % count, i) for i in range(count)])  12.7 us
    ppermute x6, starting transfers between devices, carried_in(): others.append(lax.ppermute(longer if first else sent, axis, pairs))  8.74 us
    ppermute x10, waiting for transfers between devices, rotate(): lax.ppermute(value, axis, [((i + steps) % count, i) for i in range(count)])  8.44 us
    pallas_call x1, Pallas kernels, in_vmem(): pl.pallas_call(functools.partial(load_weights, places), out_shape=pltpu.V...  5.31 us
    ppermute x6, waiting for transfers between devices, carried_in(): others.append(lax.ppermute(longer if first else sent, axis, pairs))  2.58 us
  transfers between devices with their start and end apart: 16, of which 5 were waited for; matrix products, arithmetic and copies ran while one was open for 1% of the time, Pallas kernels for 40%

profile of v4, /device:TPU:0, one launch (start us, length us, event | category | flops | bytes accessed | tf_op | source)
XLA Modules:
  0.0 75.2 jit_solution(5852971518545891502)
XLA Ops:
  0.0 0.1 pad_add_fusion.refs_0_
  0.1 1.2 %copy-done.2 = bf16[960,512]{1,0:T(8,128)(2,1)S(1)} copy-done((bf16[960,512]{1,0:T(8,128)(2,1)S(1)}, bf16[960,512]{1,0:T(8,128)(2,1)}, u32[]{:S(2)}) %copy-start.2) | copy-done | bytes 983064
  1.3 0.5 first_rows.1
  1.7 3.0 %collective-permute-start.5 = (bf16[128,960]{1,0:T(8,128)(2,1)S(1)}, bf16[128,960]{1,0:T(8,128)(2,1)S(1)}, u32[]{:S(2)}, u32[]{:S(2)}) collective-permute-start(bf16[128,960]{1,0:T(8,128)(2,1)S(1)} %get-tuple-element.93.refs_1_), channel_id=1, source_target_pairs={{1,0},{0,1},{3,2},{2,3},{5,4},{4,5},{7,6},{6,7},{9,8},{8,9},{11,10... | collective-permute-start | bytes 737288 | tf_op jit(solution)/shard_map/ppermute | solution.py:499
  4.8 1.0 %next_rows.1 = (bf16[128,960]{1,0:T(8,128)(2,1)S(1)}, bf16[128,960]{1,0:T(8,128)(2,1)S(1)}, bf16[128,960]{1,0:T(8,128)(2,1)S(1)}) custom-call(bf16[960,512]{1,0:T(8,128)(2,1)S(1)} %copy-done.2), custom_call_target="tpu_custom_call" | custom-call | flops 1 | bytes 1 | tf_op jit(solution)/shard_map/next_rows/pallas_call | solution.py:385
  5.8 0.1 collective-permute-start.4
  5.9 2.0 %collective-permute-start.3 = (bf16[128,960]{1,0:T(8,128)(2,1)S(1)}, bf16[128,960]{1,0:T(8,128)(2,1)S(1)}, u32[]{:S(2)}, u32[]{:S(2)}) collective-permute-start(bf16[128,960]{1,0:T(8,128)(2,1)S(1)} %get-tuple-element.95.refs_1_), channel_id=1, source_target_pairs={{1,0},{0,1},{3,2},{2,3},{5,4},{4,5},{7,6},{6,7},{9,8},{8,9},{11,10... | collective-permute-start | bytes 737288 | tf_op jit(solution)/shard_map/ppermute | solution.py:499
  7.9 0.1 collective-permute-start
  8.0 0.0 collective-permute-start.1
  8.0 0.9 %sqrt_multiply_fusion.refs_6_.refs_8_ = f32[16,960]{1,0:T(8,128)S(1)} fusion(f32[16,960]{1,0:T(8,128)} %param.13, f32[16,960]{1,0:T(8,128)} %refs_7_.7), kind=kLoop, calls=%fused_computation | loop fusion | flops 46080 | bytes 184320 | tf_op jit(solution)/shard_map/mul | solution.py:592
  8.9 0.0 copy-start.1
  8.9 0.0 copy-start.3
  8.9 5.3 %load_weights.1.refs_4_.refs_9_.refs_12_.refs_3_ = bf16[3,1920,960]{2,1,0:T(8,128)(2,1)S(1)} custom-call(bf16[3,960,1920]{2,1,0:T(8,128)(2,1)} %w_hbm), custom_call_target="tpu_custom_call" | custom-call | flops 1 | bytes 1 | tf_op jit(solution)/shard_map/load_weights/pallas_call | solution.py:406
  14.3 0.0 collective-permute-done.1.refs_3_
  14.3 2.0 %collective-permute-start.2 = (bf16[2,960]{1,0:T(2,128)(2,1)S(1)}, bf16[2,960]{1,0:T(2,128)(2,1)S(1)}, u32[]{:S(2)}, u32[]{:S(2)}) collective-permute-start(bf16[2,960]{1,0:T(2,128)(2,1)S(1)} %collective-permute-done.1.refs_3_), channel_id=1, source_target_pairs={{1,0},{0,1},{3,2},{2,3},{5,4},{4,5},{7,6},{6,7},{9,8},{8,9},{11,10... | collective-permute-start | bytes 11528 | tf_op jit(solution)/shard_map/ppermute | solution.py:499
  16.3 0.0 collective-permute-done.5.refs_2_
  16.3 3.5 %signal_stage.4 = (bf16[528,1920]{1,0:T(8,128)(2,1)S(1)}, f32[512,960]{1,0:T(8,128)S(1)}, f32[4,16,8,960]{3,2,1,0:T(8,128)S(1)}, f32[16,8,960]{2,1,0:T(8,128)S(1...) custom-call(s32[2]{0:T(128)S(1)} %pad_add_fusion.refs_0_, bf16[128,960]{1,0:T(8,128)(2,1)S(1)} %get-tuple-element.93.refs_1_, ...), custom_call_target="tpu_custom_call" | custom-call | flops 1 | bytes 1 | tf_op jit(solution)/shard_map/signal_stage/pallas_call | solution.py:385
  19.8 0.0 collective-permute-done.4.refs_2_
  19.9 3.4 %signal_stage.5 = (bf16[528,1920]{1,0:T(8,128)(2,1)S(1)}, f32[512,960]{1,0:T(8,128)S(1)}, f32[4,16,8,960]{3,2,1,0:T(8,128)S(1)}, f32[16,8,960]{2,1,0:T(8,128)S(1)}, f32[2,16,960]{2,1,0:T(8,128)S(1)}) custom-call(s32[2]{0:T(128)S(1)} %pad_add_fusion.refs_0_, ...), custom_call_target="tpu_custom_call", output_to_operand_aliasing={{0}: (3, {}), {1}: (4, {}), {2}: (5, {})} | custom-call | flops 1 | bytes 1 | tf_op jit(solution)/shard_map/signal_stage/pallas_call | solution.py:385
  23.3 3.4 %signal_stage.6 = (bf16[528,1920]{1,0:T(8,128)(2,1)S(1)}, f32[512,960]{1,0:T(8,128)S(1)}, f32[4,16,8,960]{3,2,1,0:T(8,128)S(1)}, f32[16,8,960]{2,1,0:T(8,128)S(1)}, f32[2,16,960]{2,1,0:T(8,128)S(1)}) custom-call(s32[2]{0:T(128)S(1)} %pad_add_fusion.refs_0_, ...), custom_call_target="tpu_custom_call", output_to_operand_aliasing={{0}: (3, {}), {1}: (4, {}), {2}: (5, {})} | custom-call | flops 1 | bytes 1 | tf_op jit(solution)/shard_map/signal_stage/pallas_call | solution.py:385
  26.7 1.3 %collective-permute-done.2.refs_4_ = bf16[2,960]{1,0:T(2,128)(2,1)S(1)} collective-permute-done((bf16[2,960]{1,0:T(2,128)(2,1)S(1)}, bf16[2,960]{1,0:T(2,128)(2,1)S(1)}, u32[]{:S(2)}, u32[]{:S(2)}) %collective-permute-start.2) | collective-permute-done | bytes 3872 | tf_op jit(solution)/shard_map/ppermute | solution.py:499
  28.0 4.4 %signal_stage.7 = (bf16[528,1920]{1,0:T(8,128)(2,1)S(1)}, f32[512,960]{1,0:T(8,128)S(1)}, f32[4,16,8,960]{3,2,1,0:T(8,128)S(1)}, f32[16,8,960]{2,1,0:T(8,128)S(1...) custom-call(s32[2]{0:T(128)S(1)} %pad_add_fusion.refs_0_, ...), custom_call_target="tpu_custom_call", output_to_operand_aliasing={{0}: (5, {}), {1}: (6, {}), {2}: (7, {})} | custom-call | flops 1 | bytes 1 | tf_op jit(solution)/shard_map/signal_stage/pallas_call | solution.py:385
  32.5 0.1 collective-permute-start.6
  32.5 1.7 %collective-permute-start.7 = (bf16[16,960]{1,0:T(8,128)(2,1)S(1)}, bf16[16,960]{1,0:T(8,128)(2,1)S(1)}, u32[]{:S(2)}, u32[]{:S(2)}) collective-permute-start(bf16[16,960]{1,0:T(8,128)(2,1)S(1)} %get-tuple-element.127), channel_id=1, source_target_pairs={{4,0},{6,2},{0,4},{2,6},{12,8},{14,10},{8,12},{10,14},{20,16},{22,... | collective-permute-start | bytes 92168 | tf_op jit(solution)/shard_map/ppermute | solution.py:550
  34.2 1.4 %collective-permute-start.8 = (bf16[16,960]{1,0:T(8,128)(2,1)S(1)}, bf16[16,960]{1,0:T(8,128)(2,1)S(1)}, u32[]{:S(2)}, u32[]{:S(2)}) collective-permute-start(bf16[16,960]{1,0:T(8,128)(2,1)S(1)} %get-tuple-element.127), channel_id=1, source_target_pairs={{2,0},{4,2},{6,4},{0,6},{10,8},{12,10},{14,12},{8,14},{18,16},{20,... | collective-permute-start | bytes 92168 | tf_op jit(solution)/shard_map/ppermute | solution.py:550
  35.6 1.7 %local_stage.4 = (f32[128,960]{1,0:T(8,128)S(1)}, f32[128,960]{1,0:T(8,128)S(1)}, f32[16,8,960]{2,1,0:T(8,128)S(1)}, f32[16,8,960]{2,1,0:T(8,128)S(1)}) custom-call(bf16[528,1920]{1,0:T(8,128)(2,1)S(1)} %get-tuple-element.154.refs_0_, f32[512,960]{1,0:T(8,128)S(1)} %get-tuple-element.155.refs_1_, f32[16,8,960]{2,1,0:T(8,128)S(1)} %get-tuple-element.128.refs_2_, ...), custom_call_target="tpu_custom_call" | custom-call | flops 1 | bytes 1 | tf_op jit(solution)/shard_map/local_stage/pallas_call | solution.py:385
  37.4 0.6 combine_states.2
  38.1 1.6 %collective-permute-start.9 = (bf16[24,960]{1,0:T(8,128)(2,1)S(1)}, bf16[24,960]{1,0:T(8,128)(2,1)S(1)}, u32[]{:S(2)}, u32[]{:S(2)}) collective-permute-start(bf16[24,960]{1,0:T(8,128)(2,1)S(1)} %get-tuple-element.139), channel_id=1, source_target_pairs={{24,0},{26,2},{28,4},{30,6},{0,8},{2,10},{4,12},{6,14},{8,16},{10,... | collective-permute-start | bytes 138248 | tf_op jit(solution)/shard_map/ppermute | solution.py:550
  39.7 2.6 %collective-permute-start.10 = (bf16[16,960]{1,0:T(8,128)(2,1)S(1)}, bf16[16,960]{1,0:T(8,128)(2,1)S(1)}, u32[]{:S(2)}, u32[]{:S(2)}) collective-permute-start(bf16[16,960]{1,0:T(8,128)(2,1)S(1)} %get-tuple-element.140), channel_id=1, source_target_pairs={{16,0},{18,2},{20,4},{22,6},{24,8},{26,10},{28,12},{30,14},{0,16},... | collective-permute-start | bytes 92168 | tf_op jit(solution)/shard_map/ppermute | solution.py:550
  42.3 1.3 %collective-permute-start.11 = (bf16[16,960]{1,0:T(8,128)(2,1)S(1)}, bf16[16,960]{1,0:T(8,128)(2,1)S(1)}, u32[]{:S(2)}, u32[]{:S(2)}) collective-permute-start(bf16[16,960]{1,0:T(8,128)(2,1)S(1)} %get-tuple-element.140), channel_id=1, source_target_pairs={{8,0},{10,2},{12,4},{14,6},{16,8},{18,10},{20,12},{22,14},{24,16},... | collective-permute-start | bytes 92168 | tf_op jit(solution)/shard_map/ppermute | solution.py:550
  43.6 1.9 %collective-permute-done.10.refs_4_ = bf16[16,960]{1,0:T(8,128)(2,1)S(1)} collective-permute-done((bf16[16,960]{1,0:T(8,128)(2,1)S(1)}, bf16[16,960]{1,0:T(8,128)(2,1)S(1)}, u32[]{:S(2)}, u32[]{:S(2)}) %collective-permute-start.10) | collective-permute-done | bytes 30752 | tf_op jit(solution)/shard_map/ppermute | solution.py:550
  45.6 0.6 collective-permute-done.11.refs_5_
  46.2 0.6 combine_states.3.refs_6_
  46.8 2.5 %second_stage.4 = (bf16[128,960]{1,0:T(8,128)(2,1)S(1)}, f32[128,960]{1,0:T(8,128)S(1)}) custom-call(s32[2]{0:T(128)S(1)} %pad_add_fusion.refs_0_, f32[128,960]{1,0:T(8,128)S(1)} %get-tuple-element.142.refs_1_, f32[128,960]{1,0:T(8,128)S(1)} %get-tuple-element.143.refs_2_, f32[16,8,960]{2,1,0:T(8,128)S(1)} %get-tuple-element.144.refs_3_, ...), custom_call_target="tpu_custom_call" | custom-call | flops 1 | bytes 1 | tf_op jit(solution)/shard_map/second_stage/pallas_call | solution.py:385
  49.3 1.6 %collective-permute-start.12 = (bf16[128,960]{1,0:T(8,128)(2,1)S(1)}, bf16[128,960]{1,0:T(8,128)(2,1)S(1)}, u32[]{:S(2)}, u32[]{:S(2)}) collective-permute-start(bf16[128,960]{1,0:T(8,128)(2,1)S(1)} %get-tuple-element.147), channel_id=1, source_target_pairs={{1,0},{0,1},{3,2},{2,3},{5,4},{4,5},{7,6},{6,7},{9,8},{8,9},{11,10... | collective-permute-start | bytes 737288 | tf_op jit(solution)/shard_map/ppermute | solution.py:499
  50.9 1.3 %local_stage.5 = (f32[128,960]{1,0:T(8,128)S(1)}, f32[128,960]{1,0:T(8,128)S(1)}) custom-call(bf16[528,1920]{1,0:T(8,128)(2,1)S(1)} %get-tuple-element.154.refs_0_, f32[512,960]{1,0:T(8,128)S(1)} %get-tuple-element.155.refs_1_, f32[16,8,960]{2,1,0:T(8,128)S(1)} %get-tuple-element.128.refs_2_, ...), custom_call_target="tpu_custom_call" | custom-call | flops 1 | bytes 1 | tf_op jit(solution)/shard_map/local_stage/pallas_call | solution.py:385
  52.2 2.4 %second_stage.5 = (bf16[128,960]{1,0:T(8,128)(2,1)S(1)}, f32[128,960]{1,0:T(8,128)S(1)}) custom-call(s32[2]{0:T(128)S(1)} %pad_add_fusion.refs_0_, f32[128,960]{1,0:T(8,128)S(1)} %get-tuple-element.151.refs_1_, f32[128,960]{1,0:T(8,128)S(1)} %get-tuple-element.152.refs_2_, f32[16,8,960]{2,1,0:T(8,128)S(1)} %get-tuple-element.144.refs_3_, ...), custom_call_target="tpu_custom_call" | custom-call | flops 1 | bytes 1 | tf_op jit(solution)/shard_map/second_stage/pallas_call | solution.py:385
  54.5 0.6 collective-permute-start.13
  55.1 2.7 %collective-permute-done.12.refs_3_ = bf16[128,960]{1,0:T(8,128)(2,1)S(1)} collective-permute-done((bf16[128,960]{1,0:T(8,128)(2,1)S(1)}, bf16[128,960]{1,0:T(8,128)(2,1)S(1)}, u32[]{:S(2)}, u32[]{:S(2)}) %collective-permute-start.12) | collective-permute-done | bytes 245792 | tf_op jit(solution)/shard_map/ppermute | solution.py:499
  57.8 1.3 %local_stage.7 = (f32[128,960]{1,0:T(8,128)S(1)}, f32[128,960]{1,0:T(8,128)S(1)}) custom-call(bf16[528,1920]{1,0:T(8,128)(2,1)S(1)} %get-tuple-element.154.refs_0_, f32[512,960]{1,0:T(8,128)S(1)} %get-tuple-element.155.refs_1_, f32[16,8,960]{2,1,0:T(8,128)S(1)} %get-tuple-element.128.refs_2_, ...), custom_call_target="tpu_custom_call" | custom-call | flops 1 | bytes 1 | tf_op jit(solution)/shard_map/local_stage/pallas_call | solution.py:385
  59.1 2.4 %second_stage.7 = (bf16[128,960]{1,0:T(8,128)(2,1)S(1)}, f32[128,960]{1,0:T(8,128)S(1)}) custom-call(s32[2]{0:T(128)S(1)} %pad_add_fusion.refs_0_, f32[128,960]{1,0:T(8,128)S(1)} %get-tuple-element.163.refs_1_, f32[128,960]{1,0:T(8,128)S(1)} %get-tuple-element.164.refs_2_, f32[16,8,960]{2,1,0:T(8,128)S(1)} %get-tuple-element.144.refs_3_, ...), custom_call_target="tpu_custom_call" | custom-call | flops 1 | bytes 1 | tf_op jit(solution)/shard_map/second_stage/pallas_call | solution.py:385
  61.5 1.9 %collective-permute-start.15 = (bf16[128,960]{1,0:T(8,128)(2,1)S(1)}, bf16[128,960]{1,0:T(8,128)(2,1)S(1)}, u32[]{:S(2)}, u32[]{:S(2)}) collective-permute-start(bf16[128,960]{1,0:T(8,128)(2,1)S(1)} %get-tuple-element.168), channel_id=1, source_target_pairs={{1,0},{0,1},{3,2},{2,3},{5,4},{4,5},{7,6},{6,7},{9,8},{8,9},{11,10... | collective-permute-start | bytes 737288 | tf_op jit(solution)/shard_map/ppermute | solution.py:499
  63.4 1.3 %local_stage.6 = (f32[128,960]{1,0:T(8,128)S(1)}, f32[128,960]{1,0:T(8,128)S(1)}) custom-call(bf16[528,1920]{1,0:T(8,128)(2,1)S(1)} %get-tuple-element.154.refs_0_, f32[512,960]{1,0:T(8,128)S(1)} %get-tuple-element.155.refs_1_, f32[16,8,960]{2,1,0:T(8,128)S(1)} %get-tuple-element.128.refs_2_, ...), custom_call_target="tpu_custom_call" | custom-call | flops 1 | bytes 1 | tf_op jit(solution)/shard_map/local_stage/pallas_call | solution.py:385
  64.7 2.4 %second_stage.6 = (bf16[128,960]{1,0:T(8,128)(2,1)S(1)}, f32[128,960]{1,0:T(8,128)S(1)}) custom-call(s32[2]{0:T(128)S(1)} %pad_add_fusion.refs_0_, f32[128,960]{1,0:T(8,128)S(1)} %get-tuple-element.156.refs_1_, f32[128,960]{1,0:T(8,128)S(1)} %get-tuple-element.157.refs_2_, f32[16,8,960]{2,1,0:T(8,128)S(1)} %get-tuple-element.144.refs_3_, ...), custom_call_target="tpu_custom_call" | custom-call | flops 1 | bytes 1 | tf_op jit(solution)/shard_map/second_stage/pallas_call | solution.py:385
  67.1 1.5 %collective-permute-start.14 = (bf16[128,960]{1,0:T(8,128)(2,1)S(1)}, bf16[128,960]{1,0:T(8,128)(2,1)S(1)}, u32[]{:S(2)}, u32[]{:S(2)}) collective-permute-start(bf16[128,960]{1,0:T(8,128)(2,1)S(1)} %get-tuple-element.160), channel_id=1, source_target_pairs={{1,0},{0,1},{3,2},{2,3},{5,4},{4,5},{7,6},{6,7},{9,8},{8,9},{11,10... | collective-permute-start | bytes 737288 | tf_op jit(solution)/shard_map/ppermute | solution.py:499
  68.6 0.8 %last_stage.2.refs_2_ = bf16[960,512]{1,0:T(8,128)(2,1)S(1)} custom-call(f32[128,960]{1,0:T(8,128)S(1)} %get-tuple-element.161.refs_0_, f32[128,960]{1,0:T(8,128)S(1)} %get-tuple-element.162.refs_1_, f32[128,960]{1,0:T(8,128)S(1)} %get-tuple-element.165.refs_2_, bf16[128,960]{1,0:T(8,128)(2,1)S(1)} %collective-permute-done.12.refs_3_, ...), custom_call_target="tpu_custom_call" | custom-call | flops 1 | bytes 1 | tf_op jit(solution)/shard_map/last_stage/pallas_call | solution.py:385
  69.4 4.5 %collective-permute-done.14.refs_1_ = bf16[128,960]{1,0:T(8,128)(2,1)S(1)} collective-permute-done((bf16[128,960]{1,0:T(8,128)(2,1)S(1)}, bf16[128,960]{1,0:T(8,128)(2,1)S(1)}, u32[]{:S(2)}, u32[]{:S(2)}) %collective-permute-start.14) | collective-permute-done | bytes 245792 | tf_op jit(solution)/shard_map/ppermute | solution.py:499
  73.8 1.2 %last_stage.3 = bf16[960,512]{1,0:T(8,128)(2,1)} custom-call(f32[128,960]{1,0:T(8,128)S(1)} %get-tuple-element.159.refs_0_, bf16[128,960]{1,0:T(8,128)(2,1)S(1)} %collective-permute-done.14.refs_1_, bf16[960,512]{1,0:T(8,128)(2,1)S(1)} %last_stage.2.refs_2_), custom_call_target="tpu_custom_call" | custom-call | flops 1 | bytes 1 | tf_op jit(solution)/shard_map/last_stage/pallas_call | solution.py:385
  (18 shorter events, 0.0 us)
Async XLA Ops:
  0.0 8.9 %copy-start.5 = (f32[1920]{0:T(1024)S(1)}, f32[1920]{0:T(1024)}, u32[]{:S(2)}) copy-start(f32[1920]{0:T(1024)} %param.9) | copy-start | bytes 23044
  0.1 1.2 %copy-start.2 = (bf16[960,512]{1,0:T(8,128)(2,1)S(1)}, bf16[960,512]{1,0:T(8,128)(2,1)}, u32[]{:S(2)}) copy-start(bf16[960,512]{1,0:T(8,128)(2,1)} %tokens_ref.1) | copy-start | bytes 2949124
  1.7 14.5 %collective-permute-start.5 = (bf16[128,960]{1,0:T(8,128)(2,1)S(1)}, bf16[128,960]{1,0:T(8,128)(2,1)S(1)}, u32[]{:S(2)}, u32[]{:S(2)}) collective-permute-start(bf16[128,960]{1,0:T(8,128)(2,1)S(1)} %get-tuple-element.93.refs_1_), channel_id=1, source_target_pairs={{1,0},{0,1},{3,2},{2,3},{5,4},{4,5},{7,6},{6,7},{9,8},{8,9},{11,10... | collective-permute-start | bytes 737288 | tf_op jit(solution)/shard_map/ppermute | solution.py:499
  5.8 14.0 %collective-permute-start.4 = (bf16[128,960]{1,0:T(8,128)(2,1)S(1)}, bf16[128,960]{1,0:T(8,128)(2,1)S(1)}, u32[]{:S(2)}, u32[]{:S(2)}) collective-permute-start(bf16[128,960]{1,0:T(8,128)(2,1)S(1)} %get-tuple-element.94.refs_1_), channel_id=1, source_target_pairs={{1,0},{0,1},{3,2},{2,3},{5,4},{4,5},{7,6},{6,7},{9,8},{8,9},{11,10... | collective-permute-start | bytes 737288 | tf_op jit(solution)/shard_map/ppermute | solution.py:499
  5.9 17.4 %collective-permute-start.3 = (bf16[128,960]{1,0:T(8,128)(2,1)S(1)}, bf16[128,960]{1,0:T(8,128)(2,1)S(1)}, u32[]{:S(2)}, u32[]{:S(2)}) collective-permute-start(bf16[128,960]{1,0:T(8,128)(2,1)S(1)} %get-tuple-element.95.refs_1_), channel_id=1, source_target_pairs={{1,0},{0,1},{3,2},{2,3},{5,4},{4,5},{7,6},{6,7},{9,8},{8,9},{11,10... | collective-permute-start | bytes 737288 | tf_op jit(solution)/shard_map/ppermute | solution.py:499
  7.9 20.1 %collective-permute-start = (bf16[128,960]{1,0:T(8,128)(2,1)S(1)}, bf16[128,960]{1,0:T(8,128)(2,1)S(1)}, u32[]{:S(2)}, u32[]{:S(2)}) collective-permute-start(bf16[128,960]{1,0:T(8,128)(2,1)S(1)} %get-tuple-element.91.refs_1_), channel_id=1, source_target_pairs={{1,0},{0,1},{3,2},{2,3},{5,4},{4,5},{7,6},{6,7},{9,8},{8,9},{11,10... | collective-permute-start | bytes 737288 | tf_op jit(solution)/shard_map/ppermute | solution.py:499
  8.0 6.3 %collective-permute-start.1 = (bf16[2,960]{1,0:T(2,128)(2,1)S(1)}, bf16[2,960]{1,0:T(2,128)(2,1)S(1)}, u32[]{:S(2)}, u32[]{:S(2)}) collective-permute-start(bf16[2,960]{1,0:T(2,128)(2,1)S(1)} %get-tuple-element.92), channel_id=1, source_target_pairs={{30,0},{0,2},{2,4},{4,6},{6,8},{8,10},{10,12},{12,14},{14,16},{16,... | collective-permute-start | bytes 11528 | tf_op jit(solution)/shard_map/ppermute | solution.py:499
  8.9 7.4 %copy-start.1 = (f32[16,960]{1,0:T(8,128)S(1)}, f32[16,960]{1,0:T(8,128)}, u32[]{:S(2)}) copy-start(f32[16,960]{1,0:T(8,128)} %refs_7_.7) | copy-start | bytes 184324
  8.9 7.4 %copy-start.3 = (f32[3,3,960]{2,1,0:T(4,128)S(1)}, f32[3,3,960]{2,1,0:T(4,128)}, u32[]{:S(2)}) copy-start(f32[3,3,960]{2,1,0:T(4,128)} %refs_4_.7) | copy-start | bytes 103684
  14.3 13.7 %collective-permute-start.2 = (bf16[2,960]{1,0:T(2,128)(2,1)S(1)}, bf16[2,960]{1,0:T(2,128)(2,1)S(1)}, u32[]{:S(2)}, u32[]{:S(2)}) collective-permute-start(bf16[2,960]{1,0:T(2,128)(2,1)S(1)} %collective-permute-done.1.refs_3_), channel_id=1, source_target_pairs={{1,0},{0,1},{3,2},{2,3},{5,4},{4,5},{7,6},{6,7},{9,8},{8,9},{11,10... | collective-permute-start | bytes 11528 | tf_op jit(solution)/shard_map/ppermute | solution.py:499
  28.0 7.6 %copy-start.4 = (f32[960]{0:T(1024)S(1)}, f32[960]{0:T(1024)}, u32[]{:S(2)}) copy-start(f32[960]{0:T(1024)} %param.14) | copy-start | bytes 11524
  32.5 4.9 %collective-permute-start.6 = (bf16[16,960]{1,0:T(8,128)(2,1)S(1)}, bf16[16,960]{1,0:T(8,128)(2,1)S(1)}, u32[]{:S(2)}, u32[]{:S(2)}) collective-permute-start(bf16[16,960]{1,0:T(8,128)(2,1)S(1)} %get-tuple-element.127), channel_id=1, source_target_pairs={{6,0},{0,2},{2,4},{4,6},{14,8},{8,10},{10,12},{12,14},{22,16},{16,... | collective-permute-start | bytes 92168 | tf_op jit(solution)/shard_map/ppermute | solution.py:550
  32.5 4.9 %collective-permute-start.7 = (bf16[16,960]{1,0:T(8,128)(2,1)S(1)}, bf16[16,960]{1,0:T(8,128)(2,1)S(1)}, u32[]{:S(2)}, u32[]{:S(2)}) collective-permute-start(bf16[16,960]{1,0:T(8,128)(2,1)S(1)} %get-tuple-element.127), channel_id=1, source_target_pairs={{4,0},{6,2},{0,4},{2,6},{12,8},{14,10},{8,12},{10,14},{20,16},{22,... | collective-permute-start | bytes 92168 | tf_op jit(solution)/shard_map/ppermute | solution.py:550
  34.2 3.2 %collective-permute-start.8 = (bf16[16,960]{1,0:T(8,128)(2,1)S(1)}, bf16[16,960]{1,0:T(8,128)(2,1)S(1)}, u32[]{:S(2)}, u32[]{:S(2)}) collective-permute-start(bf16[16,960]{1,0:T(8,128)(2,1)S(1)} %get-tuple-element.127), channel_id=1, source_target_pairs={{2,0},{4,2},{6,4},{0,6},{10,8},{12,10},{14,12},{8,14},{18,16},{20,... | collective-permute-start | bytes 92168 | tf_op jit(solution)/shard_map/ppermute | solution.py:550
  35.6 11.2 %copy-start = (bf16[960,1920]{1,0:T(8,128)(2,1)S(1)}, bf16[960,1920]{1,0:T(8,128)(2,1)}, u32[]{:S(2)}) copy-start(bf16[960,1920]{1,0:T(8,128)(2,1)} %refs_9_.7) | copy-start | bytes 11059204
  38.1 8.1 %collective-permute-start.9 = (bf16[24,960]{1,0:T(8,128)(2,1)S(1)}, bf16[24,960]{1,0:T(8,128)(2,1)S(1)}, u32[]{:S(2)}, u32[]{:S(2)}) collective-permute-start(bf16[24,960]{1,0:T(8,128)(2,1)S(1)} %get-tuple-element.139), channel_id=1, source_target_pairs={{24,0},{26,2},{28,4},{30,6},{0,8},{2,10},{4,12},{6,14},{8,16},{10,... | collective-permute-start | bytes 138248 | tf_op jit(solution)/shard_map/ppermute | solution.py:550
  39.7 5.9 %collective-permute-start.10 = (bf16[16,960]{1,0:T(8,128)(2,1)S(1)}, bf16[16,960]{1,0:T(8,128)(2,1)S(1)}, u32[]{:S(2)}, u32[]{:S(2)}) collective-permute-start(bf16[16,960]{1,0:T(8,128)(2,1)S(1)} %get-tuple-element.140), channel_id=1, source_target_pairs={{16,0},{18,2},{20,4},{22,6},{24,8},{26,10},{28,12},{30,14},{0,16},... | collective-permute-start | bytes 92168 | tf_op jit(solution)/shard_map/ppermute | solution.py:550
  42.3 3.9 %collective-permute-start.11 = (bf16[16,960]{1,0:T(8,128)(2,1)S(1)}, bf16[16,960]{1,0:T(8,128)(2,1)S(1)}, u32[]{:S(2)}, u32[]{:S(2)}) collective-permute-start(bf16[16,960]{1,0:T(8,128)(2,1)S(1)} %get-tuple-element.140), channel_id=1, source_target_pairs={{8,0},{10,2},{12,4},{14,6},{16,8},{18,10},{20,12},{22,14},{24,16},... | collective-permute-start | bytes 92168 | tf_op jit(solution)/shard_map/ppermute | solution.py:550
  49.3 8.5 %collective-permute-start.12 = (bf16[128,960]{1,0:T(8,128)(2,1)S(1)}, bf16[128,960]{1,0:T(8,128)(2,1)S(1)}, u32[]{:S(2)}, u32[]{:S(2)}) collective-permute-start(bf16[128,960]{1,0:T(8,128)(2,1)S(1)} %get-tuple-element.147), channel_id=1, source_target_pairs={{1,0},{0,1},{3,2},{2,3},{5,4},{4,5},{7,6},{6,7},{9,8},{8,9},{11,10... | collective-permute-start | bytes 737288 | tf_op jit(solution)/shard_map/ppermute | solution.py:499
  54.5 8.8 %collective-permute-start.13 = (bf16[128,960]{1,0:T(8,128)(2,1)S(1)}, bf16[128,960]{1,0:T(8,128)(2,1)S(1)}, u32[]{:S(2)}, u32[]{:S(2)}) collective-permute-start(bf16[128,960]{1,0:T(8,128)(2,1)S(1)} %get-tuple-element.153), channel_id=1, source_target_pairs={{1,0},{0,1},{3,2},{2,3},{5,4},{4,5},{7,6},{6,7},{9,8},{8,9},{11,10... | collective-permute-start | bytes 737288 | tf_op jit(solution)/shard_map/ppermute | solution.py:499
  61.5 7.1 %collective-permute-start.15 = (bf16[128,960]{1,0:T(8,128)(2,1)S(1)}, bf16[128,960]{1,0:T(8,128)(2,1)S(1)}, u32[]{:S(2)}, u32[]{:S(2)}) collective-permute-start(bf16[128,960]{1,0:T(8,128)(2,1)S(1)} %get-tuple-element.168), channel_id=1, source_target_pairs={{1,0},{0,1},{3,2},{2,3},{5,4},{4,5},{7,6},{6,7},{9,8},{8,9},{11,10... | collective-permute-start | bytes 737288 | tf_op jit(solution)/shard_map/ppermute | solution.py:499
  67.1 6.7 %collective-permute-start.14 = (bf16[128,960]{1,0:T(8,128)(2,1)S(1)}, bf16[128,960]{1,0:T(8,128)(2,1)S(1)}, u32[]{:S(2)}, u32[]{:S(2)}) collective-permute-start(bf16[128,960]{1,0:T(8,128)(2,1)S(1)} %get-tuple-element.160), channel_id=1, source_target_pairs={{1,0},{0,1},{3,2},{2,3},{5,4},{4,5},{7,6},{6,7},{9,8},{8,9},{11,10... | collective-permute-start | bytes 737288 | tf_op jit(solution)/shard_map/ppermute | solution.py:499

commit v5 on v4

--- a/solution.py
+++ b/solution.py
@@ -207,8 +207,7 @@
 
             steps = rows // ROWS
             skipped = taps - 1 if start else 0
-            unroll = next(k for k in (8, 7, 4, 2, 1) if (steps - skipped) % k == 0)
-            states = lax.fori_loop(skipped, steps, step, states, unroll=unroll)
+            states = lax.fori_loop(skipped, steps, step, states, unroll=steps - skipped)
             if last:
                 for n in range(modes):
                     marks_ref[1, n, :, lanes] = states[n]
@@ -328,7 +327,7 @@
                 )
                 return states
 
-            lax.fori_loop(0, SPAN, step, tuple(states), unroll=4)
+            lax.fori_loop(0, SPAN, step, tuple(states), unroll=SPAN)
     product = jnp.dot(gated_ref[...].astype(BF16), w_ref[...], preferred_element_type=F32)
     share = own_ref.shape[1]
     me = me_ref[0]

time: 75.4 us -> 74.6 us (0.989)
  Pallas kernels: 40.1 us -> 37.3 us
  waiting for transfers between devices: 11 us -> 12.6 us
    pallas_call x18, Pallas kernels: 34.8 us -> 32 us  [call(): pl.pallas_call(kernel, out_shape=outs, in_specs=[smem] * len(scalars) + [...]
    ppermute x10, waiting for transfers between devices: 8.44 us -> 9.98 us  [rotate(): lax.ppermute(value, axis, [((i + steps) % count, i) for i in range(count)])]
  transfers between devices with their start and end apart: 16 -> 16, of which waited for: 5 -> 7; matrix products, arithmetic and copies ran while one was open for 1% -> 1% of each run, Pallas kernels for 40% -> 38%
where the time goes in v5:
time: 74.6 us; the launch traced here: 74.4 us
  Pallas kernels  37.3 us (50%)
  starting transfers between devices  22 us (29%)
  waiting for transfers between devices  12.6 us (17%)
  local copies, waits for them, and re-layouts  1.23 us (2%)
  other arithmetic  0.99 us (1%)
    pallas_call x18, Pallas kernels, call(): pl.pallas_call(kernel, out_shape=outs, in_specs=[smem] * len(scalars) + [...  32 us
    ppermute x10, starting transfers between devices, rotate(): lax.ppermute(value, axis, [((i + steps) % count, i) for i in range(count)])  13.2 us
    ppermute x10, waiting for transfers between devices, rotate(): lax.ppermute(value, axis, [((i + steps) % count, i) for i in range(count)])  9.98 us
    ppermute x6, starting transfers between devices, carried_in(): others.append(lax.ppermute(longer if first else sent, axis, pairs))  8.75 us
    pallas_call x1, Pallas kernels, in_vmem(): pl.pallas_call(functools.partial(load_weights, places), out_shape=pltpu.V...  5.31 us
    ppermute x6, waiting for transfers between devices, carried_in(): others.append(lax.ppermute(longer if first else sent, axis, pairs))  2.57 us
  transfers between devices with their start and end apart: 16, of which 7 were waited for; matrix products, arithmetic and copies ran while one was open for 1% of the time, Pallas kernels for 38%

profile of v5, /device:TPU:0, one launch (start us, length us, event | category | flops | bytes accessed | tf_op | source)
XLA Modules:
  0.0 74.4 jit_solution(7707178578466931307)
XLA Ops:
  0.0 0.1 pad_add_fusion.refs_0_
  0.1 1.2 %copy-done.2 = bf16[960,512]{1,0:T(8,128)(2,1)S(1)} copy-done((bf16[960,512]{1,0:T(8,128)(2,1)S(1)}, bf16[960,512]{1,0:T(8,128)(2,1)}, u32[]{:S(2)}) %copy-start.2) | copy-done | bytes 983064
  1.3 0.5 first_rows.1
  1.7 3.0 %collective-permute-start.5 = (bf16[128,960]{1,0:T(8,128)(2,1)S(1)}, bf16[128,960]{1,0:T(8,128)(2,1)S(1)}, u32[]{:S(2)}, u32[]{:S(2)}) collective-permute-start(bf16[128,960]{1,0:T(8,128)(2,1)S(1)} %get-tuple-element.93.refs_1_), channel_id=1, source_target_pairs={{1,0},{0,1},{3,2},{2,3},{5,4},{4,5},{7,6},{6,7},{9,8},{8,9},{11,10... | collective-permute-start | bytes 737288 | tf_op jit(solution)/shard_map/ppermute | solution.py:498
  4.8 1.0 %next_rows.1 = (bf16[128,960]{1,0:T(8,128)(2,1)S(1)}, bf16[128,960]{1,0:T(8,128)(2,1)S(1)}, bf16[128,960]{1,0:T(8,128)(2,1)S(1)}) custom-call(bf16[960,512]{1,0:T(8,128)(2,1)S(1)} %copy-done.2), custom_call_target="tpu_custom_call" | custom-call | flops 1 | bytes 1 | tf_op jit(solution)/shard_map/next_rows/pallas_call | solution.py:384
  5.8 0.1 collective-permute-start.4
  5.9 2.0 %collective-permute-start.3 = (bf16[128,960]{1,0:T(8,128)(2,1)S(1)}, bf16[128,960]{1,0:T(8,128)(2,1)S(1)}, u32[]{:S(2)}, u32[]{:S(2)}) collective-permute-start(bf16[128,960]{1,0:T(8,128)(2,1)S(1)} %get-tuple-element.95.refs_1_), channel_id=1, source_target_pairs={{1,0},{0,1},{3,2},{2,3},{5,4},{4,5},{7,6},{6,7},{9,8},{8,9},{11,10... | collective-permute-start | bytes 737288 | tf_op jit(solution)/shard_map/ppermute | solution.py:498
  7.9 0.1 collective-permute-start
  8.0 0.9 %sqrt_multiply_fusion.refs_6_.refs_8_ = f32[16,960]{1,0:T(8,128)S(1)} fusion(f32[16,960]{1,0:T(8,128)} %param.13, f32[16,960]{1,0:T(8,128)} %refs_7_.7), kind=kLoop, calls=%fused_computation | loop fusion | flops 46080 | bytes 184320 | tf_op jit(solution)/shard_map/mul | solution.py:591
  8.9 0.0 copy-start.1
  8.9 0.0 copy-start.3
  8.9 5.3 %load_weights.1.refs_4_.refs_9_.refs_12_.refs_3_ = bf16[3,1920,960]{2,1,0:T(8,128)(2,1)S(1)} custom-call(bf16[3,960,1920]{2,1,0:T(8,128)(2,1)} %w_hbm), custom_call_target="tpu_custom_call" | custom-call | flops 1 | bytes 1 | tf_op jit(solution)/shard_map/load_weights/pallas_call | solution.py:405
  14.3 0.0 collective-permute-done.1.refs_3_
  14.3 2.0 %collective-permute-start.2 = (bf16[2,960]{1,0:T(2,128)(2,1)S(1)}, bf16[2,960]{1,0:T(2,128)(2,1)S(1)}, u32[]{:S(2)}, u32[]{:S(2)}) collective-permute-start(bf16[2,960]{1,0:T(2,128)(2,1)S(1)} %collective-permute-done.1.refs_3_), channel_id=1, source_target_pairs={{1,0},{0,1},{3,2},{2,3},{5,4},{4,5},{7,6},{6,7},{9,8},{8,9},{11,10... | collective-permute-start | bytes 11528 | tf_op jit(solution)/shard_map/ppermute | solution.py:498
  16.3 2.8 %signal_stage.4 = (bf16[528,1920]{1,0:T(8,128)(2,1)S(1)}, f32[512,960]{1,0:T(8,128)S(1)}, f32[4,16,8,960]{3,2,1,0:T(8,128)S(1)}, f32[16,8,960]{2,1,0:T(8,128)S(1...) custom-call(s32[2]{0:T(128)S(1)} %pad_add_fusion.refs_0_, bf16[128,960]{1,0:T(8,128)(2,1)S(1)} %get-tuple-element.93.refs_1_, ...), custom_call_target="tpu_custom_call" | custom-call | flops 1 | bytes 1 | tf_op jit(solution)/shard_map/signal_stage/pallas_call | solution.py:384
  19.1 3.0 %signal_stage.5 = (bf16[528,1920]{1,0:T(8,128)(2,1)S(1)}, f32[512,960]{1,0:T(8,128)S(1)}, f32[4,16,8,960]{3,2,1,0:T(8,128)S(1)}, f32[16,8,960]{2,1,0:T(8,128)S(1)}, f32[2,16,960]{2,1,0:T(8,128)S(1)}) custom-call(s32[2]{0:T(128)S(1)} %pad_add_fusion.refs_0_, ...), custom_call_target="tpu_custom_call", output_to_operand_aliasing={{0}: (3, {}), {1}: (4, {}), {2}: (5, {})} | custom-call | flops 1 | bytes 1 | tf_op jit(solution)/shard_map/signal_stage/pallas_call | solution.py:384
  22.1 1.0 %collective-permute-done.3.refs_2_ = bf16[128,960]{1,0:T(8,128)(2,1)S(1)} collective-permute-done((bf16[128,960]{1,0:T(8,128)(2,1)S(1)}, bf16[128,960]{1,0:T(8,128)(2,1)S(1)}, u32[]{:S(2)}, u32[]{:S(2)}) %collective-permute-start.3) | collective-permute-done | bytes 245792 | tf_op jit(solution)/shard_map/ppermute | solution.py:498
  23.1 3.0 %signal_stage.6 = (bf16[528,1920]{1,0:T(8,128)(2,1)S(1)}, f32[512,960]{1,0:T(8,128)S(1)}, f32[4,16,8,960]{3,2,1,0:T(8,128)S(1)}, f32[16,8,960]{2,1,0:T(8,128)S(1)}, f32[2,16,960]{2,1,0:T(8,128)S(1)}) custom-call(s32[2]{0:T(128)S(1)} %pad_add_fusion.refs_0_, ...), custom_call_target="tpu_custom_call", output_to_operand_aliasing={{0}: (3, {}), {1}: (4, {}), {2}: (5, {})} | custom-call | flops 1 | bytes 1 | tf_op jit(solution)/shard_map/signal_stage/pallas_call | solution.py:384
  26.1 1.9 %collective-permute-done.2.refs_4_ = bf16[2,960]{1,0:T(2,128)(2,1)S(1)} collective-permute-done((bf16[2,960]{1,0:T(2,128)(2,1)S(1)}, bf16[2,960]{1,0:T(2,128)(2,1)S(1)}, u32[]{:S(2)}, u32[]{:S(2)}) %collective-permute-start.2) | collective-permute-done | bytes 3872 | tf_op jit(solution)/shard_map/ppermute | solution.py:498
  28.0 4.2 %signal_stage.7 = (bf16[528,1920]{1,0:T(8,128)(2,1)S(1)}, f32[512,960]{1,0:T(8,128)S(1)}, f32[4,16,8,960]{3,2,1,0:T(8,128)S(1)}, f32[16,8,960]{2,1,0:T(8,128)S(1...) custom-call(s32[2]{0:T(128)S(1)} %pad_add_fusion.refs_0_, ...), custom_call_target="tpu_custom_call", output_to_operand_aliasing={{0}: (5, {}), {1}: (6, {}), {2}: (7, {})} | custom-call | flops 1 | bytes 1 | tf_op jit(solution)/shard_map/signal_stage/pallas_call | solution.py:384
  32.2 1.8 %collective-permute-start.7 = (bf16[16,960]{1,0:T(8,128)(2,1)S(1)}, bf16[16,960]{1,0:T(8,128)(2,1)S(1)}, u32[]{:S(2)}, u32[]{:S(2)}) collective-permute-start(bf16[16,960]{1,0:T(8,128)(2,1)S(1)} %get-tuple-element.127), channel_id=1, source_target_pairs={{4,0},{6,2},{0,4},{2,6},{12,8},{14,10},{8,12},{10,14},{20,16},{22,... | collective-permute-start | bytes 92168 | tf_op jit(solution)/shard_map/ppermute | solution.py:549
  34.0 1.4 %collective-permute-start.8 = (bf16[16,960]{1,0:T(8,128)(2,1)S(1)}, bf16[16,960]{1,0:T(8,128)(2,1)S(1)}, u32[]{:S(2)}, u32[]{:S(2)}) collective-permute-start(bf16[16,960]{1,0:T(8,128)(2,1)S(1)} %get-tuple-element.127), channel_id=1, source_target_pairs={{2,0},{4,2},{6,4},{0,6},{10,8},{12,10},{14,12},{8,14},{18,16},{20,... | collective-permute-start | bytes 92168 | tf_op jit(solution)/shard_map/ppermute | solution.py:549
  35.4 1.7 %local_stage.4 = (f32[128,960]{1,0:T(8,128)S(1)}, f32[128,960]{1,0:T(8,128)S(1)}, f32[16,8,960]{2,1,0:T(8,128)S(1)}, f32[16,8,960]{2,1,0:T(8,128)S(1)}) custom-call(bf16[528,1920]{1,0:T(8,128)(2,1)S(1)} %get-tuple-element.154.refs_0_, f32[512,960]{1,0:T(8,128)S(1)} %get-tuple-element.155.refs_1_, f32[16,8,960]{2,1,0:T(8,128)S(1)} %get-tuple-element.128.refs_2_, ...), custom_call_target="tpu_custom_call" | custom-call | flops 1 | bytes 1 | tf_op jit(solution)/shard_map/local_stage/pallas_call | solution.py:384
  37.2 0.0 collective-permute-done.6.refs_3_
  37.2 0.0 collective-permute-done.8.refs_5_
  37.2 0.6 combine_states.2
  37.8 1.6 %collective-permute-start.9 = (bf16[24,960]{1,0:T(8,128)(2,1)S(1)}, bf16[24,960]{1,0:T(8,128)(2,1)S(1)}, u32[]{:S(2)}, u32[]{:S(2)}) collective-permute-start(bf16[24,960]{1,0:T(8,128)(2,1)S(1)} %get-tuple-element.139), channel_id=1, source_target_pairs={{24,0},{26,2},{28,4},{30,6},{0,8},{2,10},{4,12},{6,14},{8,16},{10,... | collective-permute-start | bytes 138248 | tf_op jit(solution)/shard_map/ppermute | solution.py:549
  39.5 2.6 %collective-permute-start.10 = (bf16[16,960]{1,0:T(8,128)(2,1)S(1)}, bf16[16,960]{1,0:T(8,128)(2,1)S(1)}, u32[]{:S(2)}, u32[]{:S(2)}) collective-permute-start(bf16[16,960]{1,0:T(8,128)(2,1)S(1)} %get-tuple-element.140), channel_id=1, source_target_pairs={{16,0},{18,2},{20,4},{22,6},{24,8},{26,10},{28,12},{30,14},{0,16},... | collective-permute-start | bytes 92168 | tf_op jit(solution)/shard_map/ppermute | solution.py:549
  42.0 1.3 %collective-permute-start.11 = (bf16[16,960]{1,0:T(8,128)(2,1)S(1)}, bf16[16,960]{1,0:T(8,128)(2,1)S(1)}, u32[]{:S(2)}, u32[]{:S(2)}) collective-permute-start(bf16[16,960]{1,0:T(8,128)(2,1)S(1)} %get-tuple-element.140), channel_id=1, source_target_pairs={{8,0},{10,2},{12,4},{14,6},{16,8},{18,10},{20,12},{22,14},{24,16},... | collective-permute-start | bytes 92168 | tf_op jit(solution)/shard_map/ppermute | solution.py:549
  43.4 1.6 %collective-permute-done.10.refs_4_ = bf16[16,960]{1,0:T(8,128)(2,1)S(1)} collective-permute-done((bf16[16,960]{1,0:T(8,128)(2,1)S(1)}, bf16[16,960]{1,0:T(8,128)(2,1)S(1)}, u32[]{:S(2)}, u32[]{:S(2)}) %collective-permute-start.10) | collective-permute-done | bytes 30752 | tf_op jit(solution)/shard_map/ppermute | solution.py:549
  45.0 1.0 %collective-permute-done.11.refs_5_ = bf16[16,960]{1,0:T(8,128)(2,1)S(1)} collective-permute-done((bf16[16,960]{1,0:T(8,128)(2,1)S(1)}, bf16[16,960]{1,0:T(8,128)(2,1)S(1)}, u32[]{:S(2)}, u32[]{:S(2)}) %collective-permute-start.11) | collective-permute-done | bytes 30752 | tf_op jit(solution)/shard_map/ppermute | solution.py:549
  46.0 0.6 combine_states.3.refs_6_
  46.6 2.0 %second_stage.4 = (bf16[128,960]{1,0:T(8,128)(2,1)S(1)}, f32[128,960]{1,0:T(8,128)S(1)}) custom-call(s32[2]{0:T(128)S(1)} %pad_add_fusion.refs_0_, f32[128,960]{1,0:T(8,128)S(1)} %get-tuple-element.142.refs_1_, f32[128,960]{1,0:T(8,128)S(1)} %get-tuple-element.143.refs_2_, f32[16,8,960]{2,1,0:T(8,128)S(1)} %get-tuple-element.144.refs_3_, ...), custom_call_target="tpu_custom_call" | custom-call | flops 1 | bytes 1 | tf_op jit(solution)/shard_map/second_stage/pallas_call | solution.py:384
  48.6 1.6 %collective-permute-start.12 = (bf16[128,960]{1,0:T(8,128)(2,1)S(1)}, bf16[128,960]{1,0:T(8,128)(2,1)S(1)}, u32[]{:S(2)}, u32[]{:S(2)}) collective-permute-start(bf16[128,960]{1,0:T(8,128)(2,1)S(1)} %get-tuple-element.147), channel_id=1, source_target_pairs={{1,0},{0,1},{3,2},{2,3},{5,4},{4,5},{7,6},{6,7},{9,8},{8,9},{11,10... | collective-permute-start | bytes 737288 | tf_op jit(solution)/shard_map/ppermute | solution.py:498
  50.2 1.3 %local_stage.5 = (f32[128,960]{1,0:T(8,128)S(1)}, f32[128,960]{1,0:T(8,128)S(1)}) custom-call(bf16[528,1920]{1,0:T(8,128)(2,1)S(1)} %get-tuple-element.154.refs_0_, f32[512,960]{1,0:T(8,128)S(1)} %get-tuple-element.155.refs_1_, f32[16,8,960]{2,1,0:T(8,128)S(1)} %get-tuple-element.128.refs_2_, ...), custom_call_target="tpu_custom_call" | custom-call | flops 1 | bytes 1 | tf_op jit(solution)/shard_map/local_stage/pallas_call | solution.py:384
  51.5 2.2 %second_stage.5 = (bf16[128,960]{1,0:T(8,128)(2,1)S(1)}, f32[128,960]{1,0:T(8,128)S(1)}) custom-call(s32[2]{0:T(128)S(1)} %pad_add_fusion.refs_0_, f32[128,960]{1,0:T(8,128)S(1)} %get-tuple-element.151.refs_1_, f32[128,960]{1,0:T(8,128)S(1)} %get-tuple-element.152.refs_2_, f32[16,8,960]{2,1,0:T(8,128)S(1)} %get-tuple-element.144.refs_3_, ...), custom_call_target="tpu_custom_call" | custom-call | flops 1 | bytes 1 | tf_op jit(solution)/shard_map/second_stage/pallas_call | solution.py:384
  53.7 0.6 collective-permute-start.13
  54.2 2.6 %collective-permute-done.12.refs_3_ = bf16[128,960]{1,0:T(8,128)(2,1)S(1)} collective-permute-done((bf16[128,960]{1,0:T(8,128)(2,1)S(1)}, bf16[128,960]{1,0:T(8,128)(2,1)S(1)}, u32[]{:S(2)}, u32[]{:S(2)}) %collective-permute-start.12) | collective-permute-done | bytes 245792 | tf_op jit(solution)/shard_map/ppermute | solution.py:498
  56.9 1.3 %local_stage.7 = (f32[128,960]{1,0:T(8,128)S(1)}, f32[128,960]{1,0:T(8,128)S(1)}) custom-call(bf16[528,1920]{1,0:T(8,128)(2,1)S(1)} %get-tuple-element.154.refs_0_, f32[512,960]{1,0:T(8,128)S(1)} %get-tuple-element.155.refs_1_, f32[16,8,960]{2,1,0:T(8,128)S(1)} %get-tuple-element.128.refs_2_, ...), custom_call_target="tpu_custom_call" | custom-call | flops 1 | bytes 1 | tf_op jit(solution)/shard_map/local_stage/pallas_call | solution.py:384
  58.2 2.3 %second_stage.7 = (bf16[128,960]{1,0:T(8,128)(2,1)S(1)}, f32[128,960]{1,0:T(8,128)S(1)}) custom-call(s32[2]{0:T(128)S(1)} %pad_add_fusion.refs_0_, f32[128,960]{1,0:T(8,128)S(1)} %get-tuple-element.163.refs_1_, f32[128,960]{1,0:T(8,128)S(1)} %get-tuple-element.164.refs_2_, f32[16,8,960]{2,1,0:T(8,128)S(1)} %get-tuple-element.144.refs_3_, ...), custom_call_target="tpu_custom_call" | custom-call | flops 1 | bytes 1 | tf_op jit(solution)/shard_map/second_stage/pallas_call | solution.py:384
  60.5 2.5 %collective-permute-start.15 = (bf16[128,960]{1,0:T(8,128)(2,1)S(1)}, bf16[128,960]{1,0:T(8,128)(2,1)S(1)}, u32[]{:S(2)}, u32[]{:S(2)}) collective-permute-start(bf16[128,960]{1,0:T(8,128)(2,1)S(1)} %get-tuple-element.168), channel_id=1, source_target_pairs={{1,0},{0,1},{3,2},{2,3},{5,4},{4,5},{7,6},{6,7},{9,8},{8,9},{11,10... | collective-permute-start | bytes 737288 | tf_op jit(solution)/shard_map/ppermute | solution.py:498
  63.0 1.3 %local_stage.6 = (f32[128,960]{1,0:T(8,128)S(1)}, f32[128,960]{1,0:T(8,128)S(1)}) custom-call(bf16[528,1920]{1,0:T(8,128)(2,1)S(1)} %get-tuple-element.154.refs_0_, f32[512,960]{1,0:T(8,128)S(1)} %get-tuple-element.155.refs_1_, f32[16,8,960]{2,1,0:T(8,128)S(1)} %get-tuple-element.128.refs_2_, ...), custom_call_target="tpu_custom_call" | custom-call | flops 1 | bytes 1 | tf_op jit(solution)/shard_map/local_stage/pallas_call | solution.py:384
  64.3 2.3 %second_stage.6 = (bf16[128,960]{1,0:T(8,128)(2,1)S(1)}, f32[128,960]{1,0:T(8,128)S(1)}) custom-call(s32[2]{0:T(128)S(1)} %pad_add_fusion.refs_0_, f32[128,960]{1,0:T(8,128)S(1)} %get-tuple-element.156.refs_1_, f32[128,960]{1,0:T(8,128)S(1)} %get-tuple-element.157.refs_2_, f32[16,8,960]{2,1,0:T(8,128)S(1)} %get-tuple-element.144.refs_3_, ...), custom_call_target="tpu_custom_call" | custom-call | flops 1 | bytes 1 | tf_op jit(solution)/shard_map/second_stage/pallas_call | solution.py:384
  66.6 1.3 %collective-permute-start.14 = (bf16[128,960]{1,0:T(8,128)(2,1)S(1)}, bf16[128,960]{1,0:T(8,128)(2,1)S(1)}, u32[]{:S(2)}, u32[]{:S(2)}) collective-permute-start(bf16[128,960]{1,0:T(8,128)(2,1)S(1)} %get-tuple-element.160), channel_id=1, source_target_pairs={{1,0},{0,1},{3,2},{2,3},{5,4},{4,5},{7,6},{6,7},{9,8},{8,9},{11,10... | collective-permute-start | bytes 737288 | tf_op jit(solution)/shard_map/ppermute | solution.py:498
  67.9 0.7 collective-permute-done.15.refs_5_
  68.6 0.8 %last_stage.2.refs_2_ = bf16[960,512]{1,0:T(8,128)(2,1)S(1)} custom-call(f32[128,960]{1,0:T(8,128)S(1)} %get-tuple-element.161.refs_0_, f32[128,960]{1,0:T(8,128)S(1)} %get-tuple-element.162.refs_1_, f32[128,960]{1,0:T(8,128)S(1)} %get-tuple-element.165.refs_2_, bf16[128,960]{1,0:T(8,128)(2,1)S(1)} %collective-permute-done.12.refs_3_, ...), custom_call_target="tpu_custom_call" | custom-call | flops 1 | bytes 1 | tf_op jit(solution)/shard_map/last_stage/pallas_call | solution.py:384
  69.3 3.7 %collective-permute-done.14.refs_1_ = bf16[128,960]{1,0:T(8,128)(2,1)S(1)} collective-permute-done((bf16[128,960]{1,0:T(8,128)(2,1)S(1)}, bf16[128,960]{1,0:T(8,128)(2,1)S(1)}, u32[]{:S(2)}, u32[]{:S(2)}) %collective-permute-start.14) | collective-permute-done | bytes 245792 | tf_op jit(solution)/shard_map/ppermute | solution.py:498
  73.0 1.2 %last_stage.3 = bf16[960,512]{1,0:T(8,128)(2,1)} custom-call(f32[128,960]{1,0:T(8,128)S(1)} %get-tuple-element.159.refs_0_, bf16[128,960]{1,0:T(8,128)(2,1)S(1)} %collective-permute-done.14.refs_1_, bf16[960,512]{1,0:T(8,128)(2,1)S(1)} %last_stage.2.refs_2_), custom_call_target="tpu_custom_call" | custom-call | flops 1 | bytes 1 | tf_op jit(solution)/shard_map/last_stage/pallas_call | solution.py:384
  (18 shorter events, 0.0 us)
Async XLA Ops:
  0.0 8.9 %copy-start.5 = (f32[1920]{0:T(1024)S(1)}, f32[1920]{0:T(1024)}, u32[]{:S(2)}) copy-start(f32[1920]{0:T(1024)} %param.9) | copy-start | bytes 23044
  0.1 1.2 %copy-start.2 = (bf16[960,512]{1,0:T(8,128)(2,1)S(1)}, bf16[960,512]{1,0:T(8,128)(2,1)}, u32[]{:S(2)}) copy-start(bf16[960,512]{1,0:T(8,128)(2,1)} %tokens_ref.1) | copy-start | bytes 2949124
  1.7 14.5 %collective-permute-start.5 = (bf16[128,960]{1,0:T(8,128)(2,1)S(1)}, bf16[128,960]{1,0:T(8,128)(2,1)S(1)}, u32[]{:S(2)}, u32[]{:S(2)}) collective-permute-start(bf16[128,960]{1,0:T(8,128)(2,1)S(1)} %get-tuple-element.93.refs_1_), channel_id=1, source_target_pairs={{1,0},{0,1},{3,2},{2,3},{5,4},{4,5},{7,6},{6,7},{9,8},{8,9},{11,10... | collective-permute-start | bytes 737288 | tf_op jit(solution)/shard_map/ppermute | solution.py:498
  5.8 13.3 %collective-permute-start.4 = (bf16[128,960]{1,0:T(8,128)(2,1)S(1)}, bf16[128,960]{1,0:T(8,128)(2,1)S(1)}, u32[]{:S(2)}, u32[]{:S(2)}) collective-permute-start(bf16[128,960]{1,0:T(8,128)(2,1)S(1)} %get-tuple-element.94.refs_1_), channel_id=1, source_target_pairs={{1,0},{0,1},{3,2},{2,3},{5,4},{4,5},{7,6},{6,7},{9,8},{8,9},{11,10... | collective-permute-start | bytes 737288 | tf_op jit(solution)/shard_map/ppermute | solution.py:498
  5.9 17.3 %collective-permute-start.3 = (bf16[128,960]{1,0:T(8,128)(2,1)S(1)}, bf16[128,960]{1,0:T(8,128)(2,1)S(1)}, u32[]{:S(2)}, u32[]{:S(2)}) collective-permute-start(bf16[128,960]{1,0:T(8,128)(2,1)S(1)} %get-tuple-element.95.refs_1_), channel_id=1, source_target_pairs={{1,0},{0,1},{3,2},{2,3},{5,4},{4,5},{7,6},{6,7},{9,8},{8,9},{11,10... | collective-permute-start | bytes 737288 | tf_op jit(solution)/shard_map/ppermute | solution.py:498
  7.9 20.1 %collective-permute-start = (bf16[128,960]{1,0:T(8,128)(2,1)S(1)}, bf16[128,960]{1,0:T(8,128)(2,1)S(1)}, u32[]{:S(2)}, u32[]{:S(2)}) collective-permute-start(bf16[128,960]{1,0:T(8,128)(2,1)S(1)} %get-tuple-element.91.refs_1_), channel_id=1, source_target_pairs={{1,0},{0,1},{3,2},{2,3},{5,4},{4,5},{7,6},{6,7},{9,8},{8,9},{11,10... | collective-permute-start | bytes 737288 | tf_op jit(solution)/shard_map/ppermute | solution.py:498
  8.0 6.3 %collective-permute-start.1 = (bf16[2,960]{1,0:T(2,128)(2,1)S(1)}, bf16[2,960]{1,0:T(2,128)(2,1)S(1)}, u32[]{:S(2)}, u32[]{:S(2)}) collective-permute-start(bf16[2,960]{1,0:T(2,128)(2,1)S(1)} %get-tuple-element.92), channel_id=1, source_target_pairs={{30,0},{0,2},{2,4},{4,6},{6,8},{8,10},{10,12},{12,14},{14,16},{16,... | collective-permute-start | bytes 11528 | tf_op jit(solution)/shard_map/ppermute | solution.py:498
  8.9 7.4 %copy-start.1 = (f32[16,960]{1,0:T(8,128)S(1)}, f32[16,960]{1,0:T(8,128)}, u32[]{:S(2)}) copy-start(f32[16,960]{1,0:T(8,128)} %refs_7_.7) | copy-start | bytes 184324
  8.9 7.4 %copy-start.3 = (f32[3,3,960]{2,1,0:T(4,128)S(1)}, f32[3,3,960]{2,1,0:T(4,128)}, u32[]{:S(2)}) copy-start(f32[3,3,960]{2,1,0:T(4,128)} %refs_4_.7) | copy-start | bytes 103684
  14.3 13.7 %collective-permute-start.2 = (bf16[2,960]{1,0:T(2,128)(2,1)S(1)}, bf16[2,960]{1,0:T(2,128)(2,1)S(1)}, u32[]{:S(2)}, u32[]{:S(2)}) collective-permute-start(bf16[2,960]{1,0:T(2,128)(2,1)S(1)} %collective-permute-done.1.refs_3_), channel_id=1, source_target_pairs={{1,0},{0,1},{3,2},{2,3},{5,4},{4,5},{7,6},{6,7},{9,8},{8,9},{11,10... | collective-permute-start | bytes 11528 | tf_op jit(solution)/shard_map/ppermute | solution.py:498
  28.0 7.4 %copy-start.4 = (f32[960]{0:T(1024)S(1)}, f32[960]{0:T(1024)}, u32[]{:S(2)}) copy-start(f32[960]{0:T(1024)} %param.14) | copy-start | bytes 11524
  32.2 4.9 %collective-permute-start.6 = (bf16[16,960]{1,0:T(8,128)(2,1)S(1)}, bf16[16,960]{1,0:T(8,128)(2,1)S(1)}, u32[]{:S(2)}, u32[]{:S(2)}) collective-permute-start(bf16[16,960]{1,0:T(8,128)(2,1)S(1)} %get-tuple-element.127), channel_id=1, source_target_pairs={{6,0},{0,2},{2,4},{4,6},{14,8},{8,10},{10,12},{12,14},{22,16},{16,... | collective-permute-start | bytes 92168 | tf_op jit(solution)/shard_map/ppermute | solution.py:549
  32.2 5.0 %collective-permute-start.7 = (bf16[16,960]{1,0:T(8,128)(2,1)S(1)}, bf16[16,960]{1,0:T(8,128)(2,1)S(1)}, u32[]{:S(2)}, u32[]{:S(2)}) collective-permute-start(bf16[16,960]{1,0:T(8,128)(2,1)S(1)} %get-tuple-element.127), channel_id=1, source_target_pairs={{4,0},{6,2},{0,4},{2,6},{12,8},{14,10},{8,12},{10,14},{20,16},{22,... | collective-permute-start | bytes 92168 | tf_op jit(solution)/shard_map/ppermute | solution.py:549
  34.0 3.2 %collective-permute-start.8 = (bf16[16,960]{1,0:T(8,128)(2,1)S(1)}, bf16[16,960]{1,0:T(8,128)(2,1)S(1)}, u32[]{:S(2)}, u32[]{:S(2)}) collective-permute-start(bf16[16,960]{1,0:T(8,128)(2,1)S(1)} %get-tuple-element.127), channel_id=1, source_target_pairs={{2,0},{4,2},{6,4},{0,6},{10,8},{12,10},{14,12},{8,14},{18,16},{20,... | collective-permute-start | bytes 92168 | tf_op jit(solution)/shard_map/ppermute | solution.py:549
  35.4 11.2 %copy-start = (bf16[960,1920]{1,0:T(8,128)(2,1)S(1)}, bf16[960,1920]{1,0:T(8,128)(2,1)}, u32[]{:S(2)}) copy-start(bf16[960,1920]{1,0:T(8,128)(2,1)} %refs_9_.7) | copy-start | bytes 11059204
  37.8 8.1 %collective-permute-start.9 = (bf16[24,960]{1,0:T(8,128)(2,1)S(1)}, bf16[24,960]{1,0:T(8,128)(2,1)S(1)}, u32[]{:S(2)}, u32[]{:S(2)}) collective-permute-start(bf16[24,960]{1,0:T(8,128)(2,1)S(1)} %get-tuple-element.139), channel_id=1, source_target_pairs={{24,0},{26,2},{28,4},{30,6},{0,8},{2,10},{4,12},{6,14},{8,16},{10,... | collective-permute-start | bytes 138248 | tf_op jit(solution)/shard_map/ppermute | solution.py:549
  39.5 5.5 %collective-permute-start.10 = (bf16[16,960]{1,0:T(8,128)(2,1)S(1)}, bf16[16,960]{1,0:T(8,128)(2,1)S(1)}, u32[]{:S(2)}, u32[]{:S(2)}) collective-permute-start(bf16[16,960]{1,0:T(8,128)(2,1)S(1)} %get-tuple-element.140), channel_id=1, source_target_pairs={{16,0},{18,2},{20,4},{22,6},{24,8},{26,10},{28,12},{30,14},{0,16},... | collective-permute-start | bytes 92168 | tf_op jit(solution)/shard_map/ppermute | solution.py:549
  42.0 3.9 %collective-permute-start.11 = (bf16[16,960]{1,0:T(8,128)(2,1)S(1)}, bf16[16,960]{1,0:T(8,128)(2,1)S(1)}, u32[]{:S(2)}, u32[]{:S(2)}) collective-permute-start(bf16[16,960]{1,0:T(8,128)(2,1)S(1)} %get-tuple-element.140), channel_id=1, source_target_pairs={{8,0},{10,2},{12,4},{14,6},{16,8},{18,10},{20,12},{22,14},{24,16},... | collective-permute-start | bytes 92168 | tf_op jit(solution)/shard_map/ppermute | solution.py:549
  48.6 8.3 %collective-permute-start.12 = (bf16[128,960]{1,0:T(8,128)(2,1)S(1)}, bf16[128,960]{1,0:T(8,128)(2,1)S(1)}, u32[]{:S(2)}, u32[]{:S(2)}) collective-permute-start(bf16[128,960]{1,0:T(8,128)(2,1)S(1)} %get-tuple-element.147), channel_id=1, source_target_pairs={{1,0},{0,1},{3,2},{2,3},{5,4},{4,5},{7,6},{6,7},{9,8},{8,9},{11,10... | collective-permute-start | bytes 737288 | tf_op jit(solution)/shard_map/ppermute | solution.py:498
  53.7 9.4 %collective-permute-start.13 = (bf16[128,960]{1,0:T(8,128)(2,1)S(1)}, bf16[128,960]{1,0:T(8,128)(2,1)S(1)}, u32[]{:S(2)}, u32[]{:S(2)}) collective-permute-start(bf16[128,960]{1,0:T(8,128)(2,1)S(1)} %get-tuple-element.153), channel_id=1, source_target_pairs={{1,0},{0,1},{3,2},{2,3},{5,4},{4,5},{7,6},{6,7},{9,8},{8,9},{11,10... | collective-permute-start | bytes 737288 | tf_op jit(solution)/shard_map/ppermute | solution.py:498
  60.5 8.1 %collective-permute-start.15 = (bf16[128,960]{1,0:T(8,128)(2,1)S(1)}, bf16[128,960]{1,0:T(8,128)(2,1)S(1)}, u32[]{:S(2)}, u32[]{:S(2)}) collective-permute-start(bf16[128,960]{1,0:T(8,128)(2,1)S(1)} %get-tuple-element.168), channel_id=1, source_target_pairs={{1,0},{0,1},{3,2},{2,3},{5,4},{4,5},{7,6},{6,7},{9,8},{8,9},{11,10... | collective-permute-start | bytes 737288 | tf_op jit(solution)/shard_map/ppermute | solution.py:498
  66.6 6.4 %collective-permute-start.14 = (bf16[128,960]{1,0:T(8,128)(2,1)S(1)}, bf16[128,960]{1,0:T(8,128)(2,1)S(1)}, u32[]{:S(2)}, u32[]{:S(2)}) collective-permute-start(bf16[128,960]{1,0:T(8,128)(2,1)S(1)} %get-tuple-element.160), channel_id=1, source_target_pairs={{1,0},{0,1},{3,2},{2,3},{5,4},{4,5},{7,6},{6,7},{9,8},{8,9},{11,10... | collective-permute-start | bytes 737288 | tf_op jit(solution)/shard_map/ppermute | solution.py:498

commit v6 on v5

--- a/solution.py
+++ b/solution.py
@@ -12,7 +12,7 @@
 BF16 = jnp.bfloat16
 ROWS = 8
 LANES = 128
-BLOCK = 256
+BLOCK = 512
 CHUNKS = 4
 SPAN = 16
 VMEM_LIMIT = 10 * 2**20

time: 74.6 us -> 74.6 us (level)
  transfers between devices with their start and end apart: 16 -> 16, of which waited for: 7 -> 7; matrix products, arithmetic and copies ran while one was open for 1% -> 1% of each run, Pallas kernels for 38% -> 37%
where the time goes in v6:
time: 74.6 us; the launch traced here: 74.4 us
  Pallas kernels  36.9 us (49%)
  starting transfers between devices  21.9 us (29%)
  waiting for transfers between devices  12.9 us (17%)
  local copies, waits for them, and re-layouts  1.23 us (2%)
  other arithmetic  0.99 us (1%)
    pallas_call x18, Pallas kernels, call(): pl.pallas_call(kernel, out_shape=outs, in_specs=[smem] * len(scalars) + [...  31.7 us
    ppermute x10, starting transfers between devices, rotate(): lax.ppermute(value, axis, [((i + steps) % count, i) for i in range(count)])  13.2 us
    ppermute x10, waiting for transfers between devices, rotate(): lax.ppermute(value, axis, [((i + steps) % count, i) for i in range(count)])  10.3 us
    ppermute x6, starting transfers between devices, carried_in(): others.append(lax.ppermute(longer if first else sent, axis, pairs))  8.75 us
    pallas_call x1, Pallas kernels, in_vmem(): pl.pallas_call(functools.partial(load_weights, places), out_shape=pltpu.V...  5.28 us
    ppermute x6, waiting for transfers between devices, carried_in(): others.append(lax.ppermute(longer if first else sent, axis, pairs))  2.58 us
  transfers between devices with their start and end apart: 16, of which 7 were waited for; matrix products, arithmetic and copies ran while one was open for 1% of the time, Pallas kernels for 37%

profile of v6, /device:TPU:0, one launch (start us, length us, event | category | flops | bytes accessed | tf_op | source)
XLA Modules:
  0.0 74.4 jit_solution(15906492469967182830)
XLA Ops:
  0.0 0.1 pad_add_fusion.refs_0_
  0.1 1.2 %copy-done.2 = bf16[960,512]{1,0:T(8,128)(2,1)S(1)} copy-done((bf16[960,512]{1,0:T(8,128)(2,1)S(1)}, bf16[960,512]{1,0:T(8,128)(2,1)}, u32[]{:S(2)}) %copy-start.2) | copy-done | bytes 983064
  1.3 0.5 first_rows.1
  1.7 3.0 %collective-permute-start.5 = (bf16[128,960]{1,0:T(8,128)(2,1)S(1)}, bf16[128,960]{1,0:T(8,128)(2,1)S(1)}, u32[]{:S(2)}, u32[]{:S(2)}) collective-permute-start(bf16[128,960]{1,0:T(8,128)(2,1)S(1)} %get-tuple-element.93.refs_1_), channel_id=1, source_target_pairs={{1,0},{0,1},{3,2},{2,3},{5,4},{4,5},{7,6},{6,7},{9,8},{8,9},{11,10... | collective-permute-start | bytes 737288 | tf_op jit(solution)/shard_map/ppermute | solution.py:498
  4.8 1.0 %next_rows.1 = (bf16[128,960]{1,0:T(8,128)(2,1)S(1)}, bf16[128,960]{1,0:T(8,128)(2,1)S(1)}, bf16[128,960]{1,0:T(8,128)(2,1)S(1)}) custom-call(bf16[960,512]{1,0:T(8,128)(2,1)S(1)} %copy-done.2), custom_call_target="tpu_custom_call" | custom-call | flops 1 | bytes 1 | tf_op jit(solution)/shard_map/next_rows/pallas_call | solution.py:384
  5.8 0.1 collective-permute-start.4
  5.9 2.0 %collective-permute-start.3 = (bf16[128,960]{1,0:T(8,128)(2,1)S(1)}, bf16[128,960]{1,0:T(8,128)(2,1)S(1)}, u32[]{:S(2)}, u32[]{:S(2)}) collective-permute-start(bf16[128,960]{1,0:T(8,128)(2,1)S(1)} %get-tuple-element.95.refs_1_), channel_id=1, source_target_pairs={{1,0},{0,1},{3,2},{2,3},{5,4},{4,5},{7,6},{6,7},{9,8},{8,9},{11,10... | collective-permute-start | bytes 737288 | tf_op jit(solution)/shard_map/ppermute | solution.py:498
  7.9 0.1 collective-permute-start
  8.0 0.0 collective-permute-start.1
  8.0 0.9 %sqrt_multiply_fusion.refs_6_.refs_8_ = f32[16,960]{1,0:T(8,128)S(1)} fusion(f32[16,960]{1,0:T(8,128)} %param.13, f32[16,960]{1,0:T(8,128)} %refs_7_.7), kind=kLoop, calls=%fused_computation | loop fusion | flops 46080 | bytes 184320 | tf_op jit(solution)/shard_map/mul | solution.py:591
  8.9 0.0 copy-start.1
  8.9 0.0 copy-start.3
  8.9 5.3 %load_weights.1.refs_4_.refs_9_.refs_12_.refs_3_ = bf16[3,1920,960]{2,1,0:T(8,128)(2,1)S(1)} custom-call(bf16[3,960,1920]{2,1,0:T(8,128)(2,1)} %w_hbm), custom_call_target="tpu_custom_call" | custom-call | flops 1 | bytes 1 | tf_op jit(solution)/shard_map/load_weights/pallas_call | solution.py:405
  14.2 0.0 collective-permute-done.1.refs_3_
  14.2 2.0 %collective-permute-start.2 = (bf16[2,960]{1,0:T(2,128)(2,1)S(1)}, bf16[2,960]{1,0:T(2,128)(2,1)S(1)}, u32[]{:S(2)}, u32[]{:S(2)}) collective-permute-start(bf16[2,960]{1,0:T(2,128)(2,1)S(1)} %collective-permute-done.1.refs_3_), channel_id=1, source_target_pairs={{1,0},{0,1},{3,2},{2,3},{5,4},{4,5},{7,6},{6,7},{9,8},{8,9},{11,10... | collective-permute-start | bytes 11528 | tf_op jit(solution)/shard_map/ppermute | solution.py:498
  16.3 0.0 collective-permute-done.5.refs_2_
  16.3 2.7 %signal_stage.4 = (bf16[528,1920]{1,0:T(8,128)(2,1)S(1)}, f32[512,960]{1,0:T(8,128)S(1)}, f32[4,16,8,960]{3,2,1,0:T(8,128)S(1)}, f32[16,8,960]{2,1,0:T(8,128)S(1...) custom-call(s32[2]{0:T(128)S(1)} %pad_add_fusion.refs_0_, bf16[128,960]{1,0:T(8,128)(2,1)S(1)} %get-tuple-element.93.refs_1_, ...), custom_call_target="tpu_custom_call" | custom-call | flops 1 | bytes 1 | tf_op jit(solution)/shard_map/signal_stage/pallas_call | solution.py:384
  19.0 2.9 %signal_stage.5 = (bf16[528,1920]{1,0:T(8,128)(2,1)S(1)}, f32[512,960]{1,0:T(8,128)S(1)}, f32[4,16,8,960]{3,2,1,0:T(8,128)S(1)}, f32[16,8,960]{2,1,0:T(8,128)S(1)}, f32[2,16,960]{2,1,0:T(8,128)S(1)}) custom-call(s32[2]{0:T(128)S(1)} %pad_add_fusion.refs_0_, ...), custom_call_target="tpu_custom_call", output_to_operand_aliasing={{0}: (3, {}), {1}: (4, {}), {2}: (5, {})} | custom-call | flops 1 | bytes 1 | tf_op jit(solution)/shard_map/signal_stage/pallas_call | solution.py:384
  21.8 1.3 %collective-permute-done.3.refs_2_ = bf16[128,960]{1,0:T(8,128)(2,1)S(1)} collective-permute-done((bf16[128,960]{1,0:T(8,128)(2,1)S(1)}, bf16[128,960]{1,0:T(8,128)(2,1)S(1)}, u32[]{:S(2)}, u32[]{:S(2)}) %collective-permute-start.3) | collective-permute-done | bytes 245792 | tf_op jit(solution)/shard_map/ppermute | solution.py:498
  23.1 2.9 %signal_stage.6 = (bf16[528,1920]{1,0:T(8,128)(2,1)S(1)}, f32[512,960]{1,0:T(8,128)S(1)}, f32[4,16,8,960]{3,2,1,0:T(8,128)S(1)}, f32[16,8,960]{2,1,0:T(8,128)S(1)}, f32[2,16,960]{2,1,0:T(8,128)S(1)}) custom-call(s32[2]{0:T(128)S(1)} %pad_add_fusion.refs_0_, ...), custom_call_target="tpu_custom_call", output_to_operand_aliasing={{0}: (3, {}), {1}: (4, {}), {2}: (5, {})} | custom-call | flops 1 | bytes 1 | tf_op jit(solution)/shard_map/signal_stage/pallas_call | solution.py:384
  26.0 2.0 %collective-permute-done.2.refs_4_ = bf16[2,960]{1,0:T(2,128)(2,1)S(1)} collective-permute-done((bf16[2,960]{1,0:T(2,128)(2,1)S(1)}, bf16[2,960]{1,0:T(2,128)(2,1)S(1)}, u32[]{:S(2)}, u32[]{:S(2)}) %collective-permute-start.2) | collective-permute-done | bytes 3872 | tf_op jit(solution)/shard_map/ppermute | solution.py:498
  28.0 4.0 %signal_stage.7 = (bf16[528,1920]{1,0:T(8,128)(2,1)S(1)}, f32[512,960]{1,0:T(8,128)S(1)}, f32[4,16,8,960]{3,2,1,0:T(8,128)S(1)}, f32[16,8,960]{2,1,0:T(8,128)S(1...) custom-call(s32[2]{0:T(128)S(1)} %pad_add_fusion.refs_0_, ...), custom_call_target="tpu_custom_call", output_to_operand_aliasing={{0}: (5, {}), {1}: (6, {}), {2}: (7, {})} | custom-call | flops 1 | bytes 1 | tf_op jit(solution)/shard_map/signal_stage/pallas_call | solution.py:384
  32.1 1.7 %collective-permute-start.7 = (bf16[16,960]{1,0:T(8,128)(2,1)S(1)}, bf16[16,960]{1,0:T(8,128)(2,1)S(1)}, u32[]{:S(2)}, u32[]{:S(2)}) collective-permute-start(bf16[16,960]{1,0:T(8,128)(2,1)S(1)} %get-tuple-element.127), channel_id=1, source_target_pairs={{4,0},{6,2},{0,4},{2,6},{12,8},{14,10},{8,12},{10,14},{20,16},{22,... | collective-permute-start | bytes 92168 | tf_op jit(solution)/shard_map/ppermute | solution.py:549
  33.8 1.4 %collective-permute-start.8 = (bf16[16,960]{1,0:T(8,128)(2,1)S(1)}, bf16[16,960]{1,0:T(8,128)(2,1)S(1)}, u32[]{:S(2)}, u32[]{:S(2)}) collective-permute-start(bf16[16,960]{1,0:T(8,128)(2,1)S(1)} %get-tuple-element.127), channel_id=1, source_target_pairs={{2,0},{4,2},{6,4},{0,6},{10,8},{12,10},{14,12},{8,14},{18,16},{20,... | collective-permute-start | bytes 92168 | tf_op jit(solution)/shard_map/ppermute | solution.py:549
  35.3 1.8 %local_stage.4 = (f32[128,960]{1,0:T(8,128)S(1)}, f32[128,960]{1,0:T(8,128)S(1)}, f32[16,8,960]{2,1,0:T(8,128)S(1)}, f32[16,8,960]{2,1,0:T(8,128)S(1)}) custom-call(bf16[528,1920]{1,0:T(8,128)(2,1)S(1)} %get-tuple-element.154.refs_0_, f32[512,960]{1,0:T(8,128)S(1)} %get-tuple-element.155.refs_1_, f32[16,8,960]{2,1,0:T(8,128)S(1)} %get-tuple-element.128.refs_2_, ...), custom_call_target="tpu_custom_call" | custom-call | flops 1 | bytes 1 | tf_op jit(solution)/shard_map/local_stage/pallas_call | solution.py:384
  37.0 0.6 combine_states.2
  37.7 1.6 %collective-permute-start.9 = (bf16[24,960]{1,0:T(8,128)(2,1)S(1)}, bf16[24,960]{1,0:T(8,128)(2,1)S(1)}, u32[]{:S(2)}, u32[]{:S(2)}) collective-permute-start(bf16[24,960]{1,0:T(8,128)(2,1)S(1)} %get-tuple-element.139), channel_id=1, source_target_pairs={{24,0},{26,2},{28,4},{30,6},{0,8},{2,10},{4,12},{6,14},{8,16},{10,... | collective-permute-start | bytes 138248 | tf_op jit(solution)/shard_map/ppermute | solution.py:549
  39.3 2.6 %collective-permute-start.10 = (bf16[16,960]{1,0:T(8,128)(2,1)S(1)}, bf16[16,960]{1,0:T(8,128)(2,1)S(1)}, u32[]{:S(2)}, u32[]{:S(2)}) collective-permute-start(bf16[16,960]{1,0:T(8,128)(2,1)S(1)} %get-tuple-element.140), channel_id=1, source_target_pairs={{16,0},{18,2},{20,4},{22,6},{24,8},{26,10},{28,12},{30,14},{0,16},... | collective-permute-start | bytes 92168 | tf_op jit(solution)/shard_map/ppermute | solution.py:549
  41.9 1.3 %collective-permute-start.11 = (bf16[16,960]{1,0:T(8,128)(2,1)S(1)}, bf16[16,960]{1,0:T(8,128)(2,1)S(1)}, u32[]{:S(2)}, u32[]{:S(2)}) collective-permute-start(bf16[16,960]{1,0:T(8,128)(2,1)S(1)} %get-tuple-element.140), channel_id=1, source_target_pairs={{8,0},{10,2},{12,4},{14,6},{16,8},{18,10},{20,12},{22,14},{24,16},... | collective-permute-start | bytes 92168 | tf_op jit(solution)/shard_map/ppermute | solution.py:549
  43.3 1.6 %collective-permute-done.10.refs_4_ = bf16[16,960]{1,0:T(8,128)(2,1)S(1)} collective-permute-done((bf16[16,960]{1,0:T(8,128)(2,1)S(1)}, bf16[16,960]{1,0:T(8,128)(2,1)S(1)}, u32[]{:S(2)}, u32[]{:S(2)}) %collective-permute-start.10) | collective-permute-done | bytes 30752 | tf_op jit(solution)/shard_map/ppermute | solution.py:549
  44.9 1.0 %collective-permute-done.11.refs_5_ = bf16[16,960]{1,0:T(8,128)(2,1)S(1)} collective-permute-done((bf16[16,960]{1,0:T(8,128)(2,1)S(1)}, bf16[16,960]{1,0:T(8,128)(2,1)S(1)}, u32[]{:S(2)}, u32[]{:S(2)}) %collective-permute-start.11) | collective-permute-done | bytes 30752 | tf_op jit(solution)/shard_map/ppermute | solution.py:549
  45.8 0.6 combine_states.3.refs_6_
  46.5 2.0 %second_stage.4 = (bf16[128,960]{1,0:T(8,128)(2,1)S(1)}, f32[128,960]{1,0:T(8,128)S(1)}) custom-call(s32[2]{0:T(128)S(1)} %pad_add_fusion.refs_0_, f32[128,960]{1,0:T(8,128)S(1)} %get-tuple-element.142.refs_1_, f32[128,960]{1,0:T(8,128)S(1)} %get-tuple-element.143.refs_2_, f32[16,8,960]{2,1,0:T(8,128)S(1)} %get-tuple-element.144.refs_3_, ...), custom_call_target="tpu_custom_call" | custom-call | flops 1 | bytes 1 | tf_op jit(solution)/shard_map/second_stage/pallas_call | solution.py:384
  48.5 1.6 %collective-permute-start.12 = (bf16[128,960]{1,0:T(8,128)(2,1)S(1)}, bf16[128,960]{1,0:T(8,128)(2,1)S(1)}, u32[]{:S(2)}, u32[]{:S(2)}) collective-permute-start(bf16[128,960]{1,0:T(8,128)(2,1)S(1)} %get-tuple-element.147), channel_id=1, source_target_pairs={{1,0},{0,1},{3,2},{2,3},{5,4},{4,5},{7,6},{6,7},{9,8},{8,9},{11,10... | collective-permute-start | bytes 737288 | tf_op jit(solution)/shard_map/ppermute | solution.py:498
  50.1 1.3 %local_stage.5 = (f32[128,960]{1,0:T(8,128)S(1)}, f32[128,960]{1,0:T(8,128)S(1)}) custom-call(bf16[528,1920]{1,0:T(8,128)(2,1)S(1)} %get-tuple-element.154.refs_0_, f32[512,960]{1,0:T(8,128)S(1)} %get-tuple-element.155.refs_1_, f32[16,8,960]{2,1,0:T(8,128)S(1)} %get-tuple-element.128.refs_2_, ...), custom_call_target="tpu_custom_call" | custom-call | flops 1 | bytes 1 | tf_op jit(solution)/shard_map/local_stage/pallas_call | solution.py:384
  51.4 2.2 %second_stage.5 = (bf16[128,960]{1,0:T(8,128)(2,1)S(1)}, f32[128,960]{1,0:T(8,128)S(1)}) custom-call(s32[2]{0:T(128)S(1)} %pad_add_fusion.refs_0_, f32[128,960]{1,0:T(8,128)S(1)} %get-tuple-element.151.refs_1_, f32[128,960]{1,0:T(8,128)S(1)} %get-tuple-element.152.refs_2_, f32[16,8,960]{2,1,0:T(8,128)S(1)} %get-tuple-element.144.refs_3_, ...), custom_call_target="tpu_custom_call" | custom-call | flops 1 | bytes 1 | tf_op jit(solution)/shard_map/second_stage/pallas_call | solution.py:384
  53.6 0.6 collective-permute-start.13
  54.1 2.6 %collective-permute-done.12.refs_3_ = bf16[128,960]{1,0:T(8,128)(2,1)S(1)} collective-permute-done((bf16[128,960]{1,0:T(8,128)(2,1)S(1)}, bf16[128,960]{1,0:T(8,128)(2,1)S(1)}, u32[]{:S(2)}, u32[]{:S(2)}) %collective-permute-start.12) | collective-permute-done | bytes 245792 | tf_op jit(solution)/shard_map/ppermute | solution.py:498
  56.7 1.3 %local_stage.7 = (f32[128,960]{1,0:T(8,128)S(1)}, f32[128,960]{1,0:T(8,128)S(1)}) custom-call(bf16[528,1920]{1,0:T(8,128)(2,1)S(1)} %get-tuple-element.154.refs_0_, f32[512,960]{1,0:T(8,128)S(1)} %get-tuple-element.155.refs_1_, f32[16,8,960]{2,1,0:T(8,128)S(1)} %get-tuple-element.128.refs_2_, ...), custom_call_target="tpu_custom_call" | custom-call | flops 1 | bytes 1 | tf_op jit(solution)/shard_map/local_stage/pallas_call | solution.py:384
  58.0 2.3 %second_stage.7 = (bf16[128,960]{1,0:T(8,128)(2,1)S(1)}, f32[128,960]{1,0:T(8,128)S(1)}) custom-call(s32[2]{0:T(128)S(1)} %pad_add_fusion.refs_0_, f32[128,960]{1,0:T(8,128)S(1)} %get-tuple-element.163.refs_1_, f32[128,960]{1,0:T(8,128)S(1)} %get-tuple-element.164.refs_2_, f32[16,8,960]{2,1,0:T(8,128)S(1)} %get-tuple-element.144.refs_3_, ...), custom_call_target="tpu_custom_call" | custom-call | flops 1 | bytes 1 | tf_op jit(solution)/shard_map/second_stage/pallas_call | solution.py:384
  60.3 2.6 %collective-permute-start.15 = (bf16[128,960]{1,0:T(8,128)(2,1)S(1)}, bf16[128,960]{1,0:T(8,128)(2,1)S(1)}, u32[]{:S(2)}, u32[]{:S(2)}) collective-permute-start(bf16[128,960]{1,0:T(8,128)(2,1)S(1)} %get-tuple-element.168), channel_id=1, source_target_pairs={{1,0},{0,1},{3,2},{2,3},{5,4},{4,5},{7,6},{6,7},{9,8},{8,9},{11,10... | collective-permute-start | bytes 737288 | tf_op jit(solution)/shard_map/ppermute | solution.py:498
  62.9 1.3 %local_stage.6 = (f32[128,960]{1,0:T(8,128)S(1)}, f32[128,960]{1,0:T(8,128)S(1)}) custom-call(bf16[528,1920]{1,0:T(8,128)(2,1)S(1)} %get-tuple-element.154.refs_0_, f32[512,960]{1,0:T(8,128)S(1)} %get-tuple-element.155.refs_1_, f32[16,8,960]{2,1,0:T(8,128)S(1)} %get-tuple-element.128.refs_2_, ...), custom_call_target="tpu_custom_call" | custom-call | flops 1 | bytes 1 | tf_op jit(solution)/shard_map/local_stage/pallas_call | solution.py:384
  64.2 2.3 %second_stage.6 = (bf16[128,960]{1,0:T(8,128)(2,1)S(1)}, f32[128,960]{1,0:T(8,128)S(1)}) custom-call(s32[2]{0:T(128)S(1)} %pad_add_fusion.refs_0_, f32[128,960]{1,0:T(8,128)S(1)} %get-tuple-element.156.refs_1_, f32[128,960]{1,0:T(8,128)S(1)} %get-tuple-element.157.refs_2_, f32[16,8,960]{2,1,0:T(8,128)S(1)} %get-tuple-element.144.refs_3_, ...), custom_call_target="tpu_custom_call" | custom-call | flops 1 | bytes 1 | tf_op jit(solution)/shard_map/second_stage/pallas_call | solution.py:384
  66.5 1.3 %collective-permute-start.14 = (bf16[128,960]{1,0:T(8,128)(2,1)S(1)}, bf16[128,960]{1,0:T(8,128)(2,1)S(1)}, u32[]{:S(2)}, u32[]{:S(2)}) collective-permute-start(bf16[128,960]{1,0:T(8,128)(2,1)S(1)} %get-tuple-element.160), channel_id=1, source_target_pairs={{1,0},{0,1},{3,2},{2,3},{5,4},{4,5},{7,6},{6,7},{9,8},{8,9},{11,10... | collective-permute-start | bytes 737288 | tf_op jit(solution)/shard_map/ppermute | solution.py:498
  67.8 0.6 collective-permute-done.15.refs_5_
  68.4 0.8 %last_stage.2.refs_2_ = bf16[960,512]{1,0:T(8,128)(2,1)S(1)} custom-call(f32[128,960]{1,0:T(8,128)S(1)} %get-tuple-element.161.refs_0_, f32[128,960]{1,0:T(8,128)S(1)} %get-tuple-element.162.refs_1_, f32[128,960]{1,0:T(8,128)S(1)} %get-tuple-element.165.refs_2_, bf16[128,960]{1,0:T(8,128)(2,1)S(1)} %collective-permute-done.12.refs_3_, ...), custom_call_target="tpu_custom_call" | custom-call | flops 1 | bytes 1 | tf_op jit(solution)/shard_map/last_stage/pallas_call | solution.py:384
  69.1 3.8 %collective-permute-done.14.refs_1_ = bf16[128,960]{1,0:T(8,128)(2,1)S(1)} collective-permute-done((bf16[128,960]{1,0:T(8,128)(2,1)S(1)}, bf16[128,960]{1,0:T(8,128)(2,1)S(1)}, u32[]{:S(2)}, u32[]{:S(2)}) %collective-permute-start.14) | collective-permute-done | bytes 245792 | tf_op jit(solution)/shard_map/ppermute | solution.py:498
  72.9 1.3 %last_stage.3 = bf16[960,512]{1,0:T(8,128)(2,1)} custom-call(f32[128,960]{1,0:T(8,128)S(1)} %get-tuple-element.159.refs_0_, bf16[128,960]{1,0:T(8,128)(2,1)S(1)} %collective-permute-done.14.refs_1_, bf16[960,512]{1,0:T(8,128)(2,1)S(1)} %last_stage.2.refs_2_), custom_call_target="tpu_custom_call" | custom-call | flops 1 | bytes 1 | tf_op jit(solution)/shard_map/last_stage/pallas_call | solution.py:384
  (18 shorter events, 0.0 us)
Async XLA Ops:
  0.0 8.9 %copy-start.5 = (f32[1920]{0:T(1024)S(1)}, f32[1920]{0:T(1024)}, u32[]{:S(2)}) copy-start(f32[1920]{0:T(1024)} %param.9) | copy-start | bytes 23044
  0.1 1.2 %copy-start.2 = (bf16[960,512]{1,0:T(8,128)(2,1)S(1)}, bf16[960,512]{1,0:T(8,128)(2,1)}, u32[]{:S(2)}) copy-start(bf16[960,512]{1,0:T(8,128)(2,1)} %tokens_ref.1) | copy-start | bytes 2949124
  1.7 14.5 %collective-permute-start.5 = (bf16[128,960]{1,0:T(8,128)(2,1)S(1)}, bf16[128,960]{1,0:T(8,128)(2,1)S(1)}, u32[]{:S(2)}, u32[]{:S(2)}) collective-permute-start(bf16[128,960]{1,0:T(8,128)(2,1)S(1)} %get-tuple-element.93.refs_1_), channel_id=1, source_target_pairs={{1,0},{0,1},{3,2},{2,3},{5,4},{4,5},{7,6},{6,7},{9,8},{8,9},{11,10... | collective-permute-start | bytes 737288 | tf_op jit(solution)/shard_map/ppermute | solution.py:498
  5.8 13.2 %collective-permute-start.4 = (bf16[128,960]{1,0:T(8,128)(2,1)S(1)}, bf16[128,960]{1,0:T(8,128)(2,1)S(1)}, u32[]{:S(2)}, u32[]{:S(2)}) collective-permute-start(bf16[128,960]{1,0:T(8,128)(2,1)S(1)} %get-tuple-element.94.refs_1_), channel_id=1, source_target_pairs={{1,0},{0,1},{3,2},{2,3},{5,4},{4,5},{7,6},{6,7},{9,8},{8,9},{11,10... | collective-permute-start | bytes 737288 | tf_op jit(solution)/shard_map/ppermute | solution.py:498
  5.9 17.3 %collective-permute-start.3 = (bf16[128,960]{1,0:T(8,128)(2,1)S(1)}, bf16[128,960]{1,0:T(8,128)(2,1)S(1)}, u32[]{:S(2)}, u32[]{:S(2)}) collective-permute-start(bf16[128,960]{1,0:T(8,128)(2,1)S(1)} %get-tuple-element.95.refs_1_), channel_id=1, source_target_pairs={{1,0},{0,1},{3,2},{2,3},{5,4},{4,5},{7,6},{6,7},{9,8},{8,9},{11,10... | collective-permute-start | bytes 737288 | tf_op jit(solution)/shard_map/ppermute | solution.py:498
  7.9 20.1 %collective-permute-start = (bf16[128,960]{1,0:T(8,128)(2,1)S(1)}, bf16[128,960]{1,0:T(8,128)(2,1)S(1)}, u32[]{:S(2)}, u32[]{:S(2)}) collective-permute-start(bf16[128,960]{1,0:T(8,128)(2,1)S(1)} %get-tuple-element.91.refs_1_), channel_id=1, source_target_pairs={{1,0},{0,1},{3,2},{2,3},{5,4},{4,5},{7,6},{6,7},{9,8},{8,9},{11,10... | collective-permute-start | bytes 737288 | tf_op jit(solution)/shard_map/ppermute | solution.py:498
  8.0 6.3 %collective-permute-start.1 = (bf16[2,960]{1,0:T(2,128)(2,1)S(1)}, bf16[2,960]{1,0:T(2,128)(2,1)S(1)}, u32[]{:S(2)}, u32[]{:S(2)}) collective-permute-start(bf16[2,960]{1,0:T(2,128)(2,1)S(1)} %get-tuple-element.92), channel_id=1, source_target_pairs={{30,0},{0,2},{2,4},{4,6},{6,8},{8,10},{10,12},{12,14},{14,16},{16,... | collective-permute-start | bytes 11528 | tf_op jit(solution)/shard_map/ppermute | solution.py:498
  8.9 7.3 %copy-start.1 = (f32[16,960]{1,0:T(8,128)S(1)}, f32[16,960]{1,0:T(8,128)}, u32[]{:S(2)}) copy-start(f32[16,960]{1,0:T(8,128)} %refs_7_.7) | copy-start | bytes 184324
  8.9 7.3 %copy-start.3 = (f32[3,3,960]{2,1,0:T(4,128)S(1)}, f32[3,3,960]{2,1,0:T(4,128)}, u32[]{:S(2)}) copy-start(f32[3,3,960]{2,1,0:T(4,128)} %refs_4_.7) | copy-start | bytes 103684
  14.2 13.8 %collective-permute-start.2 = (bf16[2,960]{1,0:T(2,128)(2,1)S(1)}, bf16[2,960]{1,0:T(2,128)(2,1)S(1)}, u32[]{:S(2)}, u32[]{:S(2)}) collective-permute-start(bf16[2,960]{1,0:T(2,128)(2,1)S(1)} %collective-permute-done.1.refs_3_), channel_id=1, source_target_pairs={{1,0},{0,1},{3,2},{2,3},{5,4},{4,5},{7,6},{6,7},{9,8},{8,9},{11,10... | collective-permute-start | bytes 11528 | tf_op jit(solution)/shard_map/ppermute | solution.py:498
  28.0 7.2 %copy-start.4 = (f32[960]{0:T(1024)S(1)}, f32[960]{0:T(1024)}, u32[]{:S(2)}) copy-start(f32[960]{0:T(1024)} %param.14) | copy-start | bytes 11524
  32.1 4.9 %collective-permute-start.6 = (bf16[16,960]{1,0:T(8,128)(2,1)S(1)}, bf16[16,960]{1,0:T(8,128)(2,1)S(1)}, u32[]{:S(2)}, u32[]{:S(2)}) collective-permute-start(bf16[16,960]{1,0:T(8,128)(2,1)S(1)} %get-tuple-element.127), channel_id=1, source_target_pairs={{6,0},{0,2},{2,4},{4,6},{14,8},{8,10},{10,12},{12,14},{22,16},{16,... | collective-permute-start | bytes 92168 | tf_op jit(solution)/shard_map/ppermute | solution.py:549
  32.1 5.0 %collective-permute-start.7 = (bf16[16,960]{1,0:T(8,128)(2,1)S(1)}, bf16[16,960]{1,0:T(8,128)(2,1)S(1)}, u32[]{:S(2)}, u32[]{:S(2)}) collective-permute-start(bf16[16,960]{1,0:T(8,128)(2,1)S(1)} %get-tuple-element.127), channel_id=1, source_target_pairs={{4,0},{6,2},{0,4},{2,6},{12,8},{14,10},{8,12},{10,14},{20,16},{22,... | collective-permute-start | bytes 92168 | tf_op jit(solution)/shard_map/ppermute | solution.py:549
  33.8 3.2 %collective-permute-start.8 = (bf16[16,960]{1,0:T(8,128)(2,1)S(1)}, bf16[16,960]{1,0:T(8,128)(2,1)S(1)}, u32[]{:S(2)}, u32[]{:S(2)}) collective-permute-start(bf16[16,960]{1,0:T(8,128)(2,1)S(1)} %get-tuple-element.127), channel_id=1, source_target_pairs={{2,0},{4,2},{6,4},{0,6},{10,8},{12,10},{14,12},{8,14},{18,16},{20,... | collective-permute-start | bytes 92168 | tf_op jit(solution)/shard_map/ppermute | solution.py:549
  35.3 11.2 %copy-start = (bf16[960,1920]{1,0:T(8,128)(2,1)S(1)}, bf16[960,1920]{1,0:T(8,128)(2,1)}, u32[]{:S(2)}) copy-start(bf16[960,1920]{1,0:T(8,128)(2,1)} %refs_9_.7) | copy-start | bytes 11059204
  37.7 8.1 %collective-permute-start.9 = (bf16[24,960]{1,0:T(8,128)(2,1)S(1)}, bf16[24,960]{1,0:T(8,128)(2,1)S(1)}, u32[]{:S(2)}, u32[]{:S(2)}) collective-permute-start(bf16[24,960]{1,0:T(8,128)(2,1)S(1)} %get-tuple-element.139), channel_id=1, source_target_pairs={{24,0},{26,2},{28,4},{30,6},{0,8},{2,10},{4,12},{6,14},{8,16},{10,... | collective-permute-start | bytes 138248 | tf_op jit(solution)/shard_map/ppermute | solution.py:549
  39.3 5.5 %collective-permute-start.10 = (bf16[16,960]{1,0:T(8,128)(2,1)S(1)}, bf16[16,960]{1,0:T(8,128)(2,1)S(1)}, u32[]{:S(2)}, u32[]{:S(2)}) collective-permute-start(bf16[16,960]{1,0:T(8,128)(2,1)S(1)} %get-tuple-element.140), channel_id=1, source_target_pairs={{16,0},{18,2},{20,4},{22,6},{24,8},{26,10},{28,12},{30,14},{0,16},... | collective-permute-start | bytes 92168 | tf_op jit(solution)/shard_map/ppermute | solution.py:549
  41.9 3.9 %collective-permute-start.11 = (bf16[16,960]{1,0:T(8,128)(2,1)S(1)}, bf16[16,960]{1,0:T(8,128)(2,1)S(1)}, u32[]{:S(2)}, u32[]{:S(2)}) collective-permute-start(bf16[16,960]{1,0:T(8,128)(2,1)S(1)} %get-tuple-element.140), channel_id=1, source_target_pairs={{8,0},{10,2},{12,4},{14,6},{16,8},{18,10},{20,12},{22,14},{24,16},... | collective-permute-start | bytes 92168 | tf_op jit(solution)/shard_map/ppermute | solution.py:549
  48.5 8.2 %collective-permute-start.12 = (bf16[128,960]{1,0:T(8,128)(2,1)S(1)}, bf16[128,960]{1,0:T(8,128)(2,1)S(1)}, u32[]{:S(2)}, u32[]{:S(2)}) collective-permute-start(bf16[128,960]{1,0:T(8,128)(2,1)S(1)} %get-tuple-element.147), channel_id=1, source_target_pairs={{1,0},{0,1},{3,2},{2,3},{5,4},{4,5},{7,6},{6,7},{9,8},{8,9},{11,10... | collective-permute-start | bytes 737288 | tf_op jit(solution)/shard_map/ppermute | solution.py:498
  53.6 9.3 %collective-permute-start.13 = (bf16[128,960]{1,0:T(8,128)(2,1)S(1)}, bf16[128,960]{1,0:T(8,128)(2,1)S(1)}, u32[]{:S(2)}, u32[]{:S(2)}) collective-permute-start(bf16[128,960]{1,0:T(8,128)(2,1)S(1)} %get-tuple-element.153), channel_id=1, source_target_pairs={{1,0},{0,1},{3,2},{2,3},{5,4},{4,5},{7,6},{6,7},{9,8},{8,9},{11,10... | collective-permute-start | bytes 737288 | tf_op jit(solution)/shard_map/ppermute | solution.py:498
  60.3 8.1 %collective-permute-start.15 = (bf16[128,960]{1,0:T(8,128)(2,1)S(1)}, bf16[128,960]{1,0:T(8,128)(2,1)S(1)}, u32[]{:S(2)}, u32[]{:S(2)}) collective-permute-start(bf16[128,960]{1,0:T(8,128)(2,1)S(1)} %get-tuple-element.168), channel_id=1, source_target_pairs={{1,0},{0,1},{3,2},{2,3},{5,4},{4,5},{7,6},{6,7},{9,8},{8,9},{11,10... | collective-permute-start | bytes 737288 | tf_op jit(solution)/shard_map/ppermute | solution.py:498
  66.5 6.4 %collective-permute-start.14 = (bf16[128,960]{1,0:T(8,128)(2,1)S(1)}, bf16[128,960]{1,0:T(8,128)(2,1)S(1)}, u32[]{:S(2)}, u32[]{:S(2)}) collective-permute-start(bf16[128,960]{1,0:T(8,128)(2,1)S(1)} %get-tuple-element.160), channel_id=1, source_target_pairs={{1,0},{0,1},{3,2},{2,3},{5,4},{4,5},{7,6},{6,7},{9,8},{8,9},{11,10... | collective-permute-start | bytes 737288 | tf_op jit(solution)/shard_map/ppermute | solution.py:498
